TPU v7x, 128 devices: a whole 4x4x4 slice. The times are simulated.
128 devices in a mesh: section: 2 (over y_hi), dp: 16 (over x, y_lo, core), tensor: 4 (over z).
Axes of the slice: x: 4, y: 4 (y_hi: 2, y_lo: 2; y = y_hi * 2 + y_lo), z: 4, core: 2. Of those that a mesh axis runs over, the one named last changes fastest.
Arguments:
- ends_in: bfloat16 [2, 2, 2048, 2048], P('section', None, ('dp', 'tensor')), may hold values from -6 to 6
- segments: int32 [2, 2048], P(None, 'dp'), may hold values from 0 to 4, as said below
- decay_rate: float32 [2, 8], P('section'), may hold values from 0.0001 to 0.03
- attn_gain: bfloat16 [2, 2048], P('section', 'dp'), may hold values from 0.5 to 1.5
- w_query: bfloat16 [2, 2048, 2048], P('section', 'dp', 'tensor'), may hold values from -0.125 to 0.125
- w_key: bfloat16 [2, 2048, 2048], P('section', 'dp', 'tensor'), may hold values from -0.125 to 0.125
- w_value: bfloat16 [2, 2048, 3456], P('section', 'dp', 'tensor'), may hold values from -0.125 to 0.125
- w_gate_ret: bfloat16 [2, 2048, 3456], P('section', 'dp', 'tensor'), may hold values from -0.125 to 0.125
- w_out: bfloat16 [2, 3456, 2048], P('section', 'tensor', 'dp'), may hold values from -0.109375 to 0.109375
- ffn_gain: bfloat16 [2, 2048], P('section', 'dp'), may hold values from 0.5 to 1.5
- w_gate: bfloat16 [2, 2048, 3456], P('section', 'dp', 'tensor'), may hold values from -0.125 to 0.125
- w_up: bfloat16 [2, 2048, 3456], P('section', 'dp', 'tensor'), may hold values from -0.125 to 0.125
- w_down: bfloat16 [2, 3456, 2048], P('section', 'tensor', 'dp'), may hold values from -0.109375 to 0.109375
Outputs:
- ends_out: float32 [2, 2, 2048, 2048], P('section', None, ('dp', 'tensor'))
- grad_attn_gain: float32 [2, 2048], P('section', 'dp')
- grad_query: float32 [2, 2048, 2048], P('section', 'dp', 'tensor')
- grad_key: float32 [2, 2048, 2048], P('section', 'dp', 'tensor')
- grad_value: float32 [2, 2048, 3456], P('section', 'dp', 'tensor')
- grad_gate_ret: float32 [2, 2048, 3456], P('section', 'dp', 'tensor')
- grad_out: float32 [2, 3456, 2048], P('section', 'tensor', 'dp')
- grad_ffn_gain: float32 [2, 2048], P('section', 'dp')
- grad_gate: float32 [2, 2048, 3456], P('section', 'dp', 'tensor')
- grad_up: float32 [2, 2048, 3456], P('section', 'dp', 'tensor')
- grad_down: float32 [2, 3456, 2048], P('section', 'tensor', 'dp')
Inputs may be any that keep to these rules, and one draw needn't show every extreme that they name: `segments`: ids never fall along a micro-batch; in each micro-batch one document starts within its first 128 tokens and ends within its last 128 tokens.
All inputs are finite; a program needn't handle non-finite values.
Results may differ from a plain program's by a relative error of at most 0.038.
Values may be sent and summed in bfloat16 or wider, within the bound.
No kernel may reach another device: no remote copies, remote signals or barrier semaphores. Data moves between devices by JAX's collectives and lax.ppermute only.
A program may use at most 192 MiB of HBM per device.

v0:
```python
import jax
import jax.numpy as jnp
from jax import lax
from jax.sharding import PartitionSpec as P

epsilon = 1e-06
group_floor = 1.0
split_precision = lax.Precision.HIGH


def prefix(value, axis, combine, identity):
    devices, mine = (lax.axis_size(axis), lax.axis_index(axis))
    everything = jax.tree.map(
        lambda part, kind: lax.all_gather(part.astype(kind), axis),
        value,
        (jnp.bfloat16, jnp.bfloat16, jnp.bfloat16, jnp.bfloat16, jnp.bfloat16),
    )
    start = jax.tree.map(
        lambda part, zero: jnp.broadcast_to(jnp.asarray(zero, part.dtype), part.shape),
        value,
        identity,
    )

    def prefix_step(k, before):
        reached = k < mine
        new = combine(
            before, jax.tree.map(lambda part, own: part[k].astype(own.dtype), everything, value)
        )
        return jax.tree.map(lambda a, b: jnp.where(reached, a, b), new, before)

    return lax.fori_loop(0, devices, prefix_step, start)


def entering(value, axis, combine, identity):
    devices, mine = (lax.axis_size(axis), lax.axis_index(axis))
    everything = jax.tree.map(
        lambda part, kind: lax.all_gather(part.astype(kind), axis),
        value,
        jax.tree.map(lambda a: jnp.bfloat16 if a.dtype == jnp.float32 else a.dtype, value),
    )
    start = jax.tree.map(
        lambda part, zero: jnp.broadcast_to(jnp.asarray(zero, part.dtype), part.shape),
        value,
        identity,
    )

    def entering_step(k, before):
        at = devices - 1 - k
        reached = at > mine
        new = combine(
            before, jax.tree.map(lambda part, own: part[at].astype(own.dtype), everything, value)
        )
        return jax.tree.map(lambda a, b: jnp.where(reached, a, b), new, before)

    return lax.fori_loop(0, devices, entering_step, start)


def from_behind(value, axis, by):
    devices = lax.axis_size(axis)
    pairs = [(i, i + by) for i in range(devices) if 0 <= i + by < devices]
    return lax.ppermute(value, axis, pairs)


def rms_scale(row_block, gain_vec):
    return (
        row_block
        * lax.rsqrt(jnp.mean(row_block * row_block, axis=-1, keepdims=True) + epsilon)
        * gain_vec
    )


def to_low(array_in):
    return array_in.astype(jnp.bfloat16)


def forward_product(operand, matrix):
    return jnp.dot(operand, matrix, preferred_element_type=jnp.float32)


def transposed_right(operand, matrix):
    return jnp.einsum("tc,dc->td", operand, matrix, preferred_element_type=jnp.float32)


def transposed_left(first_rows, second_rows):
    return jnp.einsum("tc,td->cd", first_rows, second_rows, preferred_element_type=jnp.float32)


def swiglu(gate_pre, up_pre):
    return jax.nn.silu(gate_pre) * up_pre


def gate_norm(ret_gate, retained):
    normed = retained * lax.rsqrt(
        jnp.mean(retained * retained, axis=-1, keepdims=True) + group_floor
    )
    return jax.nn.silu(ret_gate) * normed.reshape(ret_gate.shape)


def retention_out(queries, keys_in, values, state_in, linked, decays, doc_ids):
    row_count = queries.shape[0]
    places = jnp.arange(row_count)
    distance = places[:, None] - places[None, :]
    allowed = (distance >= 0) & (doc_ids[:, None] == doc_ids[None, :])
    span_len = jnp.where(allowed, distance, 0).astype(jnp.float32)
    weights = jnp.where(allowed[None], jnp.exp(-decays[:, None, None] * span_len[None]), 0.0)
    scores = jnp.einsum("ihd,jhd->hij", queries, keys_in, precision=split_precision) * weights
    within = jnp.einsum("hij,jhe->ihe", scores, values, precision=split_precision)
    carried = jnp.einsum("ihd,hde->ihe", queries, state_in, precision=split_precision)
    reaching = (
        jnp.exp(-decays[None, :] * (places[:, None] + 1).astype(jnp.float32)) * linked[:, None]
    )
    return (within + carried * reaching[:, :, None]) * queries.shape[2] ** (-0.5)


def retention_state(keys_in, values, decays, doc_ids):
    row_count = keys_in.shape[0]
    places = jnp.arange(row_count)
    in_tail = (doc_ids == doc_ids[row_count - 1]).astype(jnp.float32)
    fading = (
        jnp.exp(-decays[None, :] * (row_count - 1 - places)[:, None].astype(jnp.float32))
        * in_tail[:, None]
    )
    return jnp.einsum(
        "ihd,ihe->hde", keys_in * fading[:, :, None], values, precision=split_precision
    )


def choose(latter_empty, earlier_empty, earlier, latter, joined):
    return tuple(
        (
            jnp.where(latter_empty, first_one, jnp.where(earlier_empty, second_one, third_one))
            for first_one, second_one, third_one in zip(earlier, latter, joined)
        )
    )


def carry_join(earlier, latter):
    same_doc = (earlier[1] == latter[1]).astype(jnp.float32)
    linked = same_doc * latter[2]
    joined = (
        jnp.maximum(earlier[0], latter[0]),
        latter[1],
        earlier[2] * latter[2] * same_doc,
        earlier[3] * latter[3],
        latter[4] + (linked * latter[3])[:, None, None] * earlier[4],
    )
    return choose(latter[0] == 0.0, earlier[0] == 0.0, earlier, latter, joined)


def carry_back_join(higher, beneath):
    same_doc = (beneath[2] == higher[1]).astype(jnp.float32)
    linked = same_doc * beneath[3]
    joined = (
        jnp.maximum(higher[0], beneath[0]),
        beneath[1],
        higher[2],
        beneath[3] * higher[3] * same_doc,
        beneath[4] * higher[4],
        beneath[5] + (linked * beneath[4])[:, None, None] * higher[5],
    )
    return choose(beneath[0] == 0.0, higher[0] == 0.0, higher, beneath, joined)


def spread_rows(row_block):
    return lax.all_gather(row_block, "tensor", axis=0, tiled=True)


def spread_grads(row_block):
    return lax.all_gather(row_block, "tensor", axis=0, tiled=True)


def out_rows(operand, matrix):
    return lax.psum_scatter(
        jnp.dot(operand, matrix, preferred_element_type=jnp.float32).astype(jnp.bfloat16),
        "tensor",
        scatter_dimension=0,
        tiled=True,
    ).astype(jnp.float32)


def rows_back(grad_list, matrices):
    share = grad_list[0].shape[0] // lax.axis_size("tensor")
    result = jnp.zeros((share * lax.axis_size("tensor"), matrices[0].shape[0]), jnp.float32)
    for grad_part, matrix in zip(grad_list, matrices):
        result = result + transposed_right(grad_part, matrix)
    return lax.psum_scatter(
        result.astype(jnp.bfloat16), "tensor", scatter_dimension=0, tiled=True
    ).astype(jnp.float32)


def gather_layer(shards):
    return (
        lax.all_gather(shards[0], "dp", axis=0, tiled=True),
        lax.all_gather(shards[1], "dp", axis=0, tiled=True),
        lax.all_gather(shards[2], "dp", axis=0, tiled=True),
        lax.all_gather(shards[3], "dp", axis=0, tiled=True),
        lax.all_gather(shards[4], "dp", axis=0, tiled=True),
        lax.all_gather(shards[5], "dp", axis=1, tiled=True),
        lax.all_gather(shards[6], "dp", axis=0, tiled=True),
        lax.all_gather(shards[7], "dp", axis=0, tiled=True),
        lax.all_gather(shards[8], "dp", axis=0, tiled=True),
        lax.all_gather(shards[9], "dp", axis=1, tiled=True),
    )


def reduce_total(grads):
    return (
        lax.psum_scatter(
            grads[0].astype(jnp.bfloat16), "dp", scatter_dimension=0, tiled=True
        ).astype(jnp.float32),
        lax.psum_scatter(
            grads[1].astype(jnp.bfloat16), "dp", scatter_dimension=0, tiled=True
        ).astype(jnp.float32),
        lax.psum_scatter(
            grads[2].astype(jnp.bfloat16), "dp", scatter_dimension=0, tiled=True
        ).astype(jnp.float32),
        lax.psum_scatter(
            grads[3].astype(jnp.bfloat16), "dp", scatter_dimension=0, tiled=True
        ).astype(jnp.float32),
        lax.psum_scatter(
            grads[4].astype(jnp.bfloat16), "dp", scatter_dimension=0, tiled=True
        ).astype(jnp.float32),
        lax.psum_scatter(
            grads[5].astype(jnp.bfloat16), "dp", scatter_dimension=1, tiled=True
        ).astype(jnp.float32),
        lax.psum_scatter(
            grads[6].astype(jnp.bfloat16), "dp", scatter_dimension=0, tiled=True
        ).astype(jnp.float32),
        lax.psum_scatter(
            grads[7].astype(jnp.bfloat16), "dp", scatter_dimension=0, tiled=True
        ).astype(jnp.float32),
        lax.psum_scatter(
            grads[8].astype(jnp.bfloat16), "dp", scatter_dimension=0, tiled=True
        ).astype(jnp.float32),
        lax.psum_scatter(
            grads[9].astype(jnp.bfloat16), "dp", scatter_dimension=1, tiled=True
        ).astype(jnp.float32),
    )


def layer_forward(layer_in, doc_ids, decays, weights):
    attn_gain, w_query, w_key, w_value, w_gate_ret, w_out, ffn_gain, w_gate, w_up, w_down = weights
    a_rows = spread_rows(to_low(rms_scale(layer_in, attn_gain.astype(jnp.float32))))
    row_count = a_rows.shape[0]
    local_heads = decays.shape[0]
    queries = (
        to_low(forward_product(a_rows, w_query))
        .astype(jnp.float32)
        .reshape(row_count, local_heads, -1)
    )
    keys_in = (
        to_low(forward_product(a_rows, w_key))
        .astype(jnp.float32)
        .reshape(row_count, local_heads, -1)
    )
    values = (
        to_low(forward_product(a_rows, w_value))
        .astype(jnp.float32)
        .reshape(row_count, local_heads, -1)
    )
    ret_gate = forward_product(a_rows, w_gate_ret)
    doc_float = doc_ids.astype(jnp.float32)
    single = (doc_float[0] == doc_float[row_count - 1]).astype(jnp.float32)
    fade_all = jnp.exp(-decays * row_count)
    own_state = retention_state(keys_in, values, decays, doc_ids)
    before = prefix(
        (jnp.float32(1.0), doc_float[row_count - 1], single, fade_all, own_state),
        "dp",
        carry_join,
        (
            jnp.float32(0.0),
            jnp.float32(0.0),
            jnp.float32(1.0),
            jnp.ones_like(decays),
            jnp.zeros_like(own_state),
        ),
    )
    linked = before[0] * (doc_float == before[1]).astype(jnp.float32)
    retained = retention_out(queries, keys_in, values, before[4], linked, decays, doc_ids)
    gated = to_low(gate_norm(ret_gate, retained))
    mid_rows = layer_in + out_rows(gated, w_out)
    b_rows = spread_rows(to_low(rms_scale(mid_rows, ffn_gain.astype(jnp.float32))))
    gate_pre = forward_product(b_rows, w_gate)
    up_pre = forward_product(b_rows, w_up)
    hidden = to_low(swiglu(gate_pre, up_pre))
    layer_out = mid_rows + out_rows(hidden, w_down)
    return (
        layer_in,
        a_rows,
        queries,
        keys_in,
        values,
        linked,
        before[4],
        retained,
        ret_gate,
        gated,
        mid_rows,
        b_rows,
        gate_pre,
        up_pre,
        hidden,
        layer_out,
    )


def layer_backward(upstream, record, doc_ids, decays, weights):
    attn_gain, w_query, w_key, w_value, w_gate_ret, w_out, ffn_gain, w_gate, w_up, w_down = weights
    (
        layer_in,
        a_rows,
        queries,
        keys_in,
        values,
        linked,
        state_in,
        retained,
        ret_gate,
        gated,
        mid_rows,
        b_rows,
        gate_pre,
        up_pre,
        hidden,
        layer_out,
    ) = record
    row_count = a_rows.shape[0]
    d_final = spread_grads(to_low(upstream))
    d_hidden = transposed_right(d_final, w_down)
    grad_down = transposed_left(hidden, d_final)
    ignored, pullback = jax.vjp(swiglu, gate_pre, up_pre)
    d_gate_pre, d_up_pre = pullback(d_hidden)
    d_gate_low = to_low(d_gate_pre)
    d_up_low = to_low(d_up_pre)
    grad_gate = transposed_left(b_rows, d_gate_low)
    grad_up = transposed_left(b_rows, d_up_low)
    d_b_rows = rows_back((d_gate_low, d_up_low), (w_gate, w_up))
    ignored, pullback = jax.vjp(rms_scale, mid_rows, ffn_gain.astype(jnp.float32))
    d_mid_norm, grad_ffn_gain = pullback(d_b_rows)
    d_mid = upstream + d_mid_norm
    d_branch = spread_grads(to_low(d_mid))
    d_gated = transposed_right(d_branch, w_out)
    grad_out = transposed_left(gated, d_branch)
    ignored, pullback = jax.vjp(gate_norm, ret_gate, retained)
    d_ret_gate, d_retained = pullback(d_gated)

    def local_out(query_in, key_in, value_in, state_val):
        return retention_out(query_in, key_in, value_in, state_val, linked, decays, doc_ids)

    ignored, pullback = jax.vjp(local_out, queries, keys_in, values, state_in)
    d_queries, d_keys, d_values, d_state = pullback(d_retained)
    doc_float = doc_ids.astype(jnp.float32)
    single = (doc_float[0] == doc_float[row_count - 1]).astype(jnp.float32)
    fade_all = jnp.exp(-decays * row_count)
    beyond = entering(
        (jnp.float32(1.0), doc_float[0], doc_float[row_count - 1], single, fade_all, d_state),
        "dp",
        carry_back_join,
        (
            jnp.float32(0.0),
            jnp.float32(0.0),
            jnp.float32(0.0),
            jnp.float32(1.0),
            jnp.ones_like(decays),
            jnp.zeros_like(d_state),
        ),
    )
    from_later = beyond[0] * (beyond[1] == doc_float[row_count - 1]).astype(jnp.float32) * beyond[5]

    def local_state(key_in, value_in):
        return retention_state(key_in, value_in, decays, doc_ids)

    ignored, pullback = jax.vjp(local_state, keys_in, values)
    d_keys_state, d_values_state = pullback(from_later)
    d_query_low = to_low(d_queries.reshape(row_count, -1))
    d_key_low = to_low((d_keys + d_keys_state).reshape(row_count, -1))
    d_value_low = to_low((d_values + d_values_state).reshape(row_count, -1))
    d_ret_low = to_low(d_ret_gate)
    grad_query = transposed_left(a_rows, d_query_low)
    grad_key = transposed_left(a_rows, d_key_low)
    grad_value = transposed_left(a_rows, d_value_low)
    grad_gate_ret = transposed_left(a_rows, d_ret_low)
    d_a_rows = rows_back(
        (d_query_low, d_key_low, d_value_low, d_ret_low), (w_query, w_key, w_value, w_gate_ret)
    )
    ignored, pullback = jax.vjp(rms_scale, layer_in, attn_gain.astype(jnp.float32))
    d_in_norm, grad_attn_gain = pullback(d_a_rows)
    return (
        d_mid + d_in_norm,
        (
            grad_attn_gain,
            grad_query,
            grad_key,
            grad_value,
            grad_gate_ret,
            grad_out,
            grad_ffn_gain,
            grad_gate,
            grad_up,
            grad_down,
        ),
    )


def body(
    ends_in,
    segments,
    decay_rate,
    attn_gain,
    w_query,
    w_key,
    w_value,
    w_gate_ret,
    w_out,
    ffn_gain,
    w_gate,
    w_up,
    w_down,
):
    section_index = lax.axis_index("section")
    is_first = section_index == 0
    micro_count = segments.shape[0]
    local_heads = decay_rate.shape[1] // lax.axis_size("tensor")
    decays = lax.dynamic_slice_in_dim(
        decay_rate[0], lax.axis_index("tensor") * local_heads, local_heads
    )
    shards = (
        attn_gain[0],
        w_query[0],
        w_key[0],
        w_value[0],
        w_gate_ret[0],
        w_out[0],
        ffn_gain[0],
        w_gate[0],
        w_up[0],
        w_down[0],
    )
    weights = gather_layer(shards)
    arriving = ends_in[0].astype(jnp.float32)
    incoming = jnp.zeros_like(arriving[0])
    records = []
    results = []
    for step_index in range(micro_count + 1):
        micro_index = jnp.clip(step_index - section_index, 0, micro_count - 1)
        layer_in = jnp.where(
            is_first, lax.dynamic_index_in_dim(arriving, micro_index, 0, False), incoming
        )
        doc_ids = lax.dynamic_index_in_dim(segments, micro_index, 0, False)
        record = layer_forward(layer_in, doc_ids, decays, weights)
        records.append(record)
        results.append(record[-1])
        if step_index < micro_count:
            incoming = from_behind(to_low(record[-1]), "section", 1).astype(jnp.float32)
    stored = jax.tree.map(lambda *layers: jnp.stack(layers), *records)
    weights = gather_layer(shards)
    grad_sums = tuple((jnp.zeros(piece_shape.shape, jnp.float32) for piece_shape in weights))
    returning = jnp.zeros_like(arriving[0])
    input_grads = []
    for step_index in range(micro_count + 1):
        micro_index = step_index - 1 + section_index
        active = (micro_index >= 0) & (micro_index < micro_count)
        clipped = jnp.clip(micro_index, 0, micro_count - 1)
        doc_ids = lax.dynamic_index_in_dim(segments, clipped, 0, False)
        record = jax.tree.map(
            lambda stack_all: lax.dynamic_index_in_dim(
                stack_all, clipped + section_index, 0, False
            ),
            stored,
        )
        upstream = jnp.where(
            is_first, returning, lax.dynamic_index_in_dim(arriving, clipped, 0, False)
        )
        upstream = jnp.where(active, upstream, 0.0)
        grad_rows, layer_grads = layer_backward(upstream, record, doc_ids, decays, weights)
        grad_sums = tuple((running + addend for running, addend in zip(grad_sums, layer_grads)))
        input_grads.append(grad_rows)
        if step_index < micro_count:
            returning = from_behind(to_low(grad_rows), "section", -1).astype(jnp.float32)
    reduced = reduce_total(grad_sums)
    gain_grads = lax.psum((reduced[0], reduced[6]), "tensor")
    ends_out = jnp.where(is_first, jnp.stack(input_grads[1:]), jnp.stack(results[1:]))
    return (
        ends_out[None],
        gain_grads[0][None],
        reduced[1][None],
        reduced[2][None],
        reduced[3][None],
        reduced[4][None],
        reduced[5][None],
        gain_grads[1][None],
        reduced[7][None],
        reduced[8][None],
        reduced[9][None],
    )


def solution(mesh):
    placed = (
        P("section", None, ("dp", "tensor"), None),
        P(None, "dp"),
        P("section", None),
        P("section", "dp"),
        P("section", "dp", "tensor"),
        P("section", "dp", "tensor"),
        P("section", "dp", "tensor"),
        P("section", "dp", "tensor"),
        P("section", "tensor", "dp"),
        P("section", "dp"),
        P("section", "dp", "tensor"),
        P("section", "dp", "tensor"),
        P("section", "tensor", "dp"),
    )
    return jax.shard_map(
        body,
        mesh=mesh,
        in_specs=placed,
        out_specs=(
            P("section", None, ("dp", "tensor"), None),
            P("section", "dp"),
            P("section", "dp", "tensor"),
            P("section", "dp", "tensor"),
            P("section", "dp", "tensor"),
            P("section", "dp", "tensor"),
            P("section", "tensor", "dp"),
            P("section", "dp"),
            P("section", "dp", "tensor"),
            P("section", "dp", "tensor"),
            P("section", "tensor", "dp"),
        ),
        check_vma=False,
    )
```

profile of v0, /device:TPU:1, one launch (start us, length us, event | category | flops | bytes accessed | tf_op | source)
XLA Modules:
  0.0 2841.5 jit_solution(295831316207113006)
XLA Ops:
  13.9 21.0 all-gather.1
  37.0 12.4 all_gather.215
  56.1 35.5 %all-gather.36.cloned.1.call-done = bf16[1,2048,864]{1,2,0:T(8,128)(2,1)} async-done(((bf16[1,128,864]{1,2,0:T(8,128)(2,1)}), bf16[1,2048,864]{1,2,0:T(8,128)(2,1)}) %all-gather.36.cloned.1.call-update) | async-done | bytes 3538960 | tf_op jit(solution)/shard_map/all_gather | solution.py:196
  109.6 18.2 all-gather.16
  144.6 28.6 %all-reduce.20 = (bf16[16]{0:T(256)(128)(2,1)}, bf16[16]{0:T(256)(128)(2,1)}, bf16[16]{0:T(256)(128)(2,1)}, bf16[16]{0:T(256)(128)(2,1)}, bf16[16]{0:T(256)(128)...) all-reduce(bf16[16]{0:T(256)(128)(2,1)S(1)} %dynamic-update-slice, ...), channel_id=1, replica_groups=mesh['section'=2,'dp'=16,'tensor'=4] {'dp'}, use_global_device_ids=true, to_apply=%add | all-reduce | flops 256 | bytes 1024
  176.7 155.3 %while.114 = (s32[]{:T(128)}, f32[]{:T(128)}, f32[]{:T(128)}, f32[2,256,432]{2,1,0:T(8,128)S(1)}, s32[]{:T(128)}, /*index=5*/bf16[16]{0:T(256)(128)(2,1)}, bf16[...) while((s32[]{:T(128)}, f32[]{:T(128)}, f32[]{:T(128)}, ...), condition=%wide.region_2.3_spmd.clone, body=%wide.region_1.2_spmd.clone.sunk | while | flops 1548306 | bytes 3981628 | solution.py:31
  334.8 3.8 fusion.335
  344.5 18.5 all-gather.8
  365.8 11.5 all_gather.228
  377.2 31.1 %all-gather.48.cloned.1.call-done = bf16[1,2048,864]{1,2,0:T(8,128)(2,1)} async-done(((bf16[1,128,864]{1,2,0:T(8,128)(2,1)}), bf16[1,2048,864]{1,2,0:T(8,128)(2,1)}) %all-gather.48.cloned.1.call-update) | async-done | bytes 3538960 | tf_op jit(solution)/shard_map/all_gather | solution.py:200
  411.4 41.0 %all-gather.46.cloned.1.call-done = bf16[1,2048,864]{1,2,0:T(8,128)(2,1)} async-done(((bf16[1,128,864]{1,2,0:T(8,128)(2,1)}), bf16[1,2048,864]{1,2,0:T(8,128)(2,1)}) %all-gather.46.cloned.1.call-update) | async-done | bytes 3538960 | tf_op jit(solution)/shard_map/all_gather | solution.py:201
  452.4 3.9 multiply_convert_fusion.2
  456.3 40.0 %all-gather.32.cloned.1.call-done = bf16[1,864,2048]{2,1,0:T(8,128)(2,1)} async-done(((bf16[1,864,128]{2,1,0:T(8,128)(2,1)}), bf16[1,864,2048]{2,1,0:T(8,128)(2,1)}) %all-gather.32.cloned.1.call-update) | async-done | bytes 3538960 | tf_op jit(solution)/shard_map/all_gather | solution.py:202
  500.2 19.6 reduce-scatter.35.cloned.1.call-done
  521.1 4.7 collective-permute-start
  530.6 11.0 all_gather.231
  552.8 43.5 %all-gather.50.cloned.1.call-done = bf16[32,256,432]{1,2,0:T(8,128)(2,1)} async-done(((bf16[2,256,432]{1,2,0:T(8,128)(2,1)}), bf16[32,256,432]{1,2,0:T(8,128)(2,1)}) %all-gather.50.cloned.1.call-update) | async-done | bytes 7077904 | tf_op jit(solution)/shard_map/all_gather | solution.py:14
  596.4 247.2 %while.115 = (s32[]{:T(128)}, f32[]{:T(128)}, f32[]{:T(128)}, f32[2,256,432]{2,1,0:T(8,128)}, s32[]{:T(128)}, /*index=5*/bf16[16]{0:T(256)(128)(2,1)}, bf16[16]{...) while((s32[]{:T(128)}, f32[]{:T(128)}, f32[]{:T(128)}, ...), condition=%wide.region_9.10_spmd.clone, body=%wide.region_8.9_spmd.clone.sunk | while | flops 1548306 | bytes 3981628 | solution.py:31
  847.9 4.4 fusion.334
  854.6 20.5 reduce-scatter.37.cloned.1.call-done
  877.3 11.5 all_gather.236
  896.3 23.1 reduce-scatter.39.cloned.1.call-done
  921.3 4.6 collective-permute-start.1
  929.7 10.9 all_gather.237
  954.2 41.4 %all-gather.52.cloned.1.call-done = bf16[32,256,432]{1,2,0:T(8,128)(2,1)} async-done(((bf16[2,256,432]{1,2,0:T(8,128)(2,1)}), bf16[32,256,432]{1,2,0:T(8,128)(2,1)}) %all-gather.52.cloned.1.call-update) | async-done | bytes 7077904 | tf_op jit(solution)/shard_map/all_gather | solution.py:14
  995.6 242.0 %while.116 = (s32[]{:T(128)}, f32[]{:T(128)}, f32[]{:T(128)}, f32[2,256,432]{2,1,0:T(8,128)}, s32[]{:T(128)}, /*index=5*/bf16[16]{0:T(256)(128)(2,1)}, bf16[16]{...) while((s32[]{:T(128)}, f32[]{:T(128)}, f32[]{:T(128)}, ...), condition=%wide.region_16.17_spmd.clone, body=%wide.region_15.16_spmd.clone.sunk | while | flops 1548306 | bytes 3981628 | solution.py:31
  1244.0 4.4 fusion.333
  1251.7 11.5 all_gather.212
  1279.7 10.1 all_gather.242
  1308.7 14.4 reduce-scatter.55.cloned.1.call-done
  1328.0 18.5 reduce-scatter.43.cloned.1.call-done
  1351.0 10.9 all_gather.243
  1361.9 4.2 fusion.327
  1401.6 18.0 all-gather.54.cloned.1.call-done
  1419.5 266.4 %while.117 = (s32[]{:T(128)}, f32[]{:T(128)}, f32[]{:T(128)}, f32[2,256,432]{2,1,0:T(8,128)}, s32[]{:T(128)}, /*index=5*/bf16[16]{0:T(256)(128)(2,1)}, bf16[16]{...) while((s32[]{:T(128)}, f32[]{:T(128)}, f32[]{:T(128)}, ...), condition=%wide.region_26.27_spmd.clone, body=%wide.region_25.26_spmd.clone.sunk | while | flops 1548310 | bytes 3981714 | solution.py:55
  1704.8 16.4 reduce-scatter.45.cloned.1.call-done
  1727.0 6.2 collective-permute-done.2
  1734.3 10.6 all_gather.252
  1754.0 22.1 reduce-scatter.47.cloned.1.call-done
  1780.7 11.3 all_gather.253
  1792.0 4.2 fusion.310
  1817.9 31.7 %all-gather.56.cloned.1.call-done = bf16[32,256,432]{1,2,0:T(8,128)(2,1)} async-done(((bf16[2,256,432]{1,2,0:T(8,128)(2,1)}), bf16[32,256,432]{1,2,0:T(8,128)(2,1)}) %all-gather.56.cloned.1.call-update) | async-done | bytes 7077904 | tf_op jit(solution)/shard_map/all_gather | solution.py:37
  1849.6 262.8 %while.118 = (s32[]{:T(128)}, f32[]{:T(128)}, f32[]{:T(128)}, f32[2,256,432]{2,1,0:T(8,128)}, s32[]{:T(128)}, /*index=5*/bf16[16]{0:T(256)(128)(2,1)}, bf16[16]{...) while((s32[]{:T(128)}, f32[]{:T(128)}, f32[]{:T(128)}, ...), condition=%wide.region_36.37_spmd.clone, body=%wide.region_35.36_spmd.clone.sunk | while | flops 1548310 | bytes 3981714 | solution.py:55
  2128.3 19.3 reduce-scatter.49.cloned.1.call-done
  2153.4 6.2 collective-permute-done.3
  2160.7 10.5 all_gather.262
  2180.4 22.2 reduce-scatter.51.cloned.1.call-done
  2206.9 11.1 all_gather.263
  2218.1 4.2 fusion.293
  2228.0 3.9 fusion.250
  2240.7 5.9 add_convert_fusion.7
  2254.1 6.1 copy.196
  2268.4 6.1 copy.194
  2281.0 6.0 copy.192
  2294.6 6.1 copy.190
  2311.2 6.1 copy.188
  2323.0 257.7 %while.119 = (s32[]{:T(128)}, f32[]{:T(128)}, f32[]{:T(128)}, f32[2,256,432]{2,1,0:T(8,128)}, s32[]{:T(128)}, /*index=5*/bf16[16]{0:T(256)(128)(2,1)}, bf16[16]{...) while((s32[]{:T(128)}, f32[]{:T(128)}, f32[]{:T(128)}, ...), condition=%wide.region_46.47_spmd.clone, body=%wide.region_45.46_spmd.clone.sunk | while | flops 1548310 | bytes 3981714 | solution.py:55
  2605.1 6.0 copy.186
  2620.6 55.6 %reduce-scatter.63.cloned.1.call-done = bf16[128,864]{1,0:T(8,128)(2,1)} async-done(((bf16[2048,864]{1,0:T(8,128)(2,1)}), bf16[128,864]{1,0:T(8,128)(2,1)}) %reduce-scatter.63.cloned.1.call-update) | async-done | bytes 221200
  2678.9 22.0 reduce-scatter.53.cloned.1.call-done
  2702.1 29.4 %all-reduce.19 = (bf16[2048]{0:T(1024)(128)(2,1)S(1)}, bf16[2048]{0:T(1024)(128)(2,1)S(1)}) all-reduce(bf16[2048]{0:T(1024)(128)(2,1)S(1)} %add_convert_fusion.10, bf16[2048]{0:T(1024)(128)(2,1)S(1)} %add_convert_fusion.9), channel_id=30, replica_groups=mesh['section'=2,'dp'=16,'tensor'=4] {'dp'}, use_global_device_ids=true, to_apply=%region_54.55.clone | all-reduce | flops 4096 | bytes 16384
  2731.7 7.5 all-reduce.18
  2741.1 23.6 reduce-scatter.59.cloned.1.call-done
  2766.3 66.0 %reduce-scatter.61.cloned.1.call-done = bf16[128,864]{1,0:T(8,128)(2,1)} async-done(((bf16[2048,864]{1,0:T(8,128)(2,1)}), bf16[128,864]{1,0:T(8,128)(2,1)}) %reduce-scatter.61.cloned.1.call-update) | async-done | bytes 221200
  (1439 shorter events, 1458.5 us)
Async XLA Ops:
  7.2 46.8 %all-gather.40.cloned.1.call-start = ((), (), s32[]{:S(2)}) async-start(), calls=%async_computation.38 | async-start | bytes 2228224 | tf_op jit(solution)/shard_map/all_gather | solution.py:195
  7.9 83.6 %all-gather.36.cloned.1.call-start = ((), (), s32[]{:S(2)}) async-start(), calls=%async_computation.36 | async-start | bytes 3760128 | tf_op jit(solution)/shard_map/all_gather | solution.py:196
  8.7 164.5 %all-gather.38.cloned.1.call-start = ((), (), s32[]{:S(2)}) async-start(), calls=%async_computation.37 | async-start | bytes 2228224 | tf_op jit(solution)/shard_map/all_gather | solution.py:194
  9.4 167.3 %all-gather.42.cloned.1.call-start = ((), (), s32[]{:S(2)}) async-start(), calls=%async_computation.39 | async-start | bytes 7520256 | tf_op jit(solution)/shard_map/all_gather | solution.py:14
  10.4 43.6 %copy-start.137 = (s32[1,128]{1,0:T(1,128)}, s32[1,128]{1,0:T(1,128)S(1)}, u32[]{:S(2)}) copy-start(s32[1,128]{1,0:T(1,128)S(1)} %get-tuple-element.1981) | copy-start | bytes 1540
  10.4 43.6 %copy-start.142 = (s32[1,128]{1,0:T(1,128)}, s32[1,128]{1,0:T(1,128)S(1)}, u32[]{:S(2)}) copy-start(s32[1,128]{1,0:T(1,128)S(1)} %get-tuple-element.1985) | copy-start | bytes 1540
  10.4 43.6 %copy-start.143 = (s32[1,128]{1,0:T(1,128)}, s32[1,128]{1,0:T(1,128)S(1)}, u32[]{:S(2)}) copy-start(s32[1,128]{1,0:T(1,128)S(1)} %get-tuple-element.1977) | copy-start | bytes 1540
  10.4 84.2 %copy-start.136 = (s32[1,128]{1,0:T(1,128)}, s32[1,128]{1,0:T(1,128)S(1)}, u32[]{:S(2)}) copy-start(s32[1,128]{1,0:T(1,128)S(1)} %get-tuple-element.1979) | copy-start | bytes 1540
  10.4 84.2 %copy-start.140 = (s32[1,128]{1,0:T(1,128)}, s32[1,128]{1,0:T(1,128)S(1)}, u32[]{:S(2)}) copy-start(s32[1,128]{1,0:T(1,128)S(1)} %get-tuple-element.1918) | copy-start | bytes 1540
  10.4 321.6 %copy-start.138 = (s32[1,128]{1,0:T(1,128)}, s32[1,128]{1,0:T(1,128)S(1)}, u32[]{:S(2)}) copy-start(s32[1,128]{1,0:T(1,128)S(1)} %get-tuple-element.1983) | copy-start | bytes 1540
  36.0 328.1 %copy-start.13 = (f32[1,2,32,2048]{3,2,1,0:T(8,128)}, f32[1,2,32,2048]{3,2,1,0:T(8,128)S(1)}, u32[]{:S(2)}) copy-start(f32[1,2,32,2048]{3,2,1,0:T(8,128)S(1)} %convert_element_type.1038) | copy-start | bytes 1572868
  36.9 295.2 %copy-start.129 = (f32[2]{0:T(128)}, f32[2]{0:T(128)S(1)}, u32[]{:S(2)}) copy-start(f32[2]{0:T(128)S(1)} %get-tuple-element.1989) | copy-start | bytes 28
  49.4 285.5 %copy-start.29 = (bf16[128,2048]{1,0:T(8,128)(2,1)}, bf16[128,2048]{1,0:T(8,128)(2,1)S(1)}, u32[]{:S(2)}) copy-start(bf16[128,2048]{1,0:T(8,128)(2,1)S(1)} %all_gather.215) | copy-start | bytes 1572868
  56.1 119.2 %copy-start.123 = (bf16[128,512]{1,0:T(8,128)(2,1)}, bf16[128,512]{1,0:T(8,128)(2,1)S(1)}, u32[]{:S(2)}) copy-start(bf16[128,512]{1,0:T(8,128)(2,1)S(1)} %get-tuple-element.1997) | copy-start | bytes 393220
  56.1 71.8 %copy-start.157 = (u32[128]{0:T(128)S(1)}, u32[128]{0:T(128)}, u32[]{:S(2)}) copy-start(u32[128]{0:T(128)} %constant.517) | copy-start | bytes 1540
  94.7 82.1 %copy-start.55 = (bf16[128,864]{0,1:T(8,128)(2,1)}, bf16[128,864]{0,1:T(8,128)(2,1)S(1)}, u32[]{:S(2)}) copy-start(bf16[128,864]{0,1:T(8,128)(2,1)S(1)} %fusion.162) | copy-start | bytes 663556
  95.9 238.9 %all-gather.34.cloned.1.call-start = ((), (), s32[]{:S(2)}) async-start(), calls=%async_computation.35 | async-start | bytes 3760128 | tf_op jit(solution)/shard_map/all_gather | solution.py:197
  96.5 242.2 %all-gather.44.cloned.1.call-start = ((), (), s32[]{:S(2)}) async-start(), calls=%async_computation.40 | async-start | bytes 3760128 | tf_op jit(solution)/shard_map/all_gather | solution.py:198
  97.1 265.9 %reduce-scatter.33.cloned.1.call-start = ((), (), s32[]{:S(2)}) async-start(), calls=%async_computation.20 | async-start | bytes 655360 | tf_op jit(solution)/shard_map/reduce_scatter | solution.py:173
  97.2 234.9 %copy-start.154 = (f32[128]{0:T(128)}, f32[128]{0:T(128)S(1)}, u32[]{:S(2)}) copy-start(f32[128]{0:T(128)S(1)} %add_convert_fusion.11) | copy-start | bytes 1540
  338.7 38.5 %copy-start.116 = (bf16[128,864]{0,1:T(8,128)(2,1)}, bf16[128,864]{0,1:T(8,128)(2,1)S(1)}, u32[]{:S(2)}) copy-start(bf16[128,864]{0,1:T(8,128)(2,1)S(1)} %get-tuple-element.2000) | copy-start | bytes 663556
  342.4 66.0 %all-gather.48.cloned.1.call-start = ((), (), s32[]{:S(2)}) async-start(), calls=%async_computation.42 | async-start | bytes 3760128 | tf_op jit(solution)/shard_map/all_gather | solution.py:200
  343.1 109.3 %all-gather.46.cloned.1.call-start = ((), (), s32[]{:S(2)}) async-start(), calls=%async_computation.41 | async-start | bytes 3760128 | tf_op jit(solution)/shard_map/all_gather | solution.py:201
  343.9 152.5 %all-gather.32.cloned.1.call-start = ((), (), s32[]{:S(2)}) async-start(), calls=%async_computation.34 | async-start | bytes 3760128 | tf_op jit(solution)/shard_map/all_gather | solution.py:202
  344.4 175.4 %reduce-scatter.35.cloned.1.call-start = ((), (), s32[]{:S(2)}) async-start(), calls=%async_computation.21 | async-start | bytes 655360 | tf_op jit(solution)/shard_map/reduce_scatter | solution.py:173
  377.2 79.1 %copy-start.43 = (bf16[128,2048]{1,0:T(8,128)(2,1)}, bf16[128,2048]{1,0:T(8,128)(2,1)S(1)}, u32[]{:S(2)}) copy-start(bf16[128,2048]{1,0:T(8,128)(2,1)S(1)} %all_gather.228) | copy-start | bytes 1572868
  411.4 84.9 %copy-start.84 = (f32[128,864]{0,1:T(8,128)}, f32[128,864]{0,1:T(8,128)S(1)}, u32[]{:S(2)}) copy-start(f32[128,864]{0,1:T(8,128)S(1)} %fusion.10) | copy-start | bytes 1327108
  496.4 45.3 %copy-start = (bf16[1,2048,864]{1,2,0:T(8,128)(2,1)S(1)}, bf16[1,2048,864]{1,2,0:T(8,128)(2,1)}, u32[]{:S(2)}) copy-start(bf16[1,2048,864]{1,2,0:T(8,128)(2,1)} %all-gather.36.cloned.1.call-done) | copy-start | bytes 10616836
  500.2 96.2 %all-gather.50.cloned.1.call-start = ((), (), s32[]{:S(2)}) async-start(), calls=%async_computation.43 | async-start | bytes 7520256 | tf_op jit(solution)/shard_map/all_gather | solution.py:14
  519.9 22.9 copy-start.4
  521.1 6.6 collective-permute-start
  545.1 330.0 %reduce-scatter.37.cloned.1.call-start = ((), (), s32[]{:S(2)}) async-start(), calls=%async_computation.22 | async-start | bytes 655360 | tf_op jit(solution)/shard_map/reduce_scatter | solution.py:173
  854.6 64.8 %reduce-scatter.39.cloned.1.call-start = ((), (), s32[]{:S(2)}) async-start(), calls=%async_computation.23 | async-start | bytes 655360 | tf_op jit(solution)/shard_map/reduce_scatter | solution.py:173
  896.2 99.4 %all-gather.52.cloned.1.call-start = ((), (), s32[]{:S(2)}) async-start(), calls=%async_computation.44 | async-start | bytes 7520256 | tf_op jit(solution)/shard_map/all_gather | solution.py:14
  921.3 6.5 collective-permute-start.1
  944.1 333.2 %reduce-scatter.41.cloned.1.call-start = ((), (), s32[]{:S(2)}) async-start(), calls=%async_computation.24 | async-start | bytes 655360 | tf_op jit(solution)/shard_map/reduce_scatter | solution.py:173
  1250.7 72.4 %reduce-scatter.55.cloned.1.call-start = ((), (), s32[]{:S(2)}) async-start(), calls=%async_computation.31 | async-start | bytes 655360 | tf_op jit(solution)/shard_map/reduce_scatter | solution.py:173
  1297.3 49.3 %reduce-scatter.43.cloned.1.call-start = ((), (), s32[]{:S(2)}) async-start(), calls=%async_computation.25 | async-start | bytes 655360 | tf_op jit(solution)/shard_map/reduce_scatter | solution.py:186
  1306.2 113.3 %all-gather.54.cloned.1.call-start = ((), (), s32[]{:S(2)}) async-start(), calls=%async_computation.45 | async-start | bytes 7520256 | tf_op jit(solution)/shard_map/all_gather | solution.py:37
  1370.0 351.3 %reduce-scatter.45.cloned.1.call-start = ((), (), s32[]{:S(2)}) async-start(), calls=%async_computation.26 | async-start | bytes 655360 | tf_op jit(solution)/shard_map/reduce_scatter | solution.py:186
  1700.7 75.4 %reduce-scatter.47.cloned.1.call-start = ((), (), s32[]{:S(2)}) async-start(), calls=%async_computation.27 | async-start | bytes 655360 | tf_op jit(solution)/shard_map/reduce_scatter | solution.py:186
  1725.7 7.5 collective-permute-start.2
  1752.8 96.9 %all-gather.56.cloned.1.call-start = ((), (), s32[]{:S(2)}) async-start(), calls=%async_computation.46 | async-start | bytes 7520256 | tf_op jit(solution)/shard_map/all_gather | solution.py:37
  1800.1 347.6 %reduce-scatter.49.cloned.1.call-start = ((), (), s32[]{:S(2)}) async-start(), calls=%async_computation.28 | async-start | bytes 655360 | tf_op jit(solution)/shard_map/reduce_scatter | solution.py:186
  2127.1 75.5 %reduce-scatter.51.cloned.1.call-start = ((), (), s32[]{:S(2)}) async-start(), calls=%async_computation.29 | async-start | bytes 655360 | tf_op jit(solution)/shard_map/reduce_scatter | solution.py:186
  2152.1 7.5 collective-permute-start.3
  2179.1 143.9 %all-gather.58.cloned.1.call-start = ((), (), s32[]{:S(2)}) async-start(), calls=%async_computation.47 | async-start | bytes 7520256 | tf_op jit(solution)/shard_map/all_gather | solution.py:37
  2226.1 385.9 %reduce-scatter.57.cloned.1.call-start = ((), (), s32[]{:S(2)}) async-start(), calls=%async_computation.32 | async-start | bytes 2228224 | tf_op jit(solution)/shard_map/reduce_scatter | solution.py:211
  2246.6 367.1 %reduce-scatter.71.cloned.1.call-start = ((), (), s32[]{:S(2)}) async-start(), calls=%async_computation.53 | async-start | bytes 3899392
  2260.2 354.6 %reduce-scatter.69.cloned.1.call-start = ((), (), s32[]{:S(2)}) async-start(), calls=%async_computation.52 | async-start | bytes 3899392
  2274.6 341.4 %reduce-scatter.67.cloned.1.call-start = ((), (), s32[]{:S(2)}) async-start(), calls=%async_computation.51 | async-start | bytes 3899392
  2287.0 332.5 %reduce-scatter.65.cloned.1.call-start = ((), (), s32[]{:S(2)}) async-start(), calls=%async_computation.50 | async-start | bytes 3899392
  2300.7 375.5 %reduce-scatter.63.cloned.1.call-start = ((), (), s32[]{:S(2)}) async-start(), calls=%async_computation.49 | async-start | bytes 3899392
  2319.5 381.4 %reduce-scatter.53.cloned.1.call-start = ((), (), s32[]{:S(2)}) async-start(), calls=%async_computation.30 | async-start | bytes 655360 | tf_op jit(solution)/shard_map/reduce_scatter | solution.py:186
  2323.0 258.4 %copy-start.144 = (f32[128,2]{0,1:T(2,128)S(1)}, f32[128,2]{0,1:T(2,128)}, u32[]{:S(2)}) copy-start(f32[128,2]{0,1:T(2,128)} %get-tuple-element.1960) | copy-start | bytes 3076
  2595.6 169.1 %reduce-scatter.59.cloned.1.call-start = ((), (), s32[]{:S(2)}) async-start(), calls=%async_computation.33 | async-start | bytes 2228224 | tf_op jit(solution)/shard_map/reduce_scatter | solution.py:214
  2599.5 232.7 %reduce-scatter.61.cloned.1.call-start = ((), (), s32[]{:S(2)}) async-start(), calls=%async_computation.48 | async-start | bytes 3899392
  2611.2 89.8 %copy-start.34 = (f32[3,32,2048]{2,1,0:T(8,128)S(1)}, f32[3,32,2048]{2,1,0:T(8,128)}, u32[]{:S(2)}) copy-start(f32[3,32,2048]{2,1,0:T(8,128)} %copy-done.33) | copy-start | bytes 2359300
  2611.2 90.9 %copy-start.133 = (f32[2048]{0:T(1024)S(1)}, f32[2048]{0:T(1024)}, u32[]{:S(2)}) copy-start(f32[2048]{0:T(1024)} %get-tuple-element.1744) | copy-start | bytes 24580
  2611.2 90.9 %copy-start.135 = (f32[2048]{0:T(1024)S(1)}, f32[2048]{0:T(1024)}, u32[]{:S(2)}) copy-start(f32[2048]{0:T(1024)} %get-tuple-element.1742) | copy-start | bytes 24580
  2611.2 128.0 %copy-start.111 = (f32[32,2048]{1,0:T(8,128)S(1)}, f32[32,2048]{1,0:T(8,128)}, u32[]{:S(2)}) copy-start(f32[32,2048]{1,0:T(8,128)} %get-tuple-element.1906) | copy-start | bytes 786436
  2613.6 126.6 %copy-start.108 = (f32[1,1,32,2048]{3,2,1,0:T(8,128)S(1)}, f32[1,1,32,2048]{3,2,1,0:T(8,128)}, u32[]{:S(2)}) copy-start(f32[1,1,32,2048]{3,2,1,0:T(8,128)} %get-tuple-element.1950) | copy-start | bytes 786436
  2613.6 126.6 %copy-start.109 = (f32[1,1,32,2048]{3,2,1,0:T(8,128)S(1)}, f32[1,1,32,2048]{3,2,1,0:T(8,128)}, u32[]{:S(2)}) copy-start(f32[1,1,32,2048]{3,2,1,0:T(8,128)} %get-tuple-element.1935) | copy-start | bytes 786436
  2613.7 126.6 %copy-start.110 = (f32[1,1,32,2048]{3,2,1,0:T(8,128)S(1)}, f32[1,1,32,2048]{3,2,1,0:T(8,128)}, u32[]{:S(2)}) copy-start(f32[1,1,32,2048]{3,2,1,0:T(8,128)} %get-tuple-element.1952) | copy-start | bytes 786436
  (136 other events, 465.9 us)
Sparse Core Ops, SparseCore 0:
  9.7 37.4 all-gather.39
  48.8 42.7 all-gather.35
  93.3 33.9 all-gather.37
  129.4 47.3 all-gather.41
  178.2 43.0 all-gather.33
  222.7 42.4 all-gather.43
  342.5 20.2 reduce-scatter.32
  364.4 43.9 all-gather.47
  410.0 42.4 all-gather.45
  453.9 42.4 all-gather.31
  500.3 19.5 reduce-scatter.34
  545.3 51.0 all-gather.49
  854.7 20.4 reduce-scatter.36
  896.3 22.9 reduce-scatter.38
  944.3 51.2 all-gather.51
  1250.8 20.4 reduce-scatter.40
  1297.4 25.6 reduce-scatter.54
  1325.4 21.1 reduce-scatter.42
  1370.1 49.3 all-gather.53
  1700.8 20.4 reduce-scatter.44
  1752.9 23.2 reduce-scatter.46
  1800.2 49.3 all-gather.55
  2127.2 20.4 reduce-scatter.48
  2179.3 23.2 reduce-scatter.50
  2226.3 49.3 all-gather.57
  2277.9 60.8 reduce-scatter.56
  2341.1 65.3 reduce-scatter.70
  2408.9 64.9 reduce-scatter.68
  2476.3 65.1 reduce-scatter.66
  2543.8 64.9 reduce-scatter.64
  2611.2 65.0 reduce-scatter.62
  2679.2 21.6 reduce-scatter.52
  2703.1 61.4 reduce-scatter.58
  2767.1 65.1 reduce-scatter.60
where the time goes:
time: 2880 us; the launch traced here: 2840 us
  local copies, waits for them, and re-layouts  868 us (30%)
  waiting for transfers between devices  649 us (23%)
  other arithmetic  424 us (15%)
  loops' own time  376 us (13%)
  blocking collectives  256 us (9%)
  matrix products  226 us (8%)
    dynamic_slice x288, local copies, waits for them, and re-layouts, entering_step(): part[at].astype(own.dtype)  421 us
    dynamic_slice x240, local copies, waits for them, and re-layouts, prefix_step(): part[k].astype(own.dtype)  322 us
    another operation x3, loops' own time, entering(): return lax.fori_loop(0, devices, entering_step, start)  189 us
    another operation x3, loops' own time, prefix(): return lax.fori_loop(0, devices, prefix_step, start)  187 us
    select_n x48, other arithmetic, entering_step(): return jax.tree.map(lambda a, b: jnp.where(reached, a, b), new, before)  129 us
    unnamed x40, waiting for transfers between devices  127 us
    reduce_scatter x6, waiting for transfers between devices, rows_back(): lax.psum_scatter(result.astype(jnp.bfloat16), 'tensor', scatter_dimension...  121 us
    select_n x48, other arithmetic, prefix_step(): return jax.tree.map(lambda a, b: jnp.where(reached, a, b), new, before)  97.1 us
  transfers between devices with their start and end apart: 38, of which 26 were waited for; matrix products, arithmetic and copies ran while one was open for 20% of the time, Pallas kernels for 0%

commit v1 on v0

v1 whole, which is shorter than its diff:
```python
import jax
import jax.numpy as jnp
from jax import lax
from jax.sharding import Mesh, PartitionSpec as P

epsilon = 1e-06
group_floor = 1.0
AXES = ("section", "x", "ylo", "core", "tensor")
DP = ("x", "ylo", "core")
f32 = jnp.float32
bf16 = jnp.bfloat16


def low(v):
    return v.astype(bf16)


def wide(v):
    return v.astype(f32)


def mm(a, b):
    return lax.dot_general(a, b, (((1,), (0,)), ((), ())), preferred_element_type=f32)


def mm_right(a, b):
    return lax.dot_general(a, b, (((1,), (1,)), ((), ())), preferred_element_type=f32)


def mm_left(a, b):
    return lax.dot_general(a, b, (((0,), (0,)), ((), ())), preferred_element_type=f32)


def swap(v, axis):
    return lax.ppermute(v, axis, [(0, 1), (1, 0)])


def cross(v):
    return lax.ppermute(v, ("section", "ylo"), [(0, 3), (1, 2), (2, 1), (3, 0)])


def turn(v, axis, by):
    n = lax.axis_size(axis)
    return lax.ppermute(v, axis, [(i, (i + by) % n) for i in range(n)])


def shift(v, axis, by):
    n = lax.axis_size(axis)
    return lax.ppermute(v, axis, [(i, i + by) for i in range(n) if 0 <= i + by < n])


def spread(rows):
    n = lax.axis_size("tensor")
    parts = [rows] + [turn(rows, "tensor", -k) for k in range(1, n)]
    own = jnp.concatenate(parts)
    return jnp.concatenate([own, swap(own, "core")])


def collect(partial):
    n = lax.axis_size("tensor")
    half = partial.shape[0] // 2
    share = half // n
    own = partial[:half] + wide(swap(low(partial[half:]), "core"))
    total = own[:share]
    for k in range(1, n):
        total = total + wide(turn(low(own[k * share : (k + 1) * share]), "tensor", k))
    return total


def pick(flag, a, b):
    return jnp.where(flag, a, b)


def side(flag, a, b):
    return jnp.where(flag == 0, jnp.concatenate([a, b]), jnp.concatenate([b, a]))


def rms_inverse(x):
    return lax.rsqrt(jnp.mean(x * x, axis=-1, keepdims=True) + epsilon)


def norm_back(x, gain, d_y):
    r = rms_inverse(x)
    gd = gain * d_y
    d_x = r * gd - x * (r * r * r) * jnp.mean(x * gd, axis=-1, keepdims=True)
    return d_x, jnp.sum(x * r * d_y, axis=0)


def earlier_states(state, ctx):
    fade = ctx["fade"]
    sent = low(state)
    other = wide(swap(sent, "ylo"))
    own = wide(sent)
    y = ctx["ylo"]
    first, second = pick(y == 0, own, other), pick(y == 0, other, own)
    pair = low(fade * first + second)
    total = wide(shift(pair, "x", 1))
    total = total + (fade**2) * wide(shift(pair, "x", 2)) + (fade**4) * wide(shift(pair, "x", 3))
    return pick(y == 0, total, fade * total + first)


def later_states(state, ctx):
    fade = ctx["fade"]
    sent = low(state)
    other = wide(swap(sent, "ylo"))
    own = wide(sent)
    y = ctx["ylo"]
    first, second = pick(y == 0, own, other), pick(y == 0, other, own)
    pair = low(first + fade * second)
    total = wide(shift(pair, "x", -1))
    total = total + (fade**2) * wide(shift(pair, "x", -2)) + (fade**4) * wide(shift(pair, "x", -3))
    return pick(y == 1, total, second + fade * total)


def silu(v):
    return v * jax.nn.sigmoid(v)


def forward(h, a_rows, ffn_gain, weights, ctx):
    w_kv, w_qg, w_out, w_gu, w_down = weights
    K, V, F = ctx["sizes"]
    kv = mm(a_rows, w_kv)
    k, v = low(kv[:, :K]), low(kv[:, K : K + V])
    faded_k = low(wide(k) * ctx["to_end"])
    state_in = low(earlier_states(mm_left(faded_k, v), ctx))
    qg = mm(a_rows, w_qg)
    q, ret_gate = low(qg[:, :K]), qg[:, K:]
    scores = low(mm_right(q, k) * ctx["decay_mask"])
    retained = mm(scores, v) + mm(q, state_in) * ctx["from_start"]
    n = lax.rsqrt(jnp.mean(retained * retained, axis=-1, keepdims=True) + group_floor)
    gated = low(silu(ret_gate) * (retained * n))
    mid = h + collect(mm_right(gated, w_out))
    b_rows = spread(low(mid * rms_inverse(mid) * ffn_gain))
    gu = mm(b_rows, w_gu)
    gate_pre, up_pre = gu[:, :F], gu[:, F:]
    hidden = low(silu(gate_pre) * up_pre)
    out = mid + collect(mm_right(hidden, w_down))
    record = (a_rows, k, v, q, state_in, scores, ret_gate, retained, gated, mid, b_rows, gu, hidden)
    return out, record


def backward(h, g_out, d_f, record, gains, weights, ctx):
    w_kv, w_qg, w_out, w_gu, w_down = weights
    attn_gain, ffn_gain = gains
    K, V, F = ctx["sizes"]
    a_rows, k, v, q, state_in, scores, ret_gate, retained, gated, mid, b_rows, gu, hidden = record
    d_hidden = mm(d_f, w_down)
    gate_pre, up_pre = gu[:, :F], gu[:, F:]
    s = jax.nn.sigmoid(gate_pre)
    d_gate = low(d_hidden * up_pre * s * (1.0 + gate_pre * (1.0 - s)))
    d_up = low(d_hidden * gate_pre * s)
    d_gu = jnp.concatenate([d_gate, d_up], axis=1)
    d_b = collect(mm_right(d_gu, w_gu))
    grad_down = low(mm_left(d_f, hidden))
    grad_gu = low(mm_left(b_rows, d_gu))
    d_norm, grad_ffn_gain = norm_back(mid, ffn_gain, d_b)
    d_mid = g_out + d_norm
    d_r = spread(low(d_mid))
    d_gated = mm(d_r, w_out)
    s = jax.nn.sigmoid(ret_gate)
    n = lax.rsqrt(jnp.mean(retained * retained, axis=-1, keepdims=True) + group_floor)
    d_ret_gate = low(d_gated * (retained * n) * s * (1.0 + ret_gate * (1.0 - s)))
    d_normed = d_gated * ret_gate * s
    d_ret = n * d_normed - retained * (n * n * n) * jnp.mean(
        retained * d_normed, axis=-1, keepdims=True
    )
    d_ret_low = low(d_ret)
    d_ret_start = low(d_ret * ctx["from_start"])
    beyond = low(later_states(mm_left(q, d_ret_start), ctx))
    grad_out = low(mm_left(d_r, gated))
    d_scores = low(mm_right(d_ret_low, v) * ctx["decay_mask"])
    d_q = low(mm(d_scores, k) + mm_right(d_ret_start, state_in))
    d_qg = jnp.concatenate([d_q, d_ret_gate], axis=1)
    grad_qg = low(mm_left(a_rows, d_qg))
    d_k = low(mm_left(d_scores, q) + mm_right(v, beyond) * ctx["to_end"])
    d_v = low(mm_left(scores, d_ret_low) + mm(k, beyond) * ctx["to_end"])
    d_kv = jnp.concatenate([d_k, d_v], axis=1)
    grad_kv = low(mm_left(a_rows, d_kv))
    d_kv_wide = jnp.pad(d_kv, ((0, 0), (0, w_kv.shape[1] - d_kv.shape[1])))
    d_a = collect(mm_right(d_qg, w_qg) + mm_right(d_kv_wide, w_kv))
    d_norm, grad_attn_gain = norm_back(h, attn_gain, d_a)
    return d_mid + d_norm, (grad_kv, grad_qg, grad_out, grad_gu, grad_down), (grad_attn_gain, grad_ffn_gain)


def halves(w, core):
    n = w.shape[1] // 2
    first, second = w[:, :n], w[:, n:]
    return pick(core == 0, first, second), pick(core == 0, second, first)


def bring(shards, ctx):
    core, section, ylo = ctx["core"], ctx["section"], ctx["ylo"]
    split = [halves(w, core) for w in shards]
    keep = jnp.concatenate([a for a, _ in split], axis=1)
    give = jnp.concatenate([b for _, b in split], axis=1)
    own = side(core, keep, swap(give, "core"))
    own_other = swap(own, "ylo")
    far_other = cross(own)
    far = swap(far_other, "ylo")
    mine = side(ylo, own, own_other)
    theirs = side(ylo, far, far_other)
    return pick(section == 0, mine, theirs), pick(section == 0, theirs, mine)


def gather_x(rows):
    return lax.all_gather(rows, "x", axis=0, tiled=True)


def settle(grad, layer, ctx):
    part = lax.psum_scatter(grad, "x", scatter_dimension=0, tiled=True)
    half = part.shape[0] // 2
    away = ctx["section"] != layer
    place = jnp.where(away, 1 - ctx["ylo"], ctx["ylo"])
    keep = pick(place == 0, part[:half], part[half:])
    give = pick(place == 0, part[half:], part[:half])
    total = wide(keep) + wide(swap(give, "ylo"))
    return total + wide(cross(low(total)))


def share_out(total, ctx):
    core = ctx["core"]
    half = total.shape[0] // 2
    keep = pick(core == 0, total[:half], total[half:])
    give = pick(core == 0, total[half:], total[:half])
    return keep, wide(swap(low(give), "core"))


def both(pair, lo, hi, ctx):
    keep, other = pair
    a, b = keep[:, lo:hi], other[:, lo:hi]
    return jnp.where(ctx["core"] == 0, jnp.concatenate([a, b], 1), jnp.concatenate([b, a], 1))


def body(
    ends_in,
    segments,
    decay_rate,
    attn_gain,
    w_query,
    w_key,
    w_value,
    w_gate_ret,
    w_out,
    ffn_gain,
    w_gate,
    w_up,
    w_down,
):
    section, core, tensor = (lax.axis_index(a) for a in ("section", "core", "tensor"))
    x_at, ylo = lax.axis_index("x"), lax.axis_index("ylo")
    K, V, F = w_query.shape[2] // 2, w_value.shape[2] // 2, w_gate.shape[2] // 2
    D = w_query.shape[1] * lax.axis_size("x") * 4

    ends = ends_in[0]
    mine = pick(section == 0, ends[0], ends[1])
    theirs = swap(pick(section == 0, ends[1], ends[0]), "section")
    h0 = pick(section == 0, mine, theirs)
    g1 = pick(section == 0, theirs, mine)

    stretch = segments.shape[1]
    rows = 2 * stretch
    share = stretch // lax.axis_size("tensor")
    own_docs = pick(section == 0, segments[0], segments[1])
    ring = (tensor * share + jnp.arange(stretch)) % stretch
    own_docs = lax.dynamic_slice_in_dim(jnp.concatenate([own_docs, own_docs]), tensor * share, stretch)
    docs = jnp.concatenate([own_docs, swap(own_docs, "core")])
    places = jnp.concatenate([core * stretch + ring, (1 - core) * stretch + ring])
    block = x_at * 2 + ylo
    scale = K ** (-0.5)

    decays_all = decay_rate[0]
    decays_far = swap(decays_all, "section")
    head = tensor * 2 + core

    def context(layer):
        rates = pick(section == layer, decays_all, decays_far)
        rate = lax.dynamic_index_in_dim(rates, head, 0, False)
        gap = places[:, None] - places[None, :]
        allowed = (gap >= 0) & (docs[:, None] == docs[None, :])
        decay_mask = jnp.where(allowed, jnp.exp(-rate * jnp.where(allowed, gap, 0).astype(f32)), 0.0) * scale
        to_end = jnp.exp(-rate * (rows - 1 - places).astype(f32)) * (docs == jnp.max(docs))
        linked = (docs == jnp.min(docs)) & (block > 0)
        from_start = jnp.exp(-rate * (places + 1).astype(f32)) * linked * scale
        return {
            "decay_mask": decay_mask,
            "to_end": to_end[:, None],
            "from_start": from_start[:, None],
            "fade": jnp.exp(-rate * rows),
            "ylo": ylo,
            "core": core,
            "section": section,
            "sizes": (K, V, F),
        }

    ctxs = (context(0), context(1))
    ctx = ctxs[0]

    gain_columns = jnp.stack([attn_gain[0], ffn_gain[0]], axis=1)
    gain_columns = jnp.concatenate([gain_columns, gain_columns], axis=1)
    kv0, kv1 = bring((w_key[0], w_value[0], gain_columns), ctx)
    qg0, qg1 = bring((w_query[0], w_gate_ret[0]), ctx)
    out0, out1 = bring((w_out[0].T,), ctx)
    gu0, gu1 = bring((w_gate[0], w_up[0]), ctx)
    down0, down1 = bring((w_down[0].T,), ctx)
    weights0 = tuple(gather_x(w) for w in (kv0, qg0, out0, gu0, down0))
    weights1 = tuple(gather_x(w) for w in (kv1, qg1, out1, gu1, down1))

    def gains_of(weights):
        columns = wide(weights[0][:, K + V : K + V + 2]).T
        return columns[0], columns[1]

    gains0, gains1 = gains_of(weights0), gains_of(weights1)

    h0_rows = wide(spread(h0))
    a0 = low(h0_rows * rms_inverse(h0_rows) * gains0[0])
    h0 = wide(h0)
    out_first, record0 = forward(h0, a0, gains0[1], weights0, ctxs[0])
    h1 = wide(low(out_first))
    a1 = spread(low(h1 * rms_inverse(h1) * gains1[0]))
    out_second, record1 = forward(h1, a1, gains1[1], weights1, ctxs[1])

    d_f1 = spread(g1)
    d_h1, grads1, gain_grads1 = backward(
        h1, wide(g1), d_f1, record1, gains1, weights1, ctxs[1]
    )
    settled1 = [settle(g, 1, ctx) for g in grads1]
    d_f0_rows = low(d_h1)
    d_h0, grads0, gain_grads0 = backward(
        h0, wide(d_f0_rows), spread(d_f0_rows), record0, gains0, weights0, ctxs[0]
    )
    settled0 = [settle(g, 0, ctx) for g in grads0]

    shared = [share_out(pick(section == 0, a, b), ctx) for a, b in zip(settled0, settled1)]
    kv, qg, out, gu, down = shared
    grad_key = both(kv, 0, K, ctx)
    grad_value = both(kv, K, K + V, ctx)
    grad_query = both(qg, 0, K, ctx)
    grad_gate_ret = both(qg, K, K + V, ctx)
    grad_out = both(out, 0, V, ctx).T
    grad_gate = both(gu, 0, F, ctx)
    grad_up = both(gu, F, 2 * F, ctx)
    grad_down = both(down, 0, F, ctx).T

    gain_grads = jnp.stack(gain_grads0 + gain_grads1)
    for axis, order in (
        ("tensor", ((0, 1), (1, 0), (2, 3), (3, 2))),
        ("tensor", ((0, 3), (3, 0), (1, 2), (2, 1))),
        ("core", ((0, 1), (1, 0))),
        ("x", ((0, 1), (1, 0), (2, 3), (3, 2))),
        ("x", ((0, 3), (3, 0), (1, 2), (2, 1))),
        ("ylo", ((0, 1), (1, 0))),
        ("section", ((0, 1), (1, 0))),
    ):
        gain_grads = gain_grads + lax.ppermute(gain_grads, axis, order)
    own_gains = pick(section == 0, gain_grads[:2], gain_grads[2:])
    width = attn_gain.shape[1]
    own_gains = lax.dynamic_slice_in_dim(own_gains, (block * 2 + core) * width, width, 1)

    kept = pick(section == 0, d_h0, out_second)
    passed = swap(pick(section == 0, out_second, d_h0), "section")
    ends_out = jnp.where(section == 0, jnp.stack([kept, passed]), jnp.stack([passed, kept]))
    return (
        ends_out[None],
        own_gains[:1],
        grad_query[None],
        grad_key[None],
        grad_value[None],
        grad_gate_ret[None],
        grad_out[None],
        own_gains[1:],
        grad_gate[None],
        grad_up[None],
        grad_down[None],
    )


def solution(mesh):
    fine = Mesh(mesh.devices.reshape(2, 4, 2, 2, 4), AXES)
    by_rows = P("section", DP, "tensor")
    by_columns = P("section", "tensor", DP)
    ends = P("section", None, DP + ("tensor",), None)
    gain = P("section", DP)
    return jax.shard_map(
        body,
        mesh=fine,
        in_specs=(
            ends,
            P(None, DP),
            P("section", None),
            gain,
            by_rows,
            by_rows,
            by_rows,
            by_rows,
            by_columns,
            gain,
            by_rows,
            by_rows,
            by_columns,
        ),
        out_specs=(
            ends,
            gain,
            by_rows,
            by_rows,
            by_rows,
            by_rows,
            by_columns,
            gain,
            by_rows,
            by_rows,
            by_columns,
        ),
        check_vma=False,
    )
```

time: 2880 us -> 864 us (0.30)
  local copies, waits for them, and re-layouts: 868 us -> 44.8 us
  loops' own time: 376 us -> 0 us
  other arithmetic: 424 us -> 85.1 us
  blocking collectives: 256 us -> 0 us
  waiting for transfers between devices: 649 us -> 458 us
  starting transfers between devices: 14.2 us -> 167 us
  matrix products: 226 us -> 77.8 us
    dynamic_slice x530 -> x2, local copies, waits for them, and re-layouts: 747 us -> 1.18 us  [context(): rate = lax.dynamic_index_in_dim(rates, head, 0, False)]
    another operation x6 -> x0, loops' own time: 376 us -> none  [the longest x3 189 us: entering(): return lax.fori_loop(0, devices, entering_step, start)]
    ppermute x4 -> x136, waiting for transfers between devices: 16.3 us -> 289 us  [the longest x48 103 us: turn(): return lax.ppermute(v, axis, [(i, (i + by) % n) for i in range(n)])]
    all_gather x14 -> x10, waiting for transfers between devices: 283 us -> 84.1 us  [gather_x(): return lax.all_gather(rows, 'x', axis=0, tiled=True)]
    all_gather x15 -> x0, blocking collectives: 191 us -> none  [the longest x6 67.3 us: spread_rows(): return lax.all_gather(row_block, 'tensor', axis=0, tiled=True)]
    select_n x98 -> x49, other arithmetic: 228 us -> 38.5 us  [the longest x38 32 us: pick(): return jnp.where(flag, a, b)]
    ppermute x4 -> x136, starting transfers between devices: 11.8 us -> 166 us  [the longest x54 61 us: swap(): return lax.ppermute(v, axis, [(0, 1), (1, 0)])]
    dot_general x111 -> x54, matrix products: 226 us -> 77.8 us  [the longest x18 30.1 us: mm(): lax.dot_general(a, b, (((1,), (0,)), ((), ())), preferred_element_type=f32)]
  transfers between devices with their start and end apart: 38 -> 156, of which waited for: 26 -> 99; matrix products, arithmetic and copies ran while one was open for 20% -> 20% of each run, Pallas kernels for 0% -> 0%
where the time goes in v1:
time: 864 us; the launch traced here: 854 us
  waiting for transfers between devices  458 us (53%)
  starting transfers between devices  167 us (19%)
  other arithmetic  85.1 us (10%)
  matrix products  77.8 us (9%)
  local copies, waits for them, and re-layouts  44.8 us (5%)
  between operations  21.5 us (2%)
    ppermute x48, waiting for transfers between devices, turn(): return lax.ppermute(v, axis, [(i, (i + by) % n) for i in range(n)])  103 us
    ppermute x54, waiting for transfers between devices, swap(): return lax.ppermute(v, axis, [(0, 1), (1, 0)])  89.7 us
    all_gather x10, waiting for transfers between devices, gather_x(): return lax.all_gather(rows, 'x', axis=0, tiled=True)  84.1 us
    reduce_scatter x10, waiting for transfers between devices, settle(): part = lax.psum_scatter(grad, 'x', scatter_dimension=0, tiled=True)  84 us
    ppermute x54, starting transfers between devices, swap(): return lax.ppermute(v, axis, [(0, 1), (1, 0)])  61 us
    ppermute x15, waiting for transfers between devices, cross(): return lax.ppermute(v, ('section', 'ylo'), [(0, 3), (1, 2), (2, 1), (3, 0)])  44.6 us
    ppermute x48, starting transfers between devices, turn(): return lax.ppermute(v, axis, [(i, (i + by) % n) for i in range(n)])  42.4 us
    ppermute x12, waiting for transfers between devices, shift(): lax.ppermute(v, axis, [(i, i + by) for i in range(n) if 0 <= i + by < n])  42.4 us
  transfers between devices with their start and end apart: 156, of which 99 were waited for; matrix products, arithmetic and copies ran while one was open for 20% of the time, Pallas kernels for 0%

profile of v1, /device:TPU:1, one launch (start us, length us, event | category | flops | bytes accessed | tf_op | source)
XLA Modules:
  0.0 854.2 jit_solution(5804623793806013263)
XLA Ops:
  16.3 8.2 collective-permute-done.7
  25.5 7.8 collective-permute-done.8
  41.0 8.2 collective-permute-done.11
  50.1 7.7 collective-permute-done.12
  65.2 5.5 collective-permute-done.21
  71.6 4.9 collective-permute-done.22
  83.9 10.2 %collective-permute-done.33 = bf16[256,864]{0,1:T(8,128)(2,1)S(1)} collective-permute-done((bf16[256,864]{0,1:T(8,128)(2,1)S(1)}, bf16[256,864]{0,1:T(8,128)(2,1)S(1)}, u32[]{:S(2)}, u32[]{:S(2)}) %collective-permute-start.33) | collective-permute-done | bytes 442400 | tf_op jit(solution)/shard_map/ppermute | solution.py:39
  95.0 9.7 %collective-permute-done.34 = bf16[256,864]{0,1:T(8,128)(2,1)S(1)} collective-permute-done((bf16[256,864]{0,1:T(8,128)(2,1)S(1)}, bf16[256,864]{0,1:T(8,128)(2,1)S(1)}, u32[]{:S(2)}, u32[]{:S(2)}) %collective-permute-start.34) | collective-permute-done | bytes 442400 | tf_op jit(solution)/shard_map/ppermute | solution.py:35
  117.3 3.9 collective-permute-done.37
  124.3 4.2 collective-permute-done.38
  137.0 3.8 collective-permute-start.1
  141.6 4.5 collective-permute-done.1
  146.3 3.5 collective-permute-done.3
  154.1 3.1 convolution_convert_fusion.11
  160.6 3.8 collective-permute-done.15
  164.4 4.5 collective-permute-start.18
  173.0 9.6 %collective-permute-done.18 = bf16[256,432]{0,1:T(8,128)(2,1)S(1)} collective-permute-done((bf16[256,432]{0,1:T(8,128)(2,1)S(1)}, bf16[256,432]{0,1:T(8,128)(2,1)S(1)}, u32[]{:S(2)}, u32[]{:S(2)}) %collective-permute-start.18) | collective-permute-done | bytes 221216 | tf_op jit(solution)/shard_map/ppermute | solution.py:49
  182.6 6.5 collective-permute-done.16
  201.3 3.2 collective-permute-done.26
  206.1 3.8 collective-permute-done.24
  212.4 3.2 collective-permute-done.27
  216.4 4.3 collective-permute-done.29
  223.0 3.5 fusion.167
  232.4 34.0 %all-gather.21.cloned.1.call-done = bf16[2048,690]{0,1:T(8,128)(2,1)} async-done(((bf16[512,690]{0,1:T(8,128)(2,1)}), bf16[2048,690]{0,1:T(8,128)(2,1)}) %all-gather.21.cloned.1.call-update) | async-done | bytes 2826256 | tf_op jit(solution)/shard_map/all_gather | solution.py:206
  273.2 3.3 collective-permute-done.42
  277.0 4.1 collective-permute-done.40
  299.0 6.1 all-gather.23.cloned.1.call-done
  315.8 6.6 collective-permute-done.50
  328.9 8.9 %all-gather.25.cloned.1.call-done = bf16[2048,432]{0,1:T(8,128)(2,1)} async-done(((bf16[512,432]{0,1:T(8,128)(2,1)}), bf16[2048,432]{0,1:T(8,128)(2,1)}) %all-gather.25.cloned.1.call-update) | async-done | bytes 1769488 | tf_op jit(solution)/shard_map/all_gather | solution.py:206
  356.4 4.0 collective-permute-done.52
  367.8 4.4 collective-permute-done.61
  375.9 8.5 all-gather.29.cloned.1.call-done
  384.3 4.4 fusion.171
  388.7 26.2 %all-gather.27.cloned.1.call-done = bf16[2048,432]{0,1:T(8,128)(2,1)} async-done(((bf16[512,432]{0,1:T(8,128)(2,1)}), bf16[2048,432]{0,1:T(8,128)(2,1)}) %all-gather.27.cloned.1.call-update) | async-done | bytes 1769488 | tf_op jit(solution)/shard_map/all_gather | solution.py:206
  414.9 3.6 multiply_convert_fusion.8
  427.7 4.4 collective-permute-done.66
  432.9 3.8 collective-permute-done.64
  445.2 4.3 collective-permute-done.69
  460.2 5.4 collective-permute-done.71
  470.1 10.1 %collective-permute-done.74 = bf16[256,432]{0,1:T(8,128)(2,1)S(1)} collective-permute-done((bf16[256,432]{0,1:T(8,128)(2,1)S(1)}, bf16[256,432]{0,1:T(8,128)(2,1)S(1)}, u32[]{:S(2)}, u32[]{:S(2)}) %collective-permute-start.74) | collective-permute-done | bytes 221216 | tf_op jit(solution)/shard_map/ppermute | solution.py:49
  496.5 4.3 collective-permute-done.78
  501.6 3.7 collective-permute-done.76
  507.2 3.3 collective-permute-done.79
  511.2 4.4 collective-permute-done.81
  520.7 3.4 convolution_convert_fusion.4
  525.2 4.1 convolution_convert_fusion
  541.8 3.4 collective-permute-done.86
  547.0 3.8 collective-permute-done.84
  552.8 3.1 collective-permute-done.87
  556.8 4.3 collective-permute-done.89
  574.1 4.1 convolution_convert_fusion.1
  579.9 5.4 collective-permute-done.91
  592.9 7.0 collective-permute-done.94
  604.8 5.4 collective-permute-start.95
  614.1 3.8 collective-permute-start.98
  619.6 3.6 collective-permute-done.98
  668.8 3.3 collective-permute-done.131
  680.6 5.3 collective-permute-start.135
  693.1 3.9 reduce-scatter.19.cloned.1.call-done
  702.1 10.1 %collective-permute-done.121 = bf16[256,432]{0,1:T(8,128)(2,1)S(1)} collective-permute-done((bf16[256,432]{0,1:T(8,128)(2,1)S(1)}, bf16[256,432]{0,1:T(8,128)(2,1)S(1)}, u32[]{:S(2)}, u32[]{:S(2)}) %collective-permute-start.121) | collective-permute-done | bytes 221216 | tf_op jit(solution)/shard_map/ppermute | solution.py:35
  716.0 3.9 collective-permute-done.122
  724.9 9.6 %reduce-scatter.11.cloned.1.call-done = bf16[512,688]{0,1:T(8,128)(2,1)} async-done(((bf16[2048,688]{0,1:T(8,128)(2,1)}), bf16[512,688]{0,1:T(8,128)(2,1)}) %reduce-scatter.11.cloned.1.call-update) | async-done | bytes 704528 | tf_op jit(solution)/shard_map/reduce_scatter | solution.py:210
  738.5 39.9 %reduce-scatter.23.cloned.1.call-done = bf16[512,864]{0,1:T(8,128)(2,1)} async-done(((bf16[2048,864]{0,1:T(8,128)(2,1)}), bf16[512,864]{0,1:T(8,128)(2,1)}) %reduce-scatter.23.cloned.1.call-update) | async-done | bytes 884752 | tf_op jit(solution)/shard_map/reduce_scatter | solution.py:210
  785.5 30.6 %reduce-scatter.15.cloned.1.call-done = bf16[512,688]{0,1:T(8,128)(2,1)} async-done(((bf16[2048,688]{0,1:T(8,128)(2,1)}), bf16[512,688]{0,1:T(8,128)(2,1)}) %reduce-scatter.15.cloned.1.call-update) | async-done | bytes 704528 | tf_op jit(solution)/shard_map/reduce_scatter | solution.py:210
  (807 shorter events, 389.2 us)
Async XLA Ops:
  7.2 146.2 %all-gather.11.cloned.1.call-start = ((), (), s32[]{:S(2)}) async-start(), calls=%async_computation.10 | async-start | bytes 3563520 | tf_op jit(solution)/shard_map/all_gather | solution.py:206
  13.4 11.1 %collective-permute-start.7 = (bf16[256,690]{0,1:T(8,128)(2,1)S(1)}, bf16[256,690]{0,1:T(8,128)(2,1)S(1)}, u32[]{:S(2)}, u32[]{:S(2)}) collective-permute-start(bf16[256,690]{0,1:T(8,128)(2,1)S(1)} %maximum_select_fusion.18), channel_id=1, source_target_pairs={{0,72},{8,64},{64,8},{72,0},{1,73},{9,65},{65,9},{73,1},{2,74},{10... | collective-permute-start | bytes 1059848 | tf_op jit(solution)/shard_map/ppermute | solution.py:39
  34.9 122.7 %all-gather.13.cloned.1.call-start = ((), (), s32[]{:S(2)}) async-start(), calls=%async_computation.11 | async-start | bytes 3522560 | tf_op jit(solution)/shard_map/all_gather | solution.py:206
  38.4 10.7 %collective-permute-start.11 = (bf16[256,688]{0,1:T(8,128)(2,1)S(1)}, bf16[256,688]{0,1:T(8,128)(2,1)S(1)}, u32[]{:S(2)}, u32[]{:S(2)}) collective-permute-start(bf16[256,688]{0,1:T(8,128)(2,1)S(1)} %maximum_select_fusion.19), channel_id=1, source_target_pairs={{0,72},{8,64},{64,8},{72,0},{1,73},{9,65},{65,9},{73,1},{2,74},{10... | collective-permute-start | bytes 1056776 | tf_op jit(solution)/shard_map/ppermute | solution.py:39
  59.4 132.1 %all-gather.15.cloned.1.call-start = ((), (), s32[]{:S(2)}) async-start(), calls=%async_computation.12 | async-start | bytes 2211840 | tf_op jit(solution)/shard_map/all_gather | solution.py:206
  77.7 145.2 %all-gather.17.cloned.1.call-start = ((), (), s32[]{:S(2)}) async-start(), calls=%async_computation.13 | async-start | bytes 4423680 | tf_op jit(solution)/shard_map/all_gather | solution.py:206
  81.3 12.8 %collective-permute-start.33 = (bf16[256,864]{0,1:T(8,128)(2,1)S(1)}, bf16[256,864]{0,1:T(8,128)(2,1)S(1)}, u32[]{:S(2)}, u32[]{:S(2)}) collective-permute-start(bf16[256,864]{0,1:T(8,128)(2,1)S(1)} %maximum_select_fusion.9), channel_id=1, source_target_pairs={{0,72},{8,64},{64,8},{72,0},{1,73},{9,65},{65,9},{73,1},{2,74},{10... | collective-permute-start | bytes 1327112 | tf_op jit(solution)/shard_map/ppermute | solution.py:39
  83.9 11.2 %collective-permute-start.32 = (bf16[256,864]{0,1:T(8,128)(2,1)S(1)}, bf16[256,864]{0,1:T(8,128)(2,1)S(1)}, u32[]{:S(2)}, u32[]{:S(2)}) collective-permute-start(bf16[256,864]{0,1:T(8,128)(2,1)S(1)} %maximum_select_fusion.9), channel_id=1, source_target_pairs={{0,8},{8,0},{1,9},{9,1},{2,10},{10,2},{3,11},{11,3},{4,12},{12,4},... | collective-permute-start | bytes 1327112 | tf_op jit(solution)/shard_map/ppermute | solution.py:35
  94.1 10.7 %collective-permute-start.34 = (bf16[256,864]{0,1:T(8,128)(2,1)S(1)}, bf16[256,864]{0,1:T(8,128)(2,1)S(1)}, u32[]{:S(2)}, u32[]{:S(2)}) collective-permute-start(bf16[256,864]{0,1:T(8,128)(2,1)S(1)} %collective-permute-done.33), channel_id=1, source_target_pairs={{0,8},{8,0},{1,9},{9,1},{2,10},{10,2},{3,11},{11,3},{4,12},{12,4},... | collective-permute-start | bytes 1327112 | tf_op jit(solution)/shard_map/ppermute | solution.py:35
  106.5 121.4 %all-gather.19.cloned.1.call-start = ((), (), s32[]{:S(2)}) async-start(), calls=%async_computation.14 | async-start | bytes 2211840 | tf_op jit(solution)/shard_map/all_gather | solution.py:206
  106.6 29.7 %collective-permute-start = (bf16[32,2048]{1,0:T(8,128)(2,1)S(1)}, bf16[32,2048]{1,0:T(8,128)(2,1)S(1)}, u32[]{:S(2)}, u32[]{:S(2)}) collective-permute-start(bf16[32,2048]{1,0:T(8,128)(2,1)S(1)} %select_bitcast_fusion.1), channel_id=1, source_target_pairs={{0,64},{64,0},{1,65},{65,1},{2,66},{66,2},{3,67},{67,3},{4,68},{68... | collective-permute-start | bytes 393224 | tf_op jit(solution)/shard_map/ppermute | solution.py:35
  109.2 20.6 %collective-permute-start.14 = (f32[8]{0:T(128)S(1)}, f32[8]{0:T(128)S(1)}, u32[]{:S(2)}, u32[]{:S(2)}) collective-permute-start(f32[8]{0:T(128)S(1)} %bitcast.184), channel_id=1, source_target_pairs={{0,64},{64,0},{1,65},{65,1},{2,66},{66,2},{3,67},{67,3},{4,68},{68... | collective-permute-start | bytes 104 | tf_op jit(solution)/shard_map/ppermute | solution.py:35
  116.6 15.8 %collective-permute-start.13 = (s32[128]{0:T(128)S(1)}, s32[128]{0:T(128)S(1)}, u32[]{:S(2)}, u32[]{:S(2)}) collective-permute-start(s32[128]{0:T(128)S(1)} %get-tuple-element.82), channel_id=1, source_target_pairs={{0,4},{4,0},{1,5},{5,1},{2,6},{6,2},{3,7},{7,3},{8,12},{12,8},{9,1... | collective-permute-start | bytes 1544 | tf_op jit(solution)/shard_map/ppermute | solution.py:35
  129.8 136.6 %all-gather.21.cloned.1.call-start = ((), (), s32[]{:S(2)}) async-start(), calls=%async_computation.15 | async-start | bytes 3563520 | tf_op jit(solution)/shard_map/all_gather | solution.py:206
  153.3 151.8 %all-gather.23.cloned.1.call-start = ((), (), s32[]{:S(2)}) async-start(), calls=%async_computation.16 | async-start | bytes 3522560 | tf_op jit(solution)/shard_map/all_gather | solution.py:206
  164.4 18.2 %collective-permute-start.18 = (bf16[256,432]{0,1:T(8,128)(2,1)S(1)}, bf16[256,432]{0,1:T(8,128)(2,1)S(1)}, u32[]{:S(2)}, u32[]{:S(2)}) collective-permute-start(bf16[256,432]{0,1:T(8,128)(2,1)S(1)} %fusion.20), channel_id=1, source_target_pairs={{0,48},{1,49},{2,50},{3,51},{4,52},{5,53},{6,54},{7,55},{8,56},{9,... | collective-permute-start | bytes 663560 | tf_op jit(solution)/shard_map/ppermute | solution.py:49
  168.9 13.7 %collective-permute-start.17 = (bf16[256,432]{0,1:T(8,128)(2,1)S(1)}, bf16[256,432]{0,1:T(8,128)(2,1)S(1)}, u32[]{:S(2)}, u32[]{:S(2)}) collective-permute-start(bf16[256,432]{0,1:T(8,128)(2,1)S(1)} %fusion.20), channel_id=1, source_target_pairs={{0,32},{16,48},{1,33},{17,49},{2,34},{18,50},{3,35},{19,51},{4,36}... | collective-permute-start | bytes 663560 | tf_op jit(solution)/shard_map/ppermute | solution.py:49
  170.3 18.9 %collective-permute-start.16 = (bf16[256,432]{0,1:T(8,128)(2,1)S(1)}, bf16[256,432]{0,1:T(8,128)(2,1)S(1)}, u32[]{:S(2)}, u32[]{:S(2)}) collective-permute-start(bf16[256,432]{0,1:T(8,128)(2,1)S(1)} %fusion.20), channel_id=1, source_target_pairs={{0,16},{16,32},{32,48},{1,17},{17,33},{33,49},{2,18},{18,34},{34,5... | collective-permute-start | bytes 663560 | tf_op jit(solution)/shard_map/ppermute | solution.py:49
  196.7 141.1 %all-gather.25.cloned.1.call-start = ((), (), s32[]{:S(2)}) async-start(), calls=%async_computation.17 | async-start | bytes 2211840 | tf_op jit(solution)/shard_map/all_gather | solution.py:206
  231.5 35.7 %collective-permute-start.39 = (bf16[128,2048]{1,0:T(8,128)(2,1)S(1)}, bf16[128,2048]{1,0:T(8,128)(2,1)}, u32[]{:S(2)}, u32[]{:S(2)}) collective-permute-start(bf16[128,2048]{1,0:T(8,128)(2,1)S(1)} %slice.1068), channel_id=1, source_target_pairs={{0,4},{4,0},{1,5},{5,1},{2,6},{6,2},{3,7},{7,3},{8,12},{12,8},{9,1... | collective-permute-start | bytes 1572872 | tf_op jit(solution)/shard_map/ppermute | solution.py:35
  232.4 152.0 %all-gather.29.cloned.1.call-start = ((), (), s32[]{:S(2)}) async-start(), calls=%async_computation.19 | async-start | bytes 4423680 | tf_op jit(solution)/shard_map/all_gather | solution.py:206
  284.7 56.2 %collective-permute-start.55 = (bf16[32,2048]{1,0:T(8,128)(2,1)S(1)}, bf16[32,2048]{1,0:T(8,128)(2,1)}, u32[]{:S(2)}, u32[]{:S(2)}) collective-permute-start(bf16[32,2048]{1,0:T(8,128)(2,1)S(1)} %get-tuple-element.59), channel_id=1, source_target_pairs={{0,3},{1,0},{2,1},{3,2},{4,7},{5,4},{6,5},{7,6},{8,11},{9,8},{10,9... | collective-permute-start | bytes 393224 | tf_op jit(solution)/shard_map/ppermute | solution.py:44
  287.2 53.8 %collective-permute-start.56 = (bf16[32,2048]{1,0:T(8,128)(2,1)S(1)}, bf16[32,2048]{1,0:T(8,128)(2,1)}, u32[]{:S(2)}, u32[]{:S(2)}) collective-permute-start(bf16[32,2048]{1,0:T(8,128)(2,1)S(1)} %get-tuple-element.59), channel_id=1, source_target_pairs={{0,2},{1,3},{2,0},{3,1},{4,6},{5,7},{6,4},{7,5},{8,10},{9,11},{10,... | collective-permute-start | bytes 393224 | tf_op jit(solution)/shard_map/ppermute | solution.py:44
  288.4 126.5 %all-gather.27.cloned.1.call-start = ((), (), s32[]{:S(2)}) async-start(), calls=%async_computation.18 | async-start | bytes 2211840 | tf_op jit(solution)/shard_map/all_gather | solution.py:206
  297.7 10.2 %collective-permute-start.47 = (bf16[256,432]{0,1:T(8,128)(2,1)S(1)}, bf16[256,432]{0,1:T(8,128)(2,1)}, u32[]{:S(2)}, u32[]{:S(2)}) collective-permute-start(bf16[256,432]{0,1:T(8,128)(2,1)S(1)} %convolution_convert_fusion.14), channel_id=1, source_target_pairs={{0,8},{8,0},{1,9},{9,1},{2,10},{10,2},{3,11},{11,3},{4,12},{12,4},... | collective-permute-start | bytes 663560 | tf_op jit(solution)/shard_map/ppermute | solution.py:35
  309.1 13.2 %collective-permute-start.50 = (bf16[256,432]{0,1:T(8,128)(2,1)S(1)}, bf16[256,432]{0,1:T(8,128)(2,1)S(1)}, u32[]{:S(2)}, u32[]{:S(2)}) collective-permute-start(bf16[256,432]{0,1:T(8,128)(2,1)S(1)} %fusion.22), channel_id=1, source_target_pairs={{0,48},{1,49},{2,50},{3,51},{4,52},{5,53},{6,54},{7,55},{8,56},{9,... | collective-permute-start | bytes 663560 | tf_op jit(solution)/shard_map/ppermute | solution.py:49
  311.6 12.1 %collective-permute-start.49 = (bf16[256,432]{0,1:T(8,128)(2,1)S(1)}, bf16[256,432]{0,1:T(8,128)(2,1)S(1)}, u32[]{:S(2)}, u32[]{:S(2)}) collective-permute-start(bf16[256,432]{0,1:T(8,128)(2,1)S(1)} %fusion.22), channel_id=1, source_target_pairs={{0,32},{16,48},{1,33},{17,49},{2,34},{18,50},{3,35},{19,51},{4,36}... | collective-permute-start | bytes 663560 | tf_op jit(solution)/shard_map/ppermute | solution.py:49
  313.3 13.0 %collective-permute-start.48 = (bf16[256,432]{0,1:T(8,128)(2,1)S(1)}, bf16[256,432]{0,1:T(8,128)(2,1)S(1)}, u32[]{:S(2)}, u32[]{:S(2)}) collective-permute-start(bf16[256,432]{0,1:T(8,128)(2,1)S(1)} %fusion.22), channel_id=1, source_target_pairs={{0,16},{16,32},{32,48},{1,17},{17,33},{33,49},{2,18},{18,34},{34,5... | collective-permute-start | bytes 663560 | tf_op jit(solution)/shard_map/ppermute | solution.py:49
  322.3 18.6 %collective-permute-start.57 = (bf16[32,2048]{1,0:T(8,128)(2,1)S(1)}, bf16[32,2048]{1,0:T(8,128)(2,1)}, u32[]{:S(2)}, u32[]{:S(2)}) collective-permute-start(bf16[32,2048]{1,0:T(8,128)(2,1)S(1)} %get-tuple-element.59), channel_id=1, source_target_pairs={{0,1},{1,2},{2,3},{3,0},{4,5},{5,6},{6,7},{7,4},{8,9},{9,10},{10,1... | collective-permute-start | bytes 393224 | tf_op jit(solution)/shard_map/ppermute | solution.py:44
  342.9 21.1 %collective-permute-start.58 = (bf16[128,2048]{1,0:T(8,128)(2,1)}, bf16[128,2048]{1,0:T(8,128)(2,1)}, u32[]{:S(2)}, u32[]{:S(2)}) collective-permute-start(bf16[128,2048]{1,0:T(8,128)(2,1)} %pad_maximum_fusion.3), channel_id=1, source_target_pairs={{0,4},{4,0},{1,5},{5,1},{2,6},{6,2},{3,7},{7,3},{8,12},{12,8},{9,1... | collective-permute-start | bytes 1572872 | tf_op jit(solution)/shard_map/ppermute | solution.py:35
  353.2 265.3 %reduce-scatter.29.cloned.1.call-start = ((), (), s32[]{:S(2)}) async-start(), calls=%async_computation.29 | async-start | bytes 2211840 | tf_op jit(solution)/shard_map/reduce_scatter | solution.py:210
  444.1 191.3 %reduce-scatter.21.cloned.1.call-start = ((), (), s32[]{:S(2)}) async-start(), calls=%async_computation.25 | async-start | bytes 2211840 | tf_op jit(solution)/shard_map/reduce_scatter | solution.py:210
  465.7 14.4 %collective-permute-start.74 = (bf16[256,432]{0,1:T(8,128)(2,1)S(1)}, bf16[256,432]{0,1:T(8,128)(2,1)S(1)}, u32[]{:S(2)}, u32[]{:S(2)}) collective-permute-start(bf16[256,432]{0,1:T(8,128)(2,1)S(1)} %fusion.24), channel_id=1, source_target_pairs={{48,0},{49,1},{50,2},{51,3},{52,4},{53,5},{54,6},{55,7},{56,8},{57... | collective-permute-start | bytes 663560 | tf_op jit(solution)/shard_map/ppermute | solution.py:49
  467.1 13.0 %collective-permute-start.73 = (bf16[256,432]{0,1:T(8,128)(2,1)S(1)}, bf16[256,432]{0,1:T(8,128)(2,1)S(1)}, u32[]{:S(2)}, u32[]{:S(2)}) collective-permute-start(bf16[256,432]{0,1:T(8,128)(2,1)S(1)} %fusion.24), channel_id=1, source_target_pairs={{32,0},{48,16},{33,1},{49,17},{34,2},{50,18},{35,3},{51,19},{36,4}... | collective-permute-start | bytes 663560 | tf_op jit(solution)/shard_map/ppermute | solution.py:49
  468.4 11.7 %collective-permute-start.72 = (bf16[256,432]{0,1:T(8,128)(2,1)S(1)}, bf16[256,432]{0,1:T(8,128)(2,1)S(1)}, u32[]{:S(2)}, u32[]{:S(2)}) collective-permute-start(bf16[256,432]{0,1:T(8,128)(2,1)S(1)} %fusion.24), channel_id=1, source_target_pairs={{16,0},{32,16},{48,32},{17,1},{33,17},{49,33},{18,2},{34,18},{50,3... | collective-permute-start | bytes 663560 | tf_op jit(solution)/shard_map/ppermute | solution.py:49
  491.0 172.7 %reduce-scatter.27.cloned.1.call-start = ((), (), s32[]{:S(2)}) async-start(), calls=%async_computation.28 | async-start | bytes 2211840 | tf_op jit(solution)/shard_map/reduce_scatter | solution.py:210
  520.7 154.5 %reduce-scatter.13.cloned.1.call-start = ((), (), s32[]{:S(2)}) async-start(), calls=%async_computation.21 | async-start | bytes 3522560 | tf_op jit(solution)/shard_map/reduce_scatter | solution.py:210
  524.1 161.7 %reduce-scatter.25.cloned.1.call-start = ((), (), s32[]{:S(2)}) async-start(), calls=%async_computation.27 | async-start | bytes 4423680 | tf_op jit(solution)/shard_map/reduce_scatter | solution.py:210
  529.3 161.0 %reduce-scatter.17.cloned.1.call-start = ((), (), s32[]{:S(2)}) async-start(), calls=%async_computation.23 | async-start | bytes 3522560 | tf_op jit(solution)/shard_map/reduce_scatter | solution.py:210
  532.6 164.4 %reduce-scatter.19.cloned.1.call-start = ((), (), s32[]{:S(2)}) async-start(), calls=%async_computation.24 | async-start | bytes 2211840 | tf_op jit(solution)/shard_map/reduce_scatter | solution.py:210
  566.5 168.1 %reduce-scatter.11.cloned.1.call-start = ((), (), s32[]{:S(2)}) async-start(), calls=%async_computation.20 | async-start | bytes 3522560 | tf_op jit(solution)/shard_map/reduce_scatter | solution.py:210
  573.1 205.2 %reduce-scatter.23.cloned.1.call-start = ((), (), s32[]{:S(2)}) async-start(), calls=%async_computation.26 | async-start | bytes 4423680 | tf_op jit(solution)/shard_map/reduce_scatter | solution.py:210
  578.3 237.8 %reduce-scatter.15.cloned.1.call-start = ((), (), s32[]{:S(2)}) async-start(), calls=%async_computation.22 | async-start | bytes 3522560 | tf_op jit(solution)/shard_map/reduce_scatter | solution.py:210
  585.4 14.5 %collective-permute-start.94 = (bf16[256,432]{0,1:T(8,128)(2,1)S(1)}, bf16[256,432]{0,1:T(8,128)(2,1)S(1)}, u32[]{:S(2)}, u32[]{:S(2)}) collective-permute-start(bf16[256,432]{0,1:T(8,128)(2,1)S(1)} %fusion.26), channel_id=1, source_target_pairs={{48,0},{49,1},{50,2},{51,3},{52,4},{53,5},{54,6},{55,7},{56,8},{57... | collective-permute-start | bytes 663560 | tf_op jit(solution)/shard_map/ppermute | solution.py:49
  586.7 13.2 %collective-permute-start.93 = (bf16[256,432]{0,1:T(8,128)(2,1)S(1)}, bf16[256,432]{0,1:T(8,128)(2,1)S(1)}, u32[]{:S(2)}, u32[]{:S(2)}) collective-permute-start(bf16[256,432]{0,1:T(8,128)(2,1)S(1)} %fusion.26), channel_id=1, source_target_pairs={{32,0},{48,16},{33,1},{49,17},{34,2},{50,18},{35,3},{51,19},{36,4}... | collective-permute-start | bytes 663560 | tf_op jit(solution)/shard_map/ppermute | solution.py:49
  588.0 11.9 %collective-permute-start.92 = (bf16[256,432]{0,1:T(8,128)(2,1)S(1)}, bf16[256,432]{0,1:T(8,128)(2,1)S(1)}, u32[]{:S(2)}, u32[]{:S(2)}) collective-permute-start(bf16[256,432]{0,1:T(8,128)(2,1)S(1)} %fusion.26), channel_id=1, source_target_pairs={{16,0},{32,16},{48,32},{17,1},{33,17},{49,33},{18,2},{34,18},{50,3... | collective-permute-start | bytes 663560 | tf_op jit(solution)/shard_map/ppermute | solution.py:49
  591.7 18.6 %collective-permute-start.99 = (bf16[128,2048]{1,0:T(8,128)(2,1)S(1)}, bf16[128,2048]{1,0:T(8,128)(2,1)S(1)}, u32[]{:S(2)}, u32[]{:S(2)}) collective-permute-start(bf16[128,2048]{1,0:T(8,128)(2,1)S(1)} %slice.1062), channel_id=1, source_target_pairs={{0,4},{4,0},{1,5},{5,1},{2,6},{6,2},{3,7},{7,3},{8,12},{12,8},{9,1... | collective-permute-start | bytes 1572872 | tf_op jit(solution)/shard_map/ppermute | solution.py:35
  612.2 43.3 %collective-permute-start.102 = (bf16[32,2048]{1,0:T(8,128)(2,1)}, bf16[32,2048]{1,0:T(8,128)(2,1)S(1)}, u32[]{:S(2)}, u32[]{:S(2)}) collective-permute-start(bf16[32,2048]{1,0:T(8,128)(2,1)} %get-tuple-element.105), channel_id=1, source_target_pairs={{0,3},{1,0},{2,1},{3,2},{4,7},{5,4},{6,5},{7,6},{8,11},{9,8},{10,9... | collective-permute-start | bytes 393224 | tf_op jit(solution)/shard_map/ppermute | solution.py:44
  612.2 43.4 %collective-permute-start.101 = (bf16[32,2048]{1,0:T(8,128)(2,1)}, bf16[32,2048]{1,0:T(8,128)(2,1)}, u32[]{:S(2)}, u32[]{:S(2)}) collective-permute-start(bf16[32,2048]{1,0:T(8,128)(2,1)} %get-tuple-element.106), channel_id=1, source_target_pairs={{0,2},{1,3},{2,0},{3,1},{4,6},{5,7},{6,4},{7,5},{8,10},{9,11},{10,... | collective-permute-start | bytes 393224 | tf_op jit(solution)/shard_map/ppermute | solution.py:44
  623.2 32.3 %collective-permute-start.100 = (bf16[32,2048]{1,0:T(8,128)(2,1)}, bf16[32,2048]{1,0:T(8,128)(2,1)}, u32[]{:S(2)}, u32[]{:S(2)}) collective-permute-start(bf16[32,2048]{1,0:T(8,128)(2,1)} %get-tuple-element.104), channel_id=1, source_target_pairs={{0,1},{1,2},{2,3},{3,0},{4,5},{5,6},{6,7},{7,4},{8,9},{9,10},{10,1... | collective-permute-start | bytes 393224 | tf_op jit(solution)/shard_map/ppermute | solution.py:44
  643.4 33.7 %collective-permute-start.134 = (bf16[256,432]{0,1:T(8,128)(2,1)}, bf16[256,432]{0,1:T(8,128)(2,1)}, u32[]{:S(2)}, u32[]{:S(2)}) collective-permute-start(bf16[256,432]{0,1:T(8,128)(2,1)} %fusion.32), channel_id=1, source_target_pairs={{0,72},{8,64},{64,8},{72,0},{1,73},{9,65},{65,9},{73,1},{2,74},{10... | collective-permute-start | bytes 663560 | tf_op jit(solution)/shard_map/ppermute | solution.py:39
  654.7 61.3 %collective-permute-start.124 = (bf16[256,432]{0,1:T(8,128)(2,1)}, bf16[256,432]{0,1:T(8,128)(2,1)}, u32[]{:S(2)}, u32[]{:S(2)}) collective-permute-start(bf16[256,432]{0,1:T(8,128)(2,1)} %fusion.30), channel_id=1, source_target_pairs={{0,72},{8,64},{64,8},{72,0},{1,73},{9,65},{65,9},{73,1},{2,74},{10... | collective-permute-start | bytes 663560 | tf_op jit(solution)/shard_map/ppermute | solution.py:39
  677.0 11.7 %collective-permute-start.113 = (bf16[256,688]{0,1:T(8,128)(2,1)}, bf16[256,688]{0,1:T(8,128)(2,1)S(1)}, u32[]{:S(2)}, u32[]{:S(2)}) collective-permute-start(bf16[256,688]{0,1:T(8,128)(2,1)} %broadcast_select_fusion.16), channel_id=1, source_target_pairs={{0,8},{8,0},{1,9},{9,1},{2,10},{10,2},{3,11},{11,3},{4,12},{12,4},... | collective-permute-start | bytes 1056776 | tf_op jit(solution)/shard_map/ppermute | solution.py:35
  687.9 12.1 %collective-permute-start.128 = (bf16[256,864]{0,1:T(8,128)(2,1)}, bf16[256,864]{0,1:T(8,128)(2,1)S(1)}, u32[]{:S(2)}, u32[]{:S(2)}) collective-permute-start(bf16[256,864]{0,1:T(8,128)(2,1)} %broadcast_select_fusion.6), channel_id=1, source_target_pairs={{0,8},{8,0},{1,9},{9,1},{2,10},{10,2},{3,11},{11,3},{4,12},{12,4},... | collective-permute-start | bytes 1327112 | tf_op jit(solution)/shard_map/ppermute | solution.py:35
  689.6 130.9 %collective-permute-start.114 = (bf16[256,688]{0,1:T(8,128)(2,1)}, bf16[256,688]{0,1:T(8,128)(2,1)}, u32[]{:S(2)}, u32[]{:S(2)}) collective-permute-start(bf16[256,688]{0,1:T(8,128)(2,1)} %fusion.16), channel_id=1, source_target_pairs={{0,72},{8,64},{64,8},{72,0},{1,73},{9,65},{65,9},{73,1},{2,74},{10... | collective-permute-start | bytes 1056776 | tf_op jit(solution)/shard_map/ppermute | solution.py:39
  692.3 20.9 %collective-permute-start.118 = (bf16[256,688]{0,1:T(8,128)(2,1)}, bf16[256,688]{0,1:T(8,128)(2,1)S(1)}, u32[]{:S(2)}, u32[]{:S(2)}) collective-permute-start(bf16[256,688]{0,1:T(8,128)(2,1)} %broadcast_select_fusion.14), channel_id=1, source_target_pairs={{0,8},{8,0},{1,9},{9,1},{2,10},{10,2},{3,11},{11,3},{4,12},{12,4},... | collective-permute-start | bytes 1056776 | tf_op jit(solution)/shard_map/ppermute | solution.py:35
  698.1 14.1 %collective-permute-start.121 = (bf16[256,432]{0,1:T(8,128)(2,1)S(1)}, bf16[256,432]{0,1:T(8,128)(2,1)S(1)}, u32[]{:S(2)}, u32[]{:S(2)}) collective-permute-start(bf16[256,432]{0,1:T(8,128)(2,1)S(1)} %broadcast_select_fusion.28), channel_id=1, source_target_pairs={{0,8},{8,0},{1,9},{9,1},{2,10},{10,2},{3,11},{11,3},{4,12},{12,4},... | collective-permute-start | bytes 663560 | tf_op jit(solution)/shard_map/ppermute | solution.py:35
  700.9 133.6 %collective-permute-start.129 = (bf16[256,864]{0,1:T(8,128)(2,1)}, bf16[256,864]{0,1:T(8,128)(2,1)}, u32[]{:S(2)}, u32[]{:S(2)}) collective-permute-start(bf16[256,864]{0,1:T(8,128)(2,1)} %fusion.14), channel_id=1, source_target_pairs={{0,72},{8,64},{64,8},{72,0},{1,73},{9,65},{65,9},{73,1},{2,74},{10... | collective-permute-start | bytes 1327112 | tf_op jit(solution)/shard_map/ppermute | solution.py:39
  714.0 124.2 %collective-permute-start.119 = (bf16[256,688]{0,1:T(8,128)(2,1)}, bf16[256,688]{0,1:T(8,128)(2,1)}, u32[]{:S(2)}, u32[]{:S(2)}) collective-permute-start(bf16[256,688]{0,1:T(8,128)(2,1)} %fusion.18), channel_id=1, source_target_pairs={{0,72},{8,64},{64,8},{72,0},{1,73},{9,65},{65,9},{73,1},{2,74},{10... | collective-permute-start | bytes 1056776 | tf_op jit(solution)/shard_map/ppermute | solution.py:39
  736.4 45.1 %collective-permute-start.111 = (bf16[256,688]{0,1:T(8,128)(2,1)}, bf16[256,688]{0,1:T(8,128)(2,1)}, u32[]{:S(2)}, u32[]{:S(2)}) collective-permute-start(bf16[256,688]{0,1:T(8,128)(2,1)} %broadcast_select_fusion.20), channel_id=1, source_target_pairs={{0,8},{8,0},{1,9},{9,1},{2,10},{10,2},{3,11},{11,3},{4,12},{12,4},... | collective-permute-start | bytes 1056776 | tf_op jit(solution)/shard_map/ppermute | solution.py:35
  780.4 36.9 %collective-permute-start.126 = (bf16[256,864]{0,1:T(8,128)(2,1)}, bf16[256,864]{0,1:T(8,128)(2,1)}, u32[]{:S(2)}, u32[]{:S(2)}) collective-permute-start(bf16[256,864]{0,1:T(8,128)(2,1)} %broadcast_select_fusion.8), channel_id=1, source_target_pairs={{0,8},{8,0},{1,9},{9,1},{2,10},{10,2},{3,11},{11,3},{4,12},{12,4},... | collective-permute-start | bytes 1327112 | tf_op jit(solution)/shard_map/ppermute | solution.py:35
  783.6 38.9 %collective-permute-start.112 = (bf16[256,688]{0,1:T(8,128)(2,1)}, bf16[256,688]{0,1:T(8,128)(2,1)}, u32[]{:S(2)}, u32[]{:S(2)}) collective-permute-start(bf16[256,688]{0,1:T(8,128)(2,1)} %fusion.15), channel_id=1, source_target_pairs={{0,72},{8,64},{64,8},{72,0},{1,73},{9,65},{65,9},{73,1},{2,74},{10... | collective-permute-start | bytes 1056776 | tf_op jit(solution)/shard_map/ppermute | solution.py:39
  820.5 13.9 %collective-permute-start.127 = (bf16[256,864]{0,1:T(8,128)(2,1)}, bf16[256,864]{0,1:T(8,128)(2,1)}, u32[]{:S(2)}, u32[]{:S(2)}) collective-permute-start(bf16[256,864]{0,1:T(8,128)(2,1)} %fusion.13), channel_id=1, source_target_pairs={{0,72},{8,64},{64,8},{72,0},{1,73},{9,65},{65,9},{73,1},{2,74},{10... | collective-permute-start | bytes 1327112 | tf_op jit(solution)/shard_map/ppermute | solution.py:39
  827.5 13.1 %collective-permute-start.117 = (bf16[256,688]{0,1:T(8,128)(2,1)}, bf16[256,688]{0,1:T(8,128)(2,1)}, u32[]{:S(2)}, u32[]{:S(2)}) collective-permute-start(bf16[256,688]{0,1:T(8,128)(2,1)} %fusion.17), channel_id=1, source_target_pairs={{0,72},{8,64},{64,8},{72,0},{1,73},{9,65},{65,9},{73,1},{2,74},{10... | collective-permute-start | bytes 1056776 | tf_op jit(solution)/shard_map/ppermute | solution.py:39
  (223 other events, 1922.7 us)
Sparse Core Ops, SparseCore 0:
  35.0 40.2 all-gather.10
  77.0 36.9 all-gather.12
  116.2 28.2 all-gather.14
  146.1 48.9 all-gather.16
  197.1 30.7 all-gather.18
  229.4 36.9 all-gather.20
  268.1 36.9 all-gather.22
  307.3 30.4 all-gather.24
  339.4 44.8 all-gather.28
  386.4 28.3 all-gather.26
  444.2 28.3 reduce-scatter.28
  491.1 26.2 reduce-scatter.20
  520.8 25.7 reduce-scatter.26
  549.0 35.2 reduce-scatter.12
  586.6 43.8 reduce-scatter.24
  632.7 35.0 reduce-scatter.16
  670.2 26.6 reduce-scatter.18
  699.3 35.2 reduce-scatter.10
  737.1 41.1 reduce-scatter.22
  780.7 35.2 reduce-scatter.14

commit v2 on v1

--- a/solution.py
+++ b/solution.py
@@ -1,6 +1,7 @@
 import jax
 import jax.numpy as jnp
 from jax import lax
+from jax.experimental.layout import Layout, with_layout_constraint
 from jax.sharding import Mesh, PartitionSpec as P
 
 epsilon = 1e-06
@@ -19,6 +20,10 @@
     return v.astype(f32)
 
 
+def row_major(v):
+    return with_layout_constraint(v, Layout(major_to_minor=tuple(range(v.ndim))))
+
+
 def mm(a, b):
     return lax.dot_general(a, b, (((1,), (0,)), ((), ())), preferred_element_type=f32)
 
@@ -50,21 +55,33 @@
 
 
 def spread(rows):
+    with jax.named_scope("spread"):
+        return spread_rows(rows)
+
+
+def collect(partial):
+    with jax.named_scope("collect"):
+        return collect_rows(partial)
+
+
+def spread_rows(rows):
     n = lax.axis_size("tensor")
-    parts = [rows] + [turn(rows, "tensor", -k) for k in range(1, n)]
-    own = jnp.concatenate(parts)
-    return jnp.concatenate([own, swap(own, "core")])
-
-
-def collect(partial):
+    rows = row_major(rows)
+    parts = [rows] + [row_major(turn(rows, "tensor", -k)) for k in range(1, n)]
+    own = row_major(jnp.concatenate(parts))
+    return row_major(jnp.concatenate([own, row_major(swap(own, "core"))]))
+
+
+def collect_rows(partial):
     n = lax.axis_size("tensor")
     half = partial.shape[0] // 2
     share = half // n
-    own = partial[:half] + wide(swap(low(partial[half:]), "core"))
+    partial = row_major(partial)
+    own = row_major(partial[:half] + wide(swap(row_major(low(partial[half:])), "core")))
     total = own[:share]
     for k in range(1, n):
-        total = total + wide(turn(low(own[k * share : (k + 1) * share]), "tensor", k))
-    return total
+        total = total + wide(turn(row_major(low(own[k * share : (k + 1) * share])), "tensor", k))
+    return row_major(total)
 
 
 def pick(flag, a, b):
@@ -87,19 +104,30 @@
 
 
 def earlier_states(state, ctx):
+    with jax.named_scope("earlier_states"):
+        return states_before(state, ctx)
+
+
+def later_states(state, ctx):
+    with jax.named_scope("later_states"):
+        return states_after(state, ctx)
+
+
+def states_before(state, ctx):
     fade = ctx["fade"]
     sent = low(state)
-    other = wide(swap(sent, "ylo"))
+    got = swap(sent, "ylo")
+    other = wide(got)
     own = wide(sent)
     y = ctx["ylo"]
     first, second = pick(y == 0, own, other), pick(y == 0, other, own)
     pair = low(fade * first + second)
     total = wide(shift(pair, "x", 1))
     total = total + (fade**2) * wide(shift(pair, "x", 2)) + (fade**4) * wide(shift(pair, "x", 3))
-    return pick(y == 0, total, fade * total + first)
-
-
-def later_states(state, ctx):
+    return pick(y == 0, total, fade * total + first), got
+
+
+def states_after(state, ctx):
     fade = ctx["fade"]
     sent = low(state)
     other = wide(swap(sent, "ylo"))
@@ -116,13 +144,17 @@
     return v * jax.nn.sigmoid(v)
 
 
-def forward(h, a_rows, ffn_gain, weights, ctx):
-    w_kv, w_qg, w_out, w_gu, w_down = weights
+def forward(h, a_rows, ffn_gain, weights, ctx, waits=()):
+    w_kv, w_qgo, get_gud = weights
     K, V, F = ctx["sizes"]
     kv = mm(a_rows, w_kv)
     k, v = low(kv[:, :K]), low(kv[:, K : K + V])
     faded_k = low(wide(k) * ctx["to_end"])
-    state_in = low(earlier_states(mm_left(faded_k, v), ctx))
+    state_in, swapped = earlier_states(mm_left(faded_k, v), ctx)
+    state_in = low(state_in)
+    w_gud = get_gud(swapped)
+    w_gu, w_down = w_gud[:, : 2 * F], w_gud[:, 2 * F :]
+    w_qg, w_out = w_qgo[:, : K + V], w_qgo[:, K + V :]
     qg = mm(a_rows, w_qg)
     q, ret_gate = low(qg[:, :K]), qg[:, K:]
     scores = low(mm_right(q, k) * ctx["decay_mask"])
@@ -131,19 +163,23 @@
     gated = low(silu(ret_gate) * (retained * n))
     mid = h + collect(mm_right(gated, w_out))
     b_rows = spread(low(mid * rms_inverse(mid) * ffn_gain))
+    pairs, _ = swap_halves((a_rows, b_rows), (), ctx)
     gu = mm(b_rows, w_gu)
     gate_pre, up_pre = gu[:, :F], gu[:, F:]
-    hidden = low(silu(gate_pre) * up_pre)
+    hidden = hold(low(silu(gate_pre) * up_pre), *waits)
+    _, rights = swap_halves((), (gated, hidden), ctx)
     out = mid + collect(mm_right(hidden, w_down))
-    record = (a_rows, k, v, q, state_in, scores, ret_gate, retained, gated, mid, b_rows, gu, hidden)
-    return out, record
-
-
-def backward(h, g_out, d_f, record, gains, weights, ctx):
+    record = (pairs, rights, k, v, q, state_in, scores, ret_gate, retained, mid, gu)
+    return out, record, (w_kv, w_qg, w_out, w_gu, w_down)
+
+
+def backward(h, g_out, d_f_rows, record, gains, weights, ctx, merged, waits=((), (), ())):
     w_kv, w_qg, w_out, w_gu, w_down = weights
     attn_gain, ffn_gain = gains
     K, V, F = ctx["sizes"]
-    a_rows, k, v, q, state_in, scores, ret_gate, retained, gated, mid, b_rows, gu, hidden = record
+    (a_pair, b_pair), (gated_pair, hidden_pair), k, v, q, state_in, scores, ret_gate, retained, mid, gu = record
+    d_f = spread(d_f_rows)
+    (f_pair,), _ = swap_halves((d_f,), (), ctx)
     d_hidden = mm(d_f, w_down)
     gate_pre, up_pre = gu[:, :F], gu[:, F:]
     s = jax.nn.sigmoid(gate_pre)
@@ -151,11 +187,14 @@
     d_up = low(d_hidden * gate_pre * s)
     d_gu = jnp.concatenate([d_gate, d_up], axis=1)
     d_b = collect(mm_right(d_gu, w_gu))
-    grad_down = low(mm_left(d_f, hidden))
-    grad_gu = low(mm_left(b_rows, d_gu))
+    _, (gu_pair,) = swap_halves((), (d_gu,), ctx)
+    part_down = settle(weight_grad(f_pair, hidden_pair))
+    part_gu = settle(weight_grad(b_pair, gu_pair))
+    d_b = hold(d_b, *waits[0])
     d_norm, grad_ffn_gain = norm_back(mid, ffn_gain, d_b)
     d_mid = g_out + d_norm
     d_r = spread(low(d_mid))
+    (r_pair,), _ = swap_halves((d_r,), (), ctx)
     d_gated = mm(d_r, w_out)
     s = jax.nn.sigmoid(ret_gate)
     n = lax.rsqrt(jnp.mean(retained * retained, axis=-1, keepdims=True) + group_floor)
@@ -167,19 +206,57 @@
     d_ret_low = low(d_ret)
     d_ret_start = low(d_ret * ctx["from_start"])
     beyond = low(later_states(mm_left(q, d_ret_start), ctx))
-    grad_out = low(mm_left(d_r, gated))
+    part_out = settle(weight_grad(r_pair, gated_pair))
     d_scores = low(mm_right(d_ret_low, v) * ctx["decay_mask"])
     d_q = low(mm(d_scores, k) + mm_right(d_ret_start, state_in))
     d_qg = jnp.concatenate([d_q, d_ret_gate], axis=1)
-    grad_qg = low(mm_left(a_rows, d_qg))
+    _, (qg_pair,) = swap_halves((), (d_qg,), ctx)
+    beyond = hold(beyond, *waits[1])
+    if not merged:
+        part_qg = settle(weight_grad(a_pair, qg_pair))
     d_k = low(mm_left(d_scores, q) + mm_right(v, beyond) * ctx["to_end"])
     d_v = low(mm_left(scores, d_ret_low) + mm(k, beyond) * ctx["to_end"])
     d_kv = jnp.concatenate([d_k, d_v], axis=1)
-    grad_kv = low(mm_left(a_rows, d_kv))
     d_kv_wide = jnp.pad(d_kv, ((0, 0), (0, w_kv.shape[1] - d_kv.shape[1])))
-    d_a = collect(mm_right(d_qg, w_qg) + mm_right(d_kv_wide, w_kv))
+    partial = mm_right(d_qg, w_qg) + mm_right(d_kv_wide, w_kv)
+    d_a = collect(partial)
+    _, (kv_pair,) = swap_halves((), (d_kv,), ctx)
+    if merged:
+        pair = tuple(jnp.concatenate(p, axis=1) for p in zip(kv_pair, qg_pair))
+        part_in = settle(weight_grad(a_pair, pair))
+        part_kv, part_qg = part_in[:, : K + V], part_in[:, K + V :]
+    else:
+        part_kv = settle(weight_grad(a_pair, kv_pair))
+        d_a = hold(d_a, part_down, part_gu)
     d_norm, grad_attn_gain = norm_back(h, attn_gain, d_a)
-    return d_mid + d_norm, (grad_kv, grad_qg, grad_out, grad_gu, grad_down), (grad_attn_gain, grad_ffn_gain)
+    parts = (part_kv, part_qg, part_out, part_gu, part_down)
+    return d_mid + d_norm, parts, (grad_attn_gain, grad_ffn_gain)
+
+
+def swap_halves(lefts, rights, ctx):
+    n = lax.axis_size("x")
+
+    def half(v, which):
+        width = v.shape[1] // (2 * n)
+        cut = [v[:, i * width : (i + 1) * width] for i in range(2 * n)]
+        return jnp.concatenate([pick(which == 0, cut[2 * i], cut[2 * i + 1]) for i in range(n)], axis=1)
+
+    place = ctx["place"]
+    keeps = [half(v, place) for v in lefts]
+    sent = jnp.concatenate([half(v, 1 - place) for v in lefts] + list(rights), axis=1)
+    got = swap(sent, "ylo")
+    at, left_pairs, right_pairs = 0, [], []
+    for keep in keeps:
+        left_pairs.append((keep, got[:, at : at + keep.shape[1]]))
+        at += keep.shape[1]
+    for right in rights:
+        right_pairs.append((right, got[:, at : at + right.shape[1]]))
+        at += right.shape[1]
+    return left_pairs, right_pairs
+
+
+def weight_grad(left, right):
+    return row_major(low(mm_left(left[0], right[0]) + mm_left(left[1], right[1])))
 
 
 def halves(w, core):
@@ -188,37 +265,57 @@
     return pick(core == 0, first, second), pick(core == 0, second, first)
 
 
-def bring(shards, ctx):
-    core, section, ylo = ctx["core"], ctx["section"], ctx["ylo"]
-    split = [halves(w, core) for w in shards]
+def corner(v):
+    return v[tuple(slice(n - 1, n) for n in v.shape)].reshape(1, 1)
+
+
+def hold(v, *others):
+    if not others:
+        return v
+    corners = [corner(other) for other in others]
+    bad = corners[0] != corners[0]
+    for c in corners[1:]:
+        bad = bad | (c != c)
+    return jnp.where(bad, jnp.zeros((), v.dtype), v)
+
+
+def gather_x(rows):
+    return lax.all_gather(rows, "x", axis=0, tiled=True)
+
+
+def pack(shards, ctx):
+    split = [halves(w, ctx["core"]) for w in shards]
     keep = jnp.concatenate([a for a, _ in split], axis=1)
     give = jnp.concatenate([b for _, b in split], axis=1)
-    own = side(core, keep, swap(give, "core"))
-    own_other = swap(own, "ylo")
-    far_other = cross(own)
-    far = swap(far_other, "ylo")
-    mine = side(ylo, own, own_other)
-    theirs = side(ylo, far, far_other)
-    return pick(section == 0, mine, theirs), pick(section == 0, theirs, mine)
-
-
-def gather_x(rows):
-    return lax.all_gather(rows, "x", axis=0, tiled=True)
-
-
-def settle(grad, layer, ctx):
-    part = lax.psum_scatter(grad, "x", scatter_dimension=0, tiled=True)
-    half = part.shape[0] // 2
-    away = ctx["section"] != layer
-    place = jnp.where(away, 1 - ctx["ylo"], ctx["ylo"])
-    keep = pick(place == 0, part[:half], part[half:])
-    give = pick(place == 0, part[half:], part[:half])
-    total = wide(keep) + wide(swap(give, "ylo"))
-    return total + wide(cross(low(total)))
-
-
-def share_out(total, ctx):
-    core = ctx["core"]
+    return side(ctx["core"], keep, swap(give, "core"))
+
+
+def along_y(own):
+    return swap(own, "ylo"), cross(own), swap(own, "section")
+
+
+def both_layers(own, moved, ctx):
+    near, crossed, facing = moved
+    section, at_0 = ctx["section"], ctx["ylo"] == 0
+    mine = (pick(at_0, own, near), pick(at_0, near, own))
+    theirs = (pick(at_0, facing, crossed), pick(at_0, crossed, facing))
+    first = [pick(section == 0, a, b) for a, b in zip(mine, theirs)]
+    second = [pick(section == 0, b, a) for a, b in zip(mine, theirs)]
+    return first, second
+
+
+def y_then_x(own, moved, ctx, ready=()):
+    first, second = both_layers(own, moved, ctx)
+    return hold(jnp.concatenate(first), *ready), jnp.concatenate(second)
+
+
+def settle(grad):
+    return lax.psum_scatter(grad, "x", scatter_dimension=0, tiled=True)
+
+
+def share_out(first, second, ctx):
+    section, core = ctx["section"], ctx["core"]
+    total = wide(pick(section == 0, first, second)) + wide(cross(pick(section == 0, second, first)))
     half = total.shape[0] // 2
     keep = pick(core == 0, total[:half], total[half:])
     give = pick(core == 0, total[half:], total[:half])
@@ -286,6 +383,7 @@
             "to_end": to_end[:, None],
             "from_start": from_start[:, None],
             "fade": jnp.exp(-rate * rows),
+            "place": jnp.where(section == layer, ylo, 1 - ylo),
             "ylo": ylo,
             "core": core,
             "section": section,
@@ -297,41 +395,61 @@
 
     gain_columns = jnp.stack([attn_gain[0], ffn_gain[0]], axis=1)
     gain_columns = jnp.concatenate([gain_columns, gain_columns], axis=1)
-    kv0, kv1 = bring((w_key[0], w_value[0], gain_columns), ctx)
-    qg0, qg1 = bring((w_query[0], w_gate_ret[0]), ctx)
-    out0, out1 = bring((w_out[0].T,), ctx)
-    gu0, gu1 = bring((w_gate[0], w_up[0]), ctx)
-    down0, down1 = bring((w_down[0].T,), ctx)
-    weights0 = tuple(gather_x(w) for w in (kv0, qg0, out0, gu0, down0))
-    weights1 = tuple(gather_x(w) for w in (kv1, qg1, out1, gu1, down1))
-
-    def gains_of(weights):
-        columns = wide(weights[0][:, K + V : K + V + 2]).T
+    h0_rows = wide(spread(h0))
+    with jax.named_scope("weights_key_value"):
+        own_kv = pack((w_key[0], w_value[0], gain_columns), ctx)
+        ready = (h0_rows, ctxs[0]["decay_mask"], ctxs[1]["decay_mask"])
+        kv0, kv1 = y_then_x(own_kv, along_y(own_kv), ctx, ready)
+    with jax.named_scope("weights_query_gate_out"):
+        own_qgo = hold(pack((w_query[0], w_gate_ret[0], w_out[0].T), ctx), kv0)
+        qgo0, qgo1 = y_then_x(own_qgo, along_y(own_qgo), ctx)
+    with jax.named_scope("gather_weights"):
+        kv0, kv1 = gather_x(kv0), gather_x(kv1)
+        qgo0, qgo1 = gather_x(qgo0), gather_x(qgo1)
+    second = []
+
+    def get_gud(swapped):
+        with jax.named_scope("weights_gate_up_down"):
+            own_gud = hold(pack((w_gate[0], w_up[0], w_down[0].T), ctx), swapped)
+            gud0, gud1 = y_then_x(own_gud, along_y(own_gud), ctx)
+            second.append(gather_x(gud1))
+            return gather_x(gud0)
+
+    def gain_rows(columns):
+        columns = wide(columns).T
         return columns[0], columns[1]
 
-    gains0, gains1 = gains_of(weights0), gains_of(weights1)
-
-    h0_rows = wide(spread(h0))
+    gains0 = gain_rows(kv0[:, K + V : K + V + 2])
+    gains1 = gain_rows(kv1[:, K + V : K + V + 2])
+    weights0 = (kv0, qgo0, get_gud)
+    weights1 = (kv1, qgo1, lambda swapped: second[0])
+
     a0 = low(h0_rows * rms_inverse(h0_rows) * gains0[0])
     h0 = wide(h0)
-    out_first, record0 = forward(h0, a0, gains0[1], weights0, ctxs[0])
+    with jax.named_scope("layer0_forward"):
+        out_first, record0, weights0 = forward(h0, a0, gains0[1], weights0, ctxs[0])
     h1 = wide(low(out_first))
     a1 = spread(low(h1 * rms_inverse(h1) * gains1[0]))
-    out_second, record1 = forward(h1, a1, gains1[1], weights1, ctxs[1])
-
-    d_f1 = spread(g1)
-    d_h1, grads1, gain_grads1 = backward(
-        h1, wide(g1), d_f1, record1, gains1, weights1, ctxs[1]
-    )
-    settled1 = [settle(g, 1, ctx) for g in grads1]
-    d_f0_rows = low(d_h1)
-    d_h0, grads0, gain_grads0 = backward(
-        h0, wide(d_f0_rows), spread(d_f0_rows), record0, gains0, weights0, ctxs[0]
-    )
-    settled0 = [settle(g, 0, ctx) for g in grads0]
-
-    shared = [share_out(pick(section == 0, a, b), ctx) for a, b in zip(settled0, settled1)]
-    kv, qg, out, gu, down = shared
+    early = [pair[1] for pair in record0[0] + record0[1]]
+    with jax.named_scope("layer1_forward"):
+        out_second, record1, weights1 = forward(h1, a1, gains1[1], weights1, ctxs[1], early)
+
+    with jax.named_scope("layer1_backward"):
+        d_h1, parts1, gain_grads1 = backward(
+            h1, wide(g1), g1, record1, gains1, weights1, ctxs[1], True
+        )
+    d_f0 = low(d_h1)
+    kv1, qg1, out1, gu1, down1 = parts1
+    with jax.named_scope("layer0_backward"):
+        d_h0, parts0, gain_grads0 = backward(
+            h0, wide(d_f0), d_f0, record0, gains0, weights0, ctxs[0], False, ((gu1, down1), (out1, kv1))
+        )
+    kv0, qg0, out0, gu0, down0 = parts0
+    with jax.named_scope("owners"):
+        kv, qg, out, gu, down = (
+            share_out(a, b, ctx)
+            for a, b in ((kv0, kv1), (qg0, qg1), (out0, out1), (gu0, gu1), (down0, down1))
+        )
     grad_key = both(kv, 0, K, ctx)
     grad_value = both(kv, K, K + V, ctx)
     grad_query = both(qg, 0, K, ctx)
@@ -342,16 +460,14 @@
     grad_down = both(down, 0, F, ctx).T
 
     gain_grads = jnp.stack(gain_grads0 + gain_grads1)
-    for axis, order in (
-        ("tensor", ((0, 1), (1, 0), (2, 3), (3, 2))),
-        ("tensor", ((0, 3), (3, 0), (1, 2), (2, 1))),
-        ("core", ((0, 1), (1, 0))),
-        ("x", ((0, 1), (1, 0), (2, 3), (3, 2))),
-        ("x", ((0, 3), (3, 0), (1, 2), (2, 1))),
-        ("ylo", ((0, 1), (1, 0))),
-        ("section", ((0, 1), (1, 0))),
-    ):
-        gain_grads = gain_grads + lax.ppermute(gain_grads, axis, order)
+    with jax.named_scope("gains"):
+        for moves in (
+            [lambda v, k=k: turn(v, "tensor", k) for k in (1, 2, 3)],
+            [lambda v: swap(v, "core")],
+            [lambda v, k=k: turn(v, "x", k) for k in (1, 2, 3)],
+            [lambda v: swap(v, "ylo"), cross, lambda v: swap(v, "section")],
+        ):
+            gain_grads = gain_grads + sum(move(gain_grads) for move in moves)
     own_gains = pick(section == 0, gain_grads[:2], gain_grads[2:])
     width = attn_gain.shape[1]
     own_gains = lax.dynamic_slice_in_dim(own_gains, (block * 2 + core) * width, width, 1)

time: 864 us -> 804 us (0.931)
  waiting for transfers between devices: 458 us -> 308 us
  between operations: 21.5 us -> 41.3 us
  matrix products: 77.8 us -> 96.1 us
  starting transfers between devices: 167 us -> 185 us
  other arithmetic: 85.1 us -> 103 us
  local copies, waits for them, and re-layouts: 44.8 us -> 59.8 us
    reduce_scatter x10 -> x9, waiting for transfers between devices: 84 us -> 5.74 us  [settle(): return lax.psum_scatter(grad, 'x', scatter_dimension=0, tiled=True)]
    all_gather x10 -> x6, waiting for transfers between devices: 84.1 us -> 33.8 us  [gather_x(): return lax.all_gather(rows, 'x', axis=0, tiled=True)]
    ppermute x48 -> x54, waiting for transfers between devices: 103 us -> 60.4 us  [turn(): return lax.ppermute(v, axis, [(i, (i + by) % n) for i in range(n)])]
    ppermute x15 -> x9, waiting for transfers between devices: 44.6 us -> 80.8 us  [cross(): return lax.ppermute(v, ('section', 'ylo'), [(0, 3), (1, 2), (2, 1), (3, 0)])]
    ppermute x48 -> x54, starting transfers between devices: 42.4 us -> 68.7 us  [turn(): return lax.ppermute(v, axis, [(i, (i + by) % n) for i in range(n)])]
    concatenate x11 -> x33, other arithmetic: 4.86 us -> 21.9 us  [the longest x7 7.22 us: spread_rows(): return row_major(jnp.concatenate([own, row_major(swap(own, 'core'))]))]
    slice x18 -> x33, local copies, waits for them, and re-layouts: 5.74 us -> 20 us  [the longest x13 13 us: corner(): return v[tuple((slice(n - 1, n) for n in v.shape))].reshape(1, 1)]
    select_n x38 -> x32, other arithmetic: 32 us -> 18.7 us  [pick(): return jnp.where(flag, a, b)]
  transfers between devices with their start and end apart: 156 -> 145, of which waited for: 99 -> 68; matrix products, arithmetic and copies ran while one was open for 20% -> 30% of each run, Pallas kernels for 0% -> 0%
where the time goes in v2:
time: 804 us; the launch traced here: 793 us
  waiting for transfers between devices  308 us (38%)
  starting transfers between devices  185 us (23%)
  other arithmetic  103 us (13%)
  matrix products  96.1 us (12%)
  local copies, waits for them, and re-layouts  59.8 us (7%)
  between operations  41.3 us (5%)
    ppermute x55, waiting for transfers between devices, swap(): return lax.ppermute(v, axis, [(0, 1), (1, 0)])  90 us
    ppermute x9, waiting for transfers between devices, cross(): return lax.ppermute(v, ('section', 'ylo'), [(0, 3), (1, 2), (2, 1), (3, 0)])  80.8 us
    ppermute x55, starting transfers between devices, swap(): return lax.ppermute(v, axis, [(0, 1), (1, 0)])  69.3 us
    ppermute x54, starting transfers between devices, turn(): return lax.ppermute(v, axis, [(i, (i + by) % n) for i in range(n)])  68.7 us
    ppermute x54, waiting for transfers between devices, turn(): return lax.ppermute(v, axis, [(i, (i + by) % n) for i in range(n)])  60.4 us
    dot_general x26, matrix products, mm_left(): lax.dot_general(a, b, (((0,), (0,)), ((), ())), preferred_element_type=f32)  38.3 us
    ppermute x12, waiting for transfers between devices, shift(): lax.ppermute(v, axis, [(i, i + by) for i in range(n) if 0 <= i + by < n])  37.3 us
    all_gather x6, waiting for transfers between devices, gather_x(): return lax.all_gather(rows, 'x', axis=0, tiled=True)  33.8 us
  transfers between devices with their start and end apart: 145, of which 68 were waited for; matrix products, arithmetic and copies ran while one was open for 30% of the time, Pallas kernels for 0%

profile of v2, /device:TPU:1, one launch (start us, length us, event | category | flops | bytes accessed | tf_op | source)
XLA Modules:
  0.0 793.4 jit_solution(1023033528845167855)
XLA Ops:
  10.2 3.0 collective-permute-start.6
  23.7 3.3 collective-permute-start.2
  27.9 2.8 collective-permute-start.10
  38.3 9.2 %collective-permute-done.10 = bf16[256,690]{1,0:T(8,128)(2,1)S(1)} collective-permute-done((bf16[256,690]{1,0:T(8,128)(2,1)S(1)}, bf16[256,690]{1,0:T(8,128)(2,1)S(1)}, u32[]{:S(2)}, u32[]{:S(2)}) %collective-permute-start.10) | collective-permute-done | bytes 353312 | tf_op jit(solution)/shard_map/weights_key_value/ppermute | solution.py:44
  58.2 2.7 collective-permute-start.14
  61.6 24.9 %collective-permute-done.14 = bf16[256,1120]{0,1:T(8,128)(2,1)S(1)} collective-permute-done((bf16[256,1120]{0,1:T(8,128)(2,1)S(1)}, bf16[256,1120]{0,1:T(8,128)(2,1)S(1)}, u32[]{:S(2)}, u32[]{:S(2)}) %collective-permute-start.14) | collective-permute-done | bytes 573472 | tf_op jit(solution)/shard_map/weights_query_gate_out/ppermute | solution.py:44
  106.9 7.8 collective-permute-done.15
  122.4 28.3 %collective-permute-done.30 = bf16[256,1296]{0,1:T(8,128)(2,1)} collective-permute-done((bf16[256,1296]{0,1:T(8,128)(2,1)}, bf16[256,1296]{0,1:T(8,128)(2,1)}, u32[]{:S(2)}, u32[]{:S(2)}) %collective-permute-start.30) | collective-permute-done | bytes 663584 | tf_op jit(solution)/shard_map/layer0_forward/weights_gate_up_down/ppermute | solution.py:44
  156.6 2.9 broadcast_select_fusion.5
  170.5 2.9 collective-permute-start.50
  175.1 5.1 collective-permute-start.18
  186.3 10.3 %collective-permute-done.18 = bf16[256,432]{1,0:T(8,128)(2,1)} collective-permute-done((bf16[256,432]{1,0:T(8,128)(2,1)}, bf16[256,432]{1,0:T(8,128)(2,1)}, u32[]{:S(2)}, u32[]{:S(2)}) %collective-permute-start.18) | collective-permute-done | bytes 221216 | tf_op jit(solution)/shard_map/layer0_forward/earlier_states/ppermute | solution.py:54
  198.0 3.3 fusion.14
  206.1 2.6 fusion.36
  222.5 3.9 collective-permute-done.21
  231.1 3.1 collective-permute-done.25
  240.3 21.6 %all-gather.11.cloned.1.call-done = bf16[2048,1296]{1,0:T(8,128)(2,1)} async-done(((bf16[512,1296]{1,0:T(8,128)(2,1)}), bf16[2048,1296]{1,0:T(8,128)(2,1)}) %all-gather.11.cloned.1.call-update) | async-done | bytes 5308432 | tf_op jit(solution)/shard_map/layer0_forward/weights_gate_up_down/all_gather | solution.py:283
  261.9 3.5 fusion.6
  266.6 2.8 fusion.32
  281.4 3.9 collective-permute-done.33
  290.1 3.1 collective-permute-done.37
  304.4 12.2 %all-gather.15.cloned.1.call-done = bf16[2048,1120]{1,0:T(8,128)(2,1)} async-done(((bf16[512,1120]{1,0:T(8,128)(2,1)}), bf16[2048,1120]{1,0:T(8,128)(2,1)}) %all-gather.15.cloned.1.call-update) | async-done | bytes 4587536 | tf_op jit(solution)/shard_map/gather_weights/all_gather | solution.py:283
  316.6 3.5 fusion.10
  321.6 17.6 %collective-permute-done.39 = bf16[256,432]{1,0:T(8,128)(2,1)S(1)} collective-permute-done((bf16[256,432]{1,0:T(8,128)(2,1)S(1)}, bf16[256,432]{1,0:T(8,128)(2,1)S(1)}, u32[]{:S(2)}, u32[]{:S(2)}) %collective-permute-start.39) | collective-permute-done | bytes 221216 | tf_op jit(solution)/shard_map/layer1_forward/earlier_states/ppermute | solution.py:40
  339.3 2.9 collective-permute-start.42
  347.2 11.9 %collective-permute-done.42 = bf16[256,432]{1,0:T(8,128)(2,1)S(1)} collective-permute-done((bf16[256,432]{1,0:T(8,128)(2,1)S(1)}, bf16[256,432]{1,0:T(8,128)(2,1)S(1)}, u32[]{:S(2)}, u32[]{:S(2)}) %collective-permute-start.42) | collective-permute-done | bytes 221216 | tf_op jit(solution)/shard_map/layer1_forward/earlier_states/ppermute | solution.py:54
  359.1 7.2 collective-permute-done.40
  369.2 2.6 fusion.28
  390.9 3.7 collective-permute-done.45
  409.3 3.7 fusion.2
  427.6 3.7 fusion.68
  444.9 2.9 collective-permute-start.62
  452.3 2.8 multiply_reduce_fusion.2
  458.9 18.1 %collective-permute-done.63 = bf16[256,432]{1,0:T(8,128)(2,1)S(1)} collective-permute-done((bf16[256,432]{1,0:T(8,128)(2,1)S(1)}, bf16[256,432]{1,0:T(8,128)(2,1)S(1)}, u32[]{:S(2)}, u32[]{:S(2)}) %collective-permute-start.63) | collective-permute-done | bytes 221216 | tf_op jit(solution)/shard_map/layer1_backward/later_states/ppermute | solution.py:40
  481.3 7.9 collective-permute-done.66
  494.5 5.4 collective-permute-start.67
  500.0 3.2 add_convert_fusion.2
  505.9 2.7 collective-permute-start.70
  516.5 3.0 collective-permute-start.78
  521.0 3.3 collective-permute-done.78
  532.6 11.4 %collective-permute-done.85 = bf16[256,1024]{1,0:T(8,128)(2,1)S(1)} collective-permute-done((bf16[256,1024]{1,0:T(8,128)(2,1)S(1)}, bf16[256,1024]{1,0:T(8,128)(2,1)S(1)}, u32[]{:S(2)}, u32[]{:S(2)}) %collective-permute-start.85) | collective-permute-done | bytes 524320 | tf_op jit(solution)/shard_map/layer0_backward/ppermute | solution.py:40
  546.7 3.0 multiply_convert_fusion.4
  551.4 3.3 fusion.4
  557.1 3.8 collective-permute-done.86
  561.0 3.1 add_convert_fusion.1
  581.5 2.9 collective-permute-done.89
  585.4 3.7 collective-permute-start.90
  593.5 11.6 %collective-permute-done.123 = bf16[256,1024]{1,0:T(8,128)(2,1)S(1)} collective-permute-done((bf16[256,1024]{1,0:T(8,128)(2,1)S(1)}, bf16[256,1024]{1,0:T(8,128)(2,1)S(1)}, u32[]{:S(2)}, u32[]{:S(2)}) %collective-permute-start.123) | collective-permute-done | bytes 524320 | tf_op jit(solution)/shard_map/layer0_backward/ppermute | solution.py:40
  607.6 2.7 fusion.22
  618.8 5.3 collective-permute-done.93
  624.1 8.4 %collective-permute-done.92 = bf16[256,688]{1,0:T(8,128)(2,1)S(1)} collective-permute-done((bf16[256,688]{1,0:T(8,128)(2,1)}, bf16[256,688]{1,0:T(8,128)(2,1)S(1)}, u32[]{:S(2)}, u32[]{:S(2)}) %collective-permute-start.92) | collective-permute-done | bytes 352288 | tf_op jit(solution)/shard_map/layer1_backward/ppermute | solution.py:40
  632.5 3.7 add_convert_fusion
  644.5 3.0 multiply_reduce_fusion.1
  674.7 3.0 add_convert_fusion.4
  689.3 3.1 collective-permute-start.124
  701.9 3.1 fusion.16
  719.0 2.6 fusion.151
  727.0 2.9 add_convert_fusion.3
  733.0 2.9 collective-permute-start.110
  736.8 4.3 collective-permute-start.113
  753.0 5.7 reduce-scatter.24.cloned.1.call-done
  758.9 3.0 collective-permute-start.121
  763.4 6.3 collective-permute-done.121
  769.7 8.4 %collective-permute-done.118 = bf16[256,688]{1,0:T(8,128)(2,1)S(1)} collective-permute-done((bf16[256,688]{1,0:T(8,128)(2,1)S(1)}, bf16[256,688]{1,0:T(8,128)(2,1)S(1)}, u32[]{:S(2)}, u32[]{:S(2)}) %collective-permute-start.118) | collective-permute-done | bytes 352288 | tf_op jit(solution)/shard_map/owners/ppermute | solution.py:44
  (970 shorter events, 371.8 us)
Async XLA Ops:
  7.2 94.2 %all-gather.7.cloned.1.call-start = ((), (), s32[]{:S(2)}) async-start(), calls=%async_computation.9 | async-start | bytes 3932160 | tf_op jit(solution)/shard_map/gather_weights/all_gather | solution.py:283
  8.8 18.9 %collective-permute-start.5 = (s32[128]{0:T(128)S(1)}, s32[128]{0:T(128)S(1)}, u32[]{:S(2)}, u32[]{:S(2)}) collective-permute-start(s32[128]{0:T(128)S(1)} %get-tuple-element.107), channel_id=1, source_target_pairs={{0,4},{4,0},{1,5},{5,1},{2,6},{6,2},{3,7},{7,3},{8,12},{12,8},{9,1... | collective-permute-start | bytes 1544 | tf_op jit(solution)/shard_map/ppermute | solution.py:40
  27.9 19.6 %collective-permute-start.10 = (bf16[256,690]{1,0:T(8,128)(2,1)S(1)}, bf16[256,690]{1,0:T(8,128)(2,1)S(1)}, u32[]{:S(2)}, u32[]{:S(2)}) collective-permute-start(bf16[256,690]{1,0:T(8,128)(2,1)S(1)} %maximum_select_fusion.10), channel_id=1, source_target_pairs={{0,72},{8,64},{64,8},{72,0},{1,73},{9,65},{65,9},{73,1},{2,74},{10... | collective-permute-start | bytes 1059848 | tf_op jit(solution)/shard_map/weights_key_value/ppermute | solution.py:44
  30.7 16.8 %collective-permute-start.9 = (bf16[256,690]{1,0:T(8,128)(2,1)S(1)}, bf16[256,690]{1,0:T(8,128)(2,1)S(1)}, u32[]{:S(2)}, u32[]{:S(2)}) collective-permute-start(bf16[256,690]{1,0:T(8,128)(2,1)S(1)} %maximum_select_fusion.10), channel_id=1, source_target_pairs={{0,64},{64,0},{1,65},{65,1},{2,66},{66,2},{3,67},{67,3},{4,68},{68... | collective-permute-start | bytes 1059848 | tf_op jit(solution)/shard_map/weights_key_value/ppermute | solution.py:40
  31.0 16.7 %collective-permute-start.8 = (bf16[256,690]{1,0:T(8,128)(2,1)S(1)}, bf16[256,690]{1,0:T(8,128)(2,1)S(1)}, u32[]{:S(2)}, u32[]{:S(2)}) collective-permute-start(bf16[256,690]{1,0:T(8,128)(2,1)S(1)} %maximum_select_fusion.10), channel_id=1, source_target_pairs={{0,8},{8,0},{1,9},{9,1},{2,10},{10,2},{3,11},{11,3},{4,12},{12,4},... | collective-permute-start | bytes 1059848 | tf_op jit(solution)/shard_map/weights_key_value/ppermute | solution.py:40
  33.1 15.6 %collective-permute-start.4 = (bf16[128,2048]{1,0:T(8,128)(2,1)S(1)}, bf16[128,2048]{1,0:T(8,128)(2,1)S(1)}, u32[]{:S(2)}, u32[]{:S(2)}) collective-permute-start(bf16[128,2048]{1,0:T(8,128)(2,1)S(1)} %pad_maximum_fusion.12), channel_id=1, source_target_pairs={{0,4},{4,0},{1,5},{5,1},{2,6},{6,2},{3,7},{7,3},{8,12},{12,8},{9,1... | collective-permute-start | bytes 1572872 | tf_op jit(solution)/shard_map/spread/ppermute | solution.py:40
  52.0 146.0 %all-gather.9.cloned.1.call-start = ((), (), s32[]{:S(2)}) async-start(), calls=%async_computation.10 | async-start | bytes 5898240 | tf_op jit(solution)/shard_map/gather_weights/all_gather | solution.py:283
  58.2 28.3 %collective-permute-start.14 = (bf16[256,1120]{0,1:T(8,128)(2,1)S(1)}, bf16[256,1120]{0,1:T(8,128)(2,1)S(1)}, u32[]{:S(2)}, u32[]{:S(2)}) collective-permute-start(bf16[256,1120]{0,1:T(8,128)(2,1)S(1)} %copy.190), channel_id=1, source_target_pairs={{0,72},{8,64},{64,8},{72,0},{1,73},{9,65},{65,9},{73,1},{2,74},{10... | collective-permute-start | bytes 1720328 | tf_op jit(solution)/shard_map/weights_query_gate_out/ppermute | solution.py:44
  60.9 25.9 %collective-permute-start.13 = (bf16[256,1120]{0,1:T(8,128)(2,1)S(1)}, bf16[256,1120]{0,1:T(8,128)(2,1)}, u32[]{:S(2)}, u32[]{:S(2)}) collective-permute-start(bf16[256,1120]{0,1:T(8,128)(2,1)S(1)} %copy.190), channel_id=1, source_target_pairs={{0,64},{64,0},{1,65},{65,1},{2,66},{66,2},{3,67},{67,3},{4,68},{68... | collective-permute-start | bytes 1720328 | tf_op jit(solution)/shard_map/weights_query_gate_out/ppermute | solution.py:40
  61.2 26.9 %collective-permute-start.12 = (bf16[256,1120]{0,1:T(8,128)(2,1)S(1)}, bf16[256,1120]{0,1:T(8,128)(2,1)}, u32[]{:S(2)}, u32[]{:S(2)}) collective-permute-start(bf16[256,1120]{0,1:T(8,128)(2,1)S(1)} %copy.190), channel_id=1, source_target_pairs={{0,8},{8,0},{1,9},{9,1},{2,10},{10,2},{3,11},{11,3},{4,12},{12,4},... | collective-permute-start | bytes 1720328 | tf_op jit(solution)/shard_map/weights_query_gate_out/ppermute | solution.py:40
  92.0 121.0 %all-gather.13.cloned.1.call-start = ((), (), s32[]{:S(2)}) async-start(), calls=%async_computation.12 | async-start | bytes 3932160 | tf_op jit(solution)/shard_map/gather_weights/all_gather | solution.py:283
  95.2 21.5 %collective-permute-start.27 = (bf16[128,1296]{1,0:T(8,128)(2,1)}, bf16[128,1296]{1,0:T(8,128)(2,1)}, u32[]{:S(2)}, u32[]{:S(2)}) collective-permute-start(bf16[128,1296]{1,0:T(8,128)(2,1)} %concatenate.402), channel_id=1, source_target_pairs={{0,4},{4,0},{1,5},{5,1},{2,6},{6,2},{3,7},{7,3},{8,12},{12,8},{9,1... | collective-permute-start | bytes 995336 | tf_op jit(solution)/shard_map/layer0_forward/weights_gate_up_down/ppermute | solution.py:40
  100.2 161.7 %all-gather.11.cloned.1.call-start = ((), (), s32[]{:S(2)}) async-start(), calls=%async_computation.11 | async-start | bytes 7208960 | tf_op jit(solution)/shard_map/layer0_forward/weights_gate_up_down/all_gather | solution.py:283
  119.1 31.6 %collective-permute-start.30 = (bf16[256,1296]{0,1:T(8,128)(2,1)}, bf16[256,1296]{0,1:T(8,128)(2,1)}, u32[]{:S(2)}, u32[]{:S(2)}) collective-permute-start(bf16[256,1296]{0,1:T(8,128)(2,1)} %copy.206), channel_id=1, source_target_pairs={{0,72},{8,64},{64,8},{72,0},{1,73},{9,65},{65,9},{73,1},{2,74},{10... | collective-permute-start | bytes 1990664 | tf_op jit(solution)/shard_map/layer0_forward/weights_gate_up_down/ppermute | solution.py:44
  121.7 30.4 %collective-permute-start.29 = (bf16[256,1296]{0,1:T(8,128)(2,1)}, bf16[256,1296]{0,1:T(8,128)(2,1)}, u32[]{:S(2)}, u32[]{:S(2)}) collective-permute-start(bf16[256,1296]{0,1:T(8,128)(2,1)} %copy.206), channel_id=1, source_target_pairs={{0,64},{64,0},{1,65},{65,1},{2,66},{66,2},{3,67},{67,3},{4,68},{68... | collective-permute-start | bytes 1990664 | tf_op jit(solution)/shard_map/layer0_forward/weights_gate_up_down/ppermute | solution.py:40
  121.7 32.6 %collective-permute-start.28 = (bf16[256,1296]{0,1:T(8,128)(2,1)}, bf16[256,1296]{0,1:T(8,128)(2,1)}, u32[]{:S(2)}, u32[]{:S(2)}) collective-permute-start(bf16[256,1296]{0,1:T(8,128)(2,1)} %copy.206), channel_id=1, source_target_pairs={{0,8},{8,0},{1,9},{9,1},{2,10},{10,2},{3,11},{11,3},{4,12},{12,4},... | collective-permute-start | bytes 1990664 | tf_op jit(solution)/shard_map/layer0_forward/weights_gate_up_down/ppermute | solution.py:40
  160.8 155.8 %all-gather.15.cloned.1.call-start = ((), (), s32[]{:S(2)}) async-start(), calls=%async_computation.13 | async-start | bytes 5898240 | tf_op jit(solution)/shard_map/gather_weights/all_gather | solution.py:283
  170.5 40.3 %collective-permute-start.50 = (bf16[128,2048]{1,0:T(8,128)(2,1)}, bf16[128,2048]{1,0:T(8,128)(2,1)}, u32[]{:S(2)}, u32[]{:S(2)}) collective-permute-start(bf16[128,2048]{1,0:T(8,128)(2,1)} %pad_maximum_fusion.15), channel_id=1, source_target_pairs={{0,4},{4,0},{1,5},{5,1},{2,6},{6,2},{3,7},{7,3},{8,12},{12,8},{9,1... | collective-permute-start | bytes 1572872 | tf_op jit(solution)/shard_map/layer1_backward/spread/ppermute | solution.py:40
  175.1 21.5 %collective-permute-start.18 = (bf16[256,432]{1,0:T(8,128)(2,1)}, bf16[256,432]{1,0:T(8,128)(2,1)}, u32[]{:S(2)}, u32[]{:S(2)}) collective-permute-start(bf16[256,432]{1,0:T(8,128)(2,1)} %fusion.58), channel_id=1, source_target_pairs={{0,48},{1,49},{2,50},{3,51},{4,52},{5,53},{6,54},{7,55},{8,56},{9,... | collective-permute-start | bytes 663560 | tf_op jit(solution)/shard_map/layer0_forward/earlier_states/ppermute | solution.py:54
  180.2 16.4 %collective-permute-start.17 = (bf16[256,432]{1,0:T(8,128)(2,1)}, bf16[256,432]{1,0:T(8,128)(2,1)}, u32[]{:S(2)}, u32[]{:S(2)}) collective-permute-start(bf16[256,432]{1,0:T(8,128)(2,1)} %fusion.58), channel_id=1, source_target_pairs={{0,32},{16,48},{1,33},{17,49},{2,34},{18,50},{3,35},{19,51},{4,36}... | collective-permute-start | bytes 663560 | tf_op jit(solution)/shard_map/layer0_forward/earlier_states/ppermute | solution.py:54
  182.2 14.4 %collective-permute-start.16 = (bf16[256,432]{1,0:T(8,128)(2,1)}, bf16[256,432]{1,0:T(8,128)(2,1)}, u32[]{:S(2)}, u32[]{:S(2)}) collective-permute-start(bf16[256,432]{1,0:T(8,128)(2,1)} %fusion.58), channel_id=1, source_target_pairs={{0,16},{16,32},{32,48},{1,17},{17,33},{33,49},{2,18},{18,34},{34,5... | collective-permute-start | bytes 663560 | tf_op jit(solution)/shard_map/layer0_forward/earlier_states/ppermute | solution.py:54
  185.9 223.3 %all-gather.17.cloned.1.call-start = ((), (), s32[]{:S(2)}) async-start(), calls=%async_computation.14 | async-start | bytes 7208960 | tf_op jit(solution)/shard_map/layer0_forward/weights_gate_up_down/all_gather | solution.py:283
  272.2 296.7 %reduce-scatter.12.cloned.1.call-start = ((), (), s32[]{:S(2)}) async-start(), calls=%async_computation.16 | async-start | bytes 1310720 | tf_op jit(solution)/shard_map/layer1_backward/reduce_scatter | solution.py:313
  298.6 78.0 %collective-permute-start.73 = (bf16[256,2048]{1,0:T(8,128)(2,1)}, bf16[256,2048]{1,0:T(8,128)(2,1)}, u32[]{:S(2)}, u32[]{:S(2)}) collective-permute-start(bf16[256,2048]{1,0:T(8,128)(2,1)} %select_dynamic-update-slice_fusion), channel_id=1, source_target_pairs={{0,8},{8,0},{1,9},{9,1},{2,10},{10,2},{3,11},{11,3},{4,12},{12,4},... | collective-permute-start | bytes 3145736 | tf_op jit(solution)/shard_map/layer0_forward/ppermute | solution.py:40
  300.7 79.8 %collective-permute-start.74 = (bf16[256,864]{1,0:T(8,128)(2,1)}, bf16[256,864]{1,0:T(8,128)(2,1)}, u32[]{:S(2)}, u32[]{:S(2)}) collective-permute-start(bf16[256,864]{1,0:T(8,128)(2,1)} %pad_maximum_fusion.26), channel_id=1, source_target_pairs={{0,8},{8,0},{1,9},{9,1},{2,10},{10,2},{3,11},{11,3},{4,12},{12,4},... | collective-permute-start | bytes 1327112 | tf_op jit(solution)/shard_map/layer0_forward/ppermute | solution.py:40
  303.2 36.0 %collective-permute-start.39 = (bf16[256,432]{1,0:T(8,128)(2,1)S(1)}, bf16[256,432]{1,0:T(8,128)(2,1)S(1)}, u32[]{:S(2)}, u32[]{:S(2)}) collective-permute-start(bf16[256,432]{1,0:T(8,128)(2,1)S(1)} %convolution_convert_fusion.4), channel_id=1, source_target_pairs={{0,8},{8,0},{1,9},{9,1},{2,10},{10,2},{3,11},{11,3},{4,12},{12,4},... | collective-permute-start | bytes 663560 | tf_op jit(solution)/shard_map/layer1_forward/earlier_states/ppermute | solution.py:40
  339.3 19.8 %collective-permute-start.42 = (bf16[256,432]{1,0:T(8,128)(2,1)S(1)}, bf16[256,432]{1,0:T(8,128)(2,1)S(1)}, u32[]{:S(2)}, u32[]{:S(2)}) collective-permute-start(bf16[256,432]{1,0:T(8,128)(2,1)S(1)} %fusion.60), channel_id=1, source_target_pairs={{0,48},{1,49},{2,50},{3,51},{4,52},{5,53},{6,54},{7,55},{8,56},{9,... | collective-permute-start | bytes 663560 | tf_op jit(solution)/shard_map/layer1_forward/earlier_states/ppermute | solution.py:54
  342.2 16.9 %collective-permute-start.41 = (bf16[256,432]{1,0:T(8,128)(2,1)S(1)}, bf16[256,432]{1,0:T(8,128)(2,1)S(1)}, u32[]{:S(2)}, u32[]{:S(2)}) collective-permute-start(bf16[256,432]{1,0:T(8,128)(2,1)S(1)} %fusion.60), channel_id=1, source_target_pairs={{0,32},{16,48},{1,33},{17,49},{2,34},{18,50},{3,35},{19,51},{4,36}... | collective-permute-start | bytes 663560 | tf_op jit(solution)/shard_map/layer1_forward/earlier_states/ppermute | solution.py:54
  343.7 22.5 %collective-permute-start.40 = (bf16[256,432]{1,0:T(8,128)(2,1)S(1)}, bf16[256,432]{1,0:T(8,128)(2,1)S(1)}, u32[]{:S(2)}, u32[]{:S(2)}) collective-permute-start(bf16[256,432]{1,0:T(8,128)(2,1)S(1)} %fusion.60), channel_id=1, source_target_pairs={{0,16},{16,32},{32,48},{1,17},{17,33},{33,49},{2,18},{18,34},{34,5... | collective-permute-start | bytes 663560 | tf_op jit(solution)/shard_map/layer1_forward/earlier_states/ppermute | solution.py:54
  371.9 12.6 %collective-permute-start.43 = (bf16[128,2048]{1,0:T(8,128)(2,1)S(1)}, bf16[128,2048]{1,0:T(8,128)(2,1)S(1)}, u32[]{:S(2)}, u32[]{:S(2)}) collective-permute-start(bf16[128,2048]{1,0:T(8,128)(2,1)S(1)} %slice.1561), channel_id=1, source_target_pairs={{0,4},{4,0},{1,5},{5,1},{2,6},{6,2},{3,7},{7,3},{8,12},{12,8},{9,1... | collective-permute-start | bytes 1572872 | tf_op jit(solution)/shard_map/layer1_forward/collect/ppermute | solution.py:40
  375.3 72.9 %collective-permute-start.75 = (bf16[256,1024]{1,0:T(8,128)(2,1)}, bf16[256,1024]{1,0:T(8,128)(2,1)}, u32[]{:S(2)}, u32[]{:S(2)}) collective-permute-start(bf16[256,1024]{1,0:T(8,128)(2,1)} %pad_maximum_fusion.18), channel_id=1, source_target_pairs={{0,8},{8,0},{1,9},{9,1},{2,10},{10,2},{3,11},{11,3},{4,12},{12,4},... | collective-permute-start | bytes 1572872 | tf_op jit(solution)/shard_map/layer1_backward/ppermute | solution.py:40
  416.6 83.4 %collective-permute-start.72 = (bf16[256,864]{1,0:T(8,128)(2,1)}, bf16[256,864]{1,0:T(8,128)(2,1)}, u32[]{:S(2)}, u32[]{:S(2)}) collective-permute-start(bf16[256,864]{1,0:T(8,128)(2,1)} %pad_maximum_fusion.25), channel_id=1, source_target_pairs={{0,8},{8,0},{1,9},{9,1},{2,10},{10,2},{3,11},{11,3},{4,12},{12,4},... | collective-permute-start | bytes 1327112 | tf_op jit(solution)/shard_map/layer1_backward/ppermute | solution.py:40
  442.8 57.2 %collective-permute-start.71 = (bf16[256,2048]{1,0:T(8,128)(2,1)}, bf16[256,2048]{1,0:T(8,128)(2,1)}, u32[]{:S(2)}, u32[]{:S(2)}) collective-permute-start(bf16[256,2048]{1,0:T(8,128)(2,1)} %get-tuple-element.177), channel_id=1, source_target_pairs={{0,8},{8,0},{1,9},{9,1},{2,10},{10,2},{3,11},{11,3},{4,12},{12,4},... | collective-permute-start | bytes 3145736 | tf_op jit(solution)/shard_map/layer1_forward/ppermute | solution.py:40
  452.2 119.3 %reduce-scatter.10.cloned.1.call-start = ((), (), s32[]{:S(2)}) async-start(), calls=%async_computation.15 | async-start | bytes 2293760 | tf_op jit(solution)/shard_map/layer1_backward/reduce_scatter | solution.py:313
  456.9 20.1 %collective-permute-start.63 = (bf16[256,432]{1,0:T(8,128)(2,1)S(1)}, bf16[256,432]{1,0:T(8,128)(2,1)S(1)}, u32[]{:S(2)}, u32[]{:S(2)}) collective-permute-start(bf16[256,432]{1,0:T(8,128)(2,1)S(1)} %convolution_convert_fusion.3), channel_id=1, source_target_pairs={{0,8},{8,0},{1,9},{9,1},{2,10},{10,2},{3,11},{11,3},{4,12},{12,4},... | collective-permute-start | bytes 663560 | tf_op jit(solution)/shard_map/layer1_backward/later_states/ppermute | solution.py:40
  477.1 12.0 %collective-permute-start.66 = (bf16[256,432]{1,0:T(8,128)(2,1)S(1)}, bf16[256,432]{1,0:T(8,128)(2,1)S(1)}, u32[]{:S(2)}, u32[]{:S(2)}) collective-permute-start(bf16[256,432]{1,0:T(8,128)(2,1)S(1)} %fusion.62), channel_id=1, source_target_pairs={{48,0},{49,1},{50,2},{51,3},{52,4},{53,5},{54,6},{55,7},{56,8},{57... | collective-permute-start | bytes 663560 | tf_op jit(solution)/shard_map/layer1_backward/later_states/ppermute | solution.py:54
  478.4 10.7 %collective-permute-start.65 = (bf16[256,432]{1,0:T(8,128)(2,1)S(1)}, bf16[256,432]{1,0:T(8,128)(2,1)S(1)}, u32[]{:S(2)}, u32[]{:S(2)}) collective-permute-start(bf16[256,432]{1,0:T(8,128)(2,1)S(1)} %fusion.62), channel_id=1, source_target_pairs={{32,0},{48,16},{33,1},{49,17},{34,2},{50,18},{35,3},{51,19},{36,4}... | collective-permute-start | bytes 663560 | tf_op jit(solution)/shard_map/layer1_backward/later_states/ppermute | solution.py:54
  503.2 138.8 %reduce-scatter.18.cloned.1.call-start = ((), (), s32[]{:S(2)}) async-start(), calls=%async_computation.19 | async-start | bytes 1310720 | tf_op jit(solution)/shard_map/layer1_backward/reduce_scatter | solution.py:313
  509.4 18.2 %collective-permute-start.91 = (bf16[256,1024]{1,0:T(8,128)(2,1)S(1)}, bf16[256,1024]{1,0:T(8,128)(2,1)S(1)}, u32[]{:S(2)}, u32[]{:S(2)}) collective-permute-start(bf16[256,1024]{1,0:T(8,128)(2,1)S(1)} %pad_maximum_fusion.22), channel_id=1, source_target_pairs={{0,8},{8,0},{1,9},{9,1},{2,10},{10,2},{3,11},{11,3},{4,12},{12,4},... | collective-permute-start | bytes 1572872 | tf_op jit(solution)/shard_map/layer1_backward/ppermute | solution.py:40
  529.1 125.2 %reduce-scatter.14.cloned.1.call-start = ((), (), s32[]{:S(2)}) async-start(), calls=%async_computation.17 | async-start | bytes 1310720 | tf_op jit(solution)/shard_map/layer0_backward/reduce_scatter | solution.py:313
  530.8 13.2 %collective-permute-start.85 = (bf16[256,1024]{1,0:T(8,128)(2,1)S(1)}, bf16[256,1024]{1,0:T(8,128)(2,1)S(1)}, u32[]{:S(2)}, u32[]{:S(2)}) collective-permute-start(bf16[256,1024]{1,0:T(8,128)(2,1)S(1)} %pad_maximum_fusion.20), channel_id=1, source_target_pairs={{0,8},{8,0},{1,9},{9,1},{2,10},{10,2},{3,11},{11,3},{4,12},{12,4},... | collective-permute-start | bytes 1572872 | tf_op jit(solution)/shard_map/layer0_backward/ppermute | solution.py:40
  546.6 123.7 %reduce-scatter.16.cloned.1.call-start = ((), (), s32[]{:S(2)}) async-start(), calls=%async_computation.18 | async-start | bytes 2293760 | tf_op jit(solution)/shard_map/layer0_backward/reduce_scatter | solution.py:313
  549.9 11.0 %collective-permute-start.86 = (bf16[256,864]{1,0:T(8,128)(2,1)S(1)}, bf16[256,864]{1,0:T(8,128)(2,1)S(1)}, u32[]{:S(2)}, u32[]{:S(2)}) collective-permute-start(bf16[256,864]{1,0:T(8,128)(2,1)S(1)} %pad_maximum_fusion.28), channel_id=1, source_target_pairs={{0,8},{8,0},{1,9},{9,1},{2,10},{10,2},{3,11},{11,3},{4,12},{12,4},... | collective-permute-start | bytes 1327112 | tf_op jit(solution)/shard_map/layer0_backward/ppermute | solution.py:40
  564.1 124.0 %reduce-scatter.26.cloned.1.call-start = ((), (), s32[]{:S(2)}) async-start(), calls=%async_computation.23 | async-start | bytes 1310720 | tf_op jit(solution)/shard_map/layer0_backward/reduce_scatter | solution.py:313
  591.7 13.3 %collective-permute-start.123 = (bf16[256,1024]{1,0:T(8,128)(2,1)S(1)}, bf16[256,1024]{1,0:T(8,128)(2,1)S(1)}, u32[]{:S(2)}, u32[]{:S(2)}) collective-permute-start(bf16[256,1024]{1,0:T(8,128)(2,1)S(1)} %pad_maximum_fusion.24), channel_id=1, source_target_pairs={{0,8},{8,0},{1,9},{9,1},{2,10},{10,2},{3,11},{11,3},{4,12},{12,4},... | collective-permute-start | bytes 1572872 | tf_op jit(solution)/shard_map/layer0_backward/ppermute | solution.py:40
  607.5 87.4 %reduce-scatter.20.cloned.1.call-start = ((), (), s32[]{:S(2)}) async-start(), calls=%async_computation.20 | async-start | bytes 3604480 | tf_op jit(solution)/shard_map/layer1_backward/reduce_scatter | solution.py:313
  611.1 26.3 %collective-permute-start.102 = (bf16[128,2048]{1,0:T(8,128)(2,1)}, bf16[128,2048]{1,0:T(8,128)(2,1)}, u32[]{:S(2)}, u32[]{:S(2)}) collective-permute-start(bf16[128,2048]{1,0:T(8,128)(2,1)} %slice.1556), channel_id=1, source_target_pairs={{0,4},{4,0},{1,5},{5,1},{2,6},{6,2},{3,7},{7,3},{8,12},{12,8},{9,1... | collective-permute-start | bytes 1572872 | tf_op jit(solution)/shard_map/layer1_forward/collect/ppermute | solution.py:40
  613.0 11.1 %collective-permute-start.93 = (bf16[256,688]{1,0:T(8,128)(2,1)}, bf16[256,688]{1,0:T(8,128)(2,1)}, u32[]{:S(2)}, u32[]{:S(2)}) collective-permute-start(bf16[256,688]{1,0:T(8,128)(2,1)} %pad_maximum_fusion.29), channel_id=1, source_target_pairs={{0,8},{8,0},{1,9},{9,1},{2,10},{10,2},{3,11},{11,3},{4,12},{12,4},... | collective-permute-start | bytes 1056776 | tf_op jit(solution)/shard_map/layer1_backward/ppermute | solution.py:40
  616.2 16.3 %collective-permute-start.92 = (bf16[256,688]{1,0:T(8,128)(2,1)}, bf16[256,688]{1,0:T(8,128)(2,1)S(1)}, u32[]{:S(2)}, u32[]{:S(2)}) collective-permute-start(bf16[256,688]{1,0:T(8,128)(2,1)} %copy-done.64), channel_id=1, source_target_pairs={{0,8},{8,0},{1,9},{9,1},{2,10},{10,2},{3,11},{11,3},{4,12},{12,4},... | collective-permute-start | bytes 1056776 | tf_op jit(solution)/shard_map/layer1_backward/ppermute | solution.py:40
  636.3 116.7 %reduce-scatter.22.cloned.1.call-start = ((), (), s32[]{:S(2)}) async-start(), calls=%async_computation.21 | async-start | bytes 1966080 | tf_op jit(solution)/shard_map/layer0_backward/reduce_scatter | solution.py:313
  640.4 101.8 %collective-permute-start.103 = (bf16[32,2048]{1,0:T(8,128)(2,1)}, bf16[32,2048]{1,0:T(8,128)(2,1)}, u32[]{:S(2)}, u32[]{:S(2)}) collective-permute-start(bf16[32,2048]{1,0:T(8,128)(2,1)} %get-tuple-element.186), channel_id=1, source_target_pairs={{0,1},{1,2},{2,3},{3,0},{4,5},{5,6},{6,7},{7,4},{8,9},{9,10},{10,1... | collective-permute-start | bytes 393224 | tf_op jit(solution)/shard_map/layer1_forward/collect/ppermute | solution.py:49
  649.6 10.8 %collective-permute-start.94 = (bf16[256,432]{1,0:T(8,128)(2,1)}, bf16[256,432]{1,0:T(8,128)(2,1)}, u32[]{:S(2)}, u32[]{:S(2)}) collective-permute-start(bf16[256,432]{1,0:T(8,128)(2,1)} %convolution_convert_fusion.2), channel_id=1, source_target_pairs={{0,8},{8,0},{1,9},{9,1},{2,10},{10,2},{3,11},{11,3},{4,12},{12,4},... | collective-permute-start | bytes 663560 | tf_op jit(solution)/shard_map/layer0_backward/later_states/ppermute | solution.py:40
  652.5 19.7 %collective-permute-start.117 = (bf16[256,688]{1,0:T(8,128)(2,1)}, bf16[256,688]{1,0:T(8,128)(2,1)}, u32[]{:S(2)}, u32[]{:S(2)}) collective-permute-start(bf16[256,688]{1,0:T(8,128)(2,1)} %pad_maximum_fusion.31), channel_id=1, source_target_pairs={{0,8},{8,0},{1,9},{9,1},{2,10},{10,2},{3,11},{11,3},{4,12},{12,4},... | collective-permute-start | bytes 1056776 | tf_op jit(solution)/shard_map/layer0_backward/ppermute | solution.py:40
  662.3 34.9 %collective-permute-start.97 = (bf16[256,432]{1,0:T(8,128)(2,1)}, bf16[256,432]{1,0:T(8,128)(2,1)}, u32[]{:S(2)}, u32[]{:S(2)}) collective-permute-start(bf16[256,432]{1,0:T(8,128)(2,1)} %fusion.64), channel_id=1, source_target_pairs={{48,0},{49,1},{50,2},{51,3},{52,4},{53,5},{54,6},{55,7},{56,8},{57... | collective-permute-start | bytes 663560 | tf_op jit(solution)/shard_map/layer0_backward/later_states/ppermute | solution.py:54
  663.6 33.6 %collective-permute-start.96 = (bf16[256,432]{1,0:T(8,128)(2,1)}, bf16[256,432]{1,0:T(8,128)(2,1)}, u32[]{:S(2)}, u32[]{:S(2)}) collective-permute-start(bf16[256,432]{1,0:T(8,128)(2,1)} %fusion.64), channel_id=1, source_target_pairs={{32,0},{48,16},{33,1},{49,17},{34,2},{50,18},{35,3},{51,19},{36,4}... | collective-permute-start | bytes 663560 | tf_op jit(solution)/shard_map/layer0_backward/later_states/ppermute | solution.py:54
  672.2 13.7 %collective-permute-start.126 = (bf16[256,864]{1,0:T(8,128)(2,1)}, bf16[256,864]{1,0:T(8,128)(2,1)}, u32[]{:S(2)}, u32[]{:S(2)}) collective-permute-start(bf16[256,864]{1,0:T(8,128)(2,1)} %broadcast_select_fusion.16), channel_id=1, source_target_pairs={{0,72},{8,64},{64,8},{72,0},{1,73},{9,65},{65,9},{73,1},{2,74},{10... | collective-permute-start | bytes 1327112 | tf_op jit(solution)/shard_map/owners/ppermute | solution.py:44
  677.7 81.0 %reduce-scatter.24.cloned.1.call-start = ((), (), s32[]{:S(2)}) async-start(), calls=%async_computation.22 | async-start | bytes 1966080 | tf_op jit(solution)/shard_map/layer0_backward/reduce_scatter | solution.py:313
  677.8 19.4 %collective-permute-start.95 = (bf16[256,432]{1,0:T(8,128)(2,1)}, bf16[256,432]{1,0:T(8,128)(2,1)S(1)}, u32[]{:S(2)}, u32[]{:S(2)}) collective-permute-start(bf16[256,432]{1,0:T(8,128)(2,1)} %fusion.64), channel_id=1, source_target_pairs={{16,0},{32,16},{48,32},{17,1},{33,17},{49,33},{18,2},{34,18},{50,3... | collective-permute-start | bytes 663560 | tf_op jit(solution)/shard_map/layer0_backward/later_states/ppermute | solution.py:54
  689.3 17.4 %collective-permute-start.124 = (bf16[256,432]{1,0:T(8,128)(2,1)}, bf16[256,432]{1,0:T(8,128)(2,1)}, u32[]{:S(2)}, u32[]{:S(2)}) collective-permute-start(bf16[256,432]{1,0:T(8,128)(2,1)} %broadcast_select_fusion.28), channel_id=1, source_target_pairs={{0,72},{8,64},{64,8},{72,0},{1,73},{9,65},{65,9},{73,1},{2,74},{10... | collective-permute-start | bytes 663560 | tf_op jit(solution)/shard_map/owners/ppermute | solution.py:44
  713.9 28.2 %collective-permute-start.105 = (bf16[32,2048]{1,0:T(8,128)(2,1)}, bf16[32,2048]{1,0:T(8,128)(2,1)}, u32[]{:S(2)}, u32[]{:S(2)}) collective-permute-start(bf16[32,2048]{1,0:T(8,128)(2,1)} %get-tuple-element.187), channel_id=1, source_target_pairs={{0,3},{1,0},{2,1},{3,2},{4,7},{5,4},{6,5},{7,6},{8,11},{9,8},{10,9... | collective-permute-start | bytes 393224 | tf_op jit(solution)/shard_map/layer1_forward/collect/ppermute | solution.py:49
  729.9 12.2 %collective-permute-start.104 = (bf16[32,2048]{1,0:T(8,128)(2,1)}, bf16[32,2048]{1,0:T(8,128)(2,1)S(1)}, u32[]{:S(2)}, u32[]{:S(2)}) collective-permute-start(bf16[32,2048]{1,0:T(8,128)(2,1)} %get-tuple-element.188), channel_id=1, source_target_pairs={{0,2},{1,3},{2,0},{3,1},{4,6},{5,7},{6,4},{7,5},{8,10},{9,11},{10,... | collective-permute-start | bytes 393224 | tf_op jit(solution)/shard_map/layer1_forward/collect/ppermute | solution.py:49
  750.2 12.3 %collective-permute-start.106 = (f32[32,2048]{1,0:T(8,128)S(1)}, f32[32,2048]{1,0:T(8,128)S(1)}, u32[]{:S(2)}, u32[]{:S(2)}) collective-permute-start(f32[32,2048]{1,0:T(8,128)S(1)} %broadcast_select_fusion.91), channel_id=1, source_target_pairs={{0,64},{64,0},{1,65},{65,1},{2,66},{66,2},{3,67},{67,3},{4,68},{68... | collective-permute-start | bytes 786440 | tf_op jit(solution)/shard_map/ppermute | solution.py:40
  758.9 10.8 %collective-permute-start.121 = (bf16[256,688]{1,0:T(8,128)(2,1)S(1)}, bf16[256,688]{1,0:T(8,128)(2,1)S(1)}, u32[]{:S(2)}, u32[]{:S(2)}) collective-permute-start(bf16[256,688]{1,0:T(8,128)(2,1)S(1)} %get-tuple-element.184), channel_id=1, source_target_pairs={{0,72},{8,64},{64,8},{72,0},{1,73},{9,65},{65,9},{73,1},{2,74},{10... | collective-permute-start | bytes 1056776 | tf_op jit(solution)/shard_map/owners/ppermute | solution.py:44
  761.9 16.2 %collective-permute-start.118 = (bf16[256,688]{1,0:T(8,128)(2,1)S(1)}, bf16[256,688]{1,0:T(8,128)(2,1)S(1)}, u32[]{:S(2)}, u32[]{:S(2)}) collective-permute-start(bf16[256,688]{1,0:T(8,128)(2,1)S(1)} %get-tuple-element.185), channel_id=1, source_target_pairs={{0,72},{8,64},{64,8},{72,0},{1,73},{9,65},{65,9},{73,1},{2,74},{10... | collective-permute-start | bytes 1056776 | tf_op jit(solution)/shard_map/owners/ppermute | solution.py:44
  (289 other events, 2902.5 us)
Sparse Core Ops, SparseCore 0:
  52.1 40.2 all-gather.6
  94.1 52.7 all-gather.8
  148.5 46.9 all-gather.12
  197.1 64.7 all-gather.10
  263.4 53.2 all-gather.14
  318.1 70.0 all-gather.16
  452.3 28.6 reduce-scatter.11
  503.3 28.5 reduce-scatter.9
  534.4 21.8 reduce-scatter.17
  558.5 23.3 reduce-scatter.13
  584.4 28.5 reduce-scatter.15
  615.4 21.8 reduce-scatter.25
  639.7 48.4 reduce-scatter.19
  690.4 23.4 reduce-scatter.21
  730.0 28.6 reduce-scatter.23

commit v3 on v2

--- a/solution.py
+++ b/solution.py
@@ -22,6 +22,10 @@
 
 def row_major(v):
     return with_layout_constraint(v, Layout(major_to_minor=tuple(range(v.ndim))))
+
+
+def columns_major(v):
+    return with_layout_constraint(v, Layout(major_to_minor=(1, 0)))
 
 
 def mm(a, b):
@@ -124,7 +128,7 @@
     pair = low(fade * first + second)
     total = wide(shift(pair, "x", 1))
     total = total + (fade**2) * wide(shift(pair, "x", 2)) + (fade**4) * wide(shift(pair, "x", 3))
-    return pick(y == 0, total, fade * total + first), got
+    return pick(y == 0, total, fade * total + first), pair
 
 
 def states_after(state, ctx):
@@ -145,17 +149,17 @@
 
 
 def forward(h, a_rows, ffn_gain, weights, ctx, waits=()):
-    w_kv, w_qgo, get_gud = weights
+    w_in, w_out, get_gud = weights
     K, V, F = ctx["sizes"]
-    kv = mm(a_rows, w_kv)
+    split = len(w_in) == 2
+    kv = mm(a_rows, w_in[0])
     k, v = low(kv[:, :K]), low(kv[:, K : K + V])
     faded_k = low(wide(k) * ctx["to_end"])
-    state_in, swapped = earlier_states(mm_left(faded_k, v), ctx)
+    state_in, pair = earlier_states(mm_left(faded_k, v), ctx)
     state_in = low(state_in)
-    w_gud = get_gud(swapped)
+    w_gud = get_gud(pair)
     w_gu, w_down = w_gud[:, : 2 * F], w_gud[:, 2 * F :]
-    w_qg, w_out = w_qgo[:, : K + V], w_qgo[:, K + V :]
-    qg = mm(a_rows, w_qg)
+    qg = mm(a_rows, w_in[1]) if split else kv[:, K + V :]
     q, ret_gate = low(qg[:, :K]), qg[:, K:]
     scores = low(mm_right(q, k) * ctx["decay_mask"])
     retained = mm(scores, v) + mm(q, state_in) * ctx["from_start"]
@@ -163,23 +167,25 @@
     gated = low(silu(ret_gate) * (retained * n))
     mid = h + collect(mm_right(gated, w_out))
     b_rows = spread(low(mid * rms_inverse(mid) * ffn_gain))
-    pairs, _ = swap_halves((a_rows, b_rows), (), ctx)
     gu = mm(b_rows, w_gu)
     gate_pre, up_pre = gu[:, :F], gu[:, F:]
     hidden = hold(low(silu(gate_pre) * up_pre), *waits)
-    _, rights = swap_halves((), (gated, hidden), ctx)
-    out = mid + collect(mm_right(hidden, w_down))
-    record = (pairs, rights, k, v, q, state_in, scores, ret_gate, retained, mid, gu)
-    return out, record, (w_kv, w_qg, w_out, w_gu, w_down)
-
-
-def backward(h, g_out, d_f_rows, record, gains, weights, ctx, merged, waits=((), (), ())):
-    w_kv, w_qg, w_out, w_gu, w_down = weights
+    record = (a_rows, b_rows, gated, hidden, k, v, q, state_in, scores, ret_gate, retained, mid, gu)
+    return record, (w_in, w_out, w_gu, w_down)
+
+
+def layer_out(record, weights):
+    hidden, mid = record[3], record[-2]
+    return mid + collect(mm_right(hidden, weights[-1]))
+
+
+def backward(h, g_out, d_f_rows, record, pairs, gains, weights, ctx, waits):
+    a_pair, b_pair = pairs
+    w_in, w_out, w_gu, w_down = weights
     attn_gain, ffn_gain = gains
     K, V, F = ctx["sizes"]
-    (a_pair, b_pair), (gated_pair, hidden_pair), k, v, q, state_in, scores, ret_gate, retained, mid, gu = record
+    a_rows, b_rows, gated, hidden, k, v, q, state_in, scores, ret_gate, retained, mid, gu = record
     d_f = spread(d_f_rows)
-    (f_pair,), _ = swap_halves((d_f,), (), ctx)
     d_hidden = mm(d_f, w_down)
     gate_pre, up_pre = gu[:, :F], gu[:, F:]
     s = jax.nn.sigmoid(gate_pre)
@@ -187,14 +193,11 @@
     d_up = low(d_hidden * gate_pre * s)
     d_gu = jnp.concatenate([d_gate, d_up], axis=1)
     d_b = collect(mm_right(d_gu, w_gu))
-    _, (gu_pair,) = swap_halves((), (d_gu,), ctx)
-    part_down = settle(weight_grad(f_pair, hidden_pair))
-    part_gu = settle(weight_grad(b_pair, gu_pair))
+    part_gu = settle(weight_grad(b_pair, d_gu))
     d_b = hold(d_b, *waits[0])
     d_norm, grad_ffn_gain = norm_back(mid, ffn_gain, d_b)
     d_mid = g_out + d_norm
     d_r = spread(low(d_mid))
-    (r_pair,), _ = swap_halves((d_r,), (), ctx)
     d_gated = mm(d_r, w_out)
     s = jax.nn.sigmoid(ret_gate)
     n = lax.rsqrt(jnp.mean(retained * retained, axis=-1, keepdims=True) + group_floor)
@@ -206,63 +209,53 @@
     d_ret_low = low(d_ret)
     d_ret_start = low(d_ret * ctx["from_start"])
     beyond = low(later_states(mm_left(q, d_ret_start), ctx))
-    part_out = settle(weight_grad(r_pair, gated_pair))
+    grad_od = [row_major(low(mm_left(left, right))) for left, right in ((d_r, gated), (d_f, hidden))]
+    part_od = settle(jnp.concatenate(grad_od, axis=1))
+    beyond = hold(beyond, *waits[1](part_gu))
     d_scores = low(mm_right(d_ret_low, v) * ctx["decay_mask"])
     d_q = low(mm(d_scores, k) + mm_right(d_ret_start, state_in))
     d_qg = jnp.concatenate([d_q, d_ret_gate], axis=1)
-    _, (qg_pair,) = swap_halves((), (d_qg,), ctx)
-    beyond = hold(beyond, *waits[1])
-    if not merged:
-        part_qg = settle(weight_grad(a_pair, qg_pair))
+    if len(w_in) == 2:
+        part_qg = settle(weight_grad(a_pair, d_qg))
     d_k = low(mm_left(d_scores, q) + mm_right(v, beyond) * ctx["to_end"])
     d_v = low(mm_left(scores, d_ret_low) + mm(k, beyond) * ctx["to_end"])
     d_kv = jnp.concatenate([d_k, d_v], axis=1)
-    d_kv_wide = jnp.pad(d_kv, ((0, 0), (0, w_kv.shape[1] - d_kv.shape[1])))
-    partial = mm_right(d_qg, w_qg) + mm_right(d_kv_wide, w_kv)
-    d_a = collect(partial)
-    _, (kv_pair,) = swap_halves((), (d_kv,), ctx)
-    if merged:
-        pair = tuple(jnp.concatenate(p, axis=1) for p in zip(kv_pair, qg_pair))
-        part_in = settle(weight_grad(a_pair, pair))
+    if len(w_in) == 2:
+        d_kv_wide = jnp.pad(d_kv, ((0, 0), (0, w_in[0].shape[1] - d_kv.shape[1])))
+        d_a = collect(mm_right(d_qg, w_in[1]) + mm_right(d_kv_wide, w_in[0]))
+        grad_kv = weight_grad(a_pair, d_kv)
+        part_kv = settle(grad_kv)
+        d_a = hold(d_a, grad_kv, *waits[2](part_qg))
+    else:
+        d_in = jnp.concatenate([d_kv, d_qg], axis=1)
+        d_a = collect(mm_right(d_in, w_in[0]))
+        part_in = settle(weight_grad(a_pair, d_in))
         part_kv, part_qg = part_in[:, : K + V], part_in[:, K + V :]
-    else:
-        part_kv = settle(weight_grad(a_pair, kv_pair))
-        d_a = hold(d_a, part_down, part_gu)
     d_norm, grad_attn_gain = norm_back(h, attn_gain, d_a)
-    parts = (part_kv, part_qg, part_out, part_gu, part_down)
+    parts = (part_kv, part_qg, part_od, part_gu)
     return d_mid + d_norm, parts, (grad_attn_gain, grad_ffn_gain)
-
-
-def swap_halves(lefts, rights, ctx):
-    n = lax.axis_size("x")
-
-    def half(v, which):
-        width = v.shape[1] // (2 * n)
-        cut = [v[:, i * width : (i + 1) * width] for i in range(2 * n)]
-        return jnp.concatenate([pick(which == 0, cut[2 * i], cut[2 * i + 1]) for i in range(n)], axis=1)
-
-    place = ctx["place"]
-    keeps = [half(v, place) for v in lefts]
-    sent = jnp.concatenate([half(v, 1 - place) for v in lefts] + list(rights), axis=1)
-    got = swap(sent, "ylo")
-    at, left_pairs, right_pairs = 0, [], []
-    for keep in keeps:
-        left_pairs.append((keep, got[:, at : at + keep.shape[1]]))
-        at += keep.shape[1]
-    for right in rights:
-        right_pairs.append((right, got[:, at : at + right.shape[1]]))
-        at += right.shape[1]
-    return left_pairs, right_pairs
-
-
-def weight_grad(left, right):
-    return row_major(low(mm_left(left[0], right[0]) + mm_left(left[1], right[1])))
 
 
 def halves(w, core):
     n = w.shape[1] // 2
     first, second = w[:, :n], w[:, n:]
     return pick(core == 0, first, second), pick(core == 0, second, first)
+
+
+def swap_half(v, ctx):
+    n = lax.axis_size("x")
+    width = v.shape[1] // (2 * n)
+    cut = [v[:, i * width : (i + 1) * width] for i in range(2 * n)]
+
+    def half(which):
+        return jnp.concatenate([pick(which == 0, cut[2 * i], cut[2 * i + 1]) for i in range(n)], axis=1)
+
+    place = ctx["place"]
+    return half(place), swap(half(1 - place), "ylo")
+
+
+def weight_grad(left, right):
+    return row_major(low(mm_left(left[0], right) + mm_left(left[1], swap(right, "ylo"))))
 
 
 def corner(v):
@@ -310,12 +303,25 @@
 
 
 def settle(grad):
-    return lax.psum_scatter(grad, "x", scatter_dimension=0, tiled=True)
-
-
-def share_out(first, second, ctx):
-    section, core = ctx["section"], ctx["core"]
-    total = wide(pick(section == 0, first, second)) + wide(cross(pick(section == 0, second, first)))
+    return lax.psum_scatter(row_major(grad), "x", scatter_dimension=0, tiled=True)
+
+
+def sum_along_y(first, second, ctx):
+    section, at_0 = ctx["section"], ctx["ylo"] == 0
+    half = first.shape[0] // 2
+    mine, theirs = pick(section == 0, first, second), pick(section == 0, second, first)
+    keep, near = pick(at_0, mine[:half], mine[half:]), pick(at_0, mine[half:], mine[:half])
+    facing, crossed = pick(at_0, theirs[:half], theirs[half:]), pick(at_0, theirs[half:], theirs[:half])
+    return wide(keep) + wide(swap(near, "ylo")) + wide(swap(facing, "section")) + wide(cross(crossed))
+
+
+def sum_across(first, second, ctx):
+    section = ctx["section"]
+    return wide(pick(section == 0, first, second)) + wide(cross(pick(section == 0, second, first)))
+
+
+def share_out(total, ctx):
+    core = ctx["core"]
     half = total.shape[0] // 2
     keep = pick(core == 0, total[:half], total[half:])
     give = pick(core == 0, total[half:], total[:half])
@@ -369,8 +375,8 @@
     decays_far = swap(decays_all, "section")
     head = tensor * 2 + core
 
-    def context(layer):
-        rates = pick(section == layer, decays_all, decays_far)
+    def context(layer, docs, rates_ready=()):
+        rates = hold(pick(section == layer, decays_all, decays_far)[None], *rates_ready)[0]
         rate = lax.dynamic_index_in_dim(rates, head, 0, False)
         gap = places[:, None] - places[None, :]
         allowed = (gap >= 0) & (docs[:, None] == docs[None, :])
@@ -390,84 +396,102 @@
             "sizes": (K, V, F),
         }
 
-    ctxs = (context(0), context(1))
-    ctx = ctxs[0]
+    ctx = {"ylo": ylo, "core": core, "section": section}
 
     gain_columns = jnp.stack([attn_gain[0], ffn_gain[0]], axis=1)
     gain_columns = jnp.concatenate([gain_columns, gain_columns], axis=1)
-    h0_rows = wide(spread(h0))
     with jax.named_scope("weights_key_value"):
         own_kv = pack((w_key[0], w_value[0], gain_columns), ctx)
-        ready = (h0_rows, ctxs[0]["decay_mask"], ctxs[1]["decay_mask"])
-        kv0, kv1 = y_then_x(own_kv, along_y(own_kv), ctx, ready)
+        kv0, kv1 = y_then_x(own_kv, along_y(own_kv), ctx)
+        kv0 = jnp.concatenate([kv0, kv1[:, K + V :]], axis=1)
     with jax.named_scope("weights_query_gate_out"):
         own_qgo = hold(pack((w_query[0], w_gate_ret[0], w_out[0].T), ctx), kv0)
-        qgo0, qgo1 = y_then_x(own_qgo, along_y(own_qgo), ctx)
+        moved_qgo = along_y(own_qgo)
+    h0_rows = wide(spread(hold(h0, moved_qgo[0])))
+    ctx0 = context(0, docs)
+    with jax.named_scope("weights_query_gate_out"):
+        qgo0, qgo1 = y_then_x(own_qgo, moved_qgo, ctx, (h0_rows, ctx0["decay_mask"]))
     with jax.named_scope("gather_weights"):
-        kv0, kv1 = gather_x(kv0), gather_x(kv1)
-        qgo0, qgo1 = gather_x(qgo0), gather_x(qgo1)
+        kv0, qgo0 = gather_x(kv0), gather_x(qgo0)
+        in1 = gather_x(jnp.concatenate([kv1[:, : K + V], qgo1], axis=1))
     second = []
 
-    def get_gud(swapped):
+    def get_gud(pair):
         with jax.named_scope("weights_gate_up_down"):
-            own_gud = hold(pack((w_gate[0], w_up[0], w_down[0].T), ctx), swapped)
-            gud0, gud1 = y_then_x(own_gud, along_y(own_gud), ctx)
+            own_gud = columns_major(pack((w_gate[0], w_up[0], w_down[0].T), ctx))
+            moved_gud = [columns_major(v) for v in along_y(own_gud)]
+            gud0, gud1 = y_then_x(own_gud, moved_gud, ctx, (pair,))
             second.append(gather_x(gud1))
             return gather_x(gud0)
 
-    def gain_rows(columns):
-        columns = wide(columns).T
-        return columns[0], columns[1]
-
-    gains0 = gain_rows(kv0[:, K + V : K + V + 2])
-    gains1 = gain_rows(kv1[:, K + V : K + V + 2])
-    weights0 = (kv0, qgo0, get_gud)
-    weights1 = (kv1, qgo1, lambda swapped: second[0])
+    gain_rows = wide(kv0[:, K + V :]).T
+    gains0, gains1 = gain_rows[:2], gain_rows[2:]
+    n_in = 2 * (K + V)
+    weights0 = ((kv0, qgo0[:, : K + V]), qgo0[:, K + V :], get_gud)
+    weights1 = ((in1[:, :n_in],), in1[:, n_in:], lambda pair: second[0])
 
     a0 = low(h0_rows * rms_inverse(h0_rows) * gains0[0])
     h0 = wide(h0)
     with jax.named_scope("layer0_forward"):
-        out_first, record0, weights0 = forward(h0, a0, gains0[1], weights0, ctxs[0])
+        record0, weights0 = forward(h0, a0, gains0[1], weights0, ctx0)
+        out_first = layer_out(record0, weights0)
     h1 = wide(low(out_first))
     a1 = spread(low(h1 * rms_inverse(h1) * gains1[0]))
-    early = [pair[1] for pair in record0[0] + record0[1]]
+    ctx1 = context(1, docs, (h1,))
+    pairs0 = swap_half(a0, ctx0), swap_half(record0[1], ctx0)
+    early = [pair[1] for pair in pairs0]
     with jax.named_scope("layer1_forward"):
-        out_second, record1, weights1 = forward(h1, a1, gains1[1], weights1, ctxs[1], early)
-
+        record1, weights1 = forward(h1, a1, gains1[1], weights1, ctx1, early)
+    pairs1 = swap_half(a1, ctx1), swap_half(record1[1], ctx1)
+
+    with jax.named_scope("layer1_out"):
+        out_second = layer_out(record1, weights1)
     with jax.named_scope("layer1_backward"):
+        waits = (pairs1[0][1:], lambda part: (out_second, part))
         d_h1, parts1, gain_grads1 = backward(
-            h1, wide(g1), g1, record1, gains1, weights1, ctxs[1], True
+            h1, wide(g1), hold(g1, h1), record1, pairs1, gains1, weights1, ctx1, waits
         )
     d_f0 = low(d_h1)
-    kv1, qg1, out1, gu1, down1 = parts1
+    kv1, qg1, od1, gu1 = parts1
+    sums = {}
+
+    def sum_gu(part):
+        sums["gu"] = sum_across(part, gu1, ctx)
+        return (sums["gu"],)
+
+    def sum_qg(part):
+        sums["qg"] = sum_across(part, qg1, ctx)
+        return (sums["qg"],)
+
     with jax.named_scope("layer0_backward"):
+        waits = ((od1, kv1), sum_gu, sum_qg)
         d_h0, parts0, gain_grads0 = backward(
-            h0, wide(d_f0), d_f0, record0, gains0, weights0, ctxs[0], False, ((gu1, down1), (out1, kv1))
+            h0, wide(d_f0), d_f0, record0, pairs0, gains0, weights0, ctx0, waits
         )
-    kv0, qg0, out0, gu0, down0 = parts0
+    kv0, qg0, od0, gu0 = parts0
+    gain_grads = jnp.stack(gain_grads0 + gain_grads1)
+
+    def reduce_gains(*moves):
+        with jax.named_scope("gains"):
+            return gain_grads + sum(move(gain_grads) for move in moves)
+
     with jax.named_scope("owners"):
-        kv, qg, out, gu, down = (
-            share_out(a, b, ctx)
-            for a, b in ((kv0, kv1), (qg0, qg1), (out0, out1), (gu0, gu1), (down0, down1))
-        )
+        gain_grads = reduce_gains(*(lambda v, k=k: turn(v, "tensor", k) for k in (1, 2, 3)))
+        gain_grads = reduce_gains(lambda v: swap(v, "core"))
+        gain_grads = reduce_gains(*(lambda v, k=k: turn(v, "x", k) for k in (1, 2, 3)))
+        kv = sum_across(kv0, kv1, ctx)
+        gain_grads = hold(reduce_gains(lambda v: swap(v, "ylo"), cross, lambda v: swap(v, "section")), kv)
+        od = sum_along_y(od0, od1, ctx)
+        kv, qg, od, gu = (share_out(total, ctx) for total in (kv, sums["qg"], od, sums["gu"]))
     grad_key = both(kv, 0, K, ctx)
     grad_value = both(kv, K, K + V, ctx)
     grad_query = both(qg, 0, K, ctx)
     grad_gate_ret = both(qg, K, K + V, ctx)
-    grad_out = both(out, 0, V, ctx).T
+    grad_out = both(od, 0, V, ctx).T
+    grad_down = both(od, V, V + F, ctx).T
     grad_gate = both(gu, 0, F, ctx)
     grad_up = both(gu, F, 2 * F, ctx)
-    grad_down = both(down, 0, F, ctx).T
-
-    gain_grads = jnp.stack(gain_grads0 + gain_grads1)
-    with jax.named_scope("gains"):
-        for moves in (
-            [lambda v, k=k: turn(v, "tensor", k) for k in (1, 2, 3)],
-            [lambda v: swap(v, "core")],
-            [lambda v, k=k: turn(v, "x", k) for k in (1, 2, 3)],
-            [lambda v: swap(v, "ylo"), cross, lambda v: swap(v, "section")],
-        ):
-            gain_grads = gain_grads + sum(move(gain_grads) for move in moves)
+
     own_gains = pick(section == 0, gain_grads[:2], gain_grads[2:])
     width = attn_gain.shape[1]
     own_gains = lax.dynamic_slice_in_dim(own_gains, (block * 2 + core) * width, width, 1)

time: 804 us -> 736 us (0.915)
  other arithmetic: 103 us -> 71.2 us
  matrix products: 96.1 us -> 75.4 us
  local copies, waits for them, and re-layouts: 59.8 us -> 39.3 us
  waiting for transfers between devices: 308 us -> 319 us
    ppermute x54, waiting for transfers between devices: 60.4 us -> 87.4 us  [turn(): return lax.ppermute(v, axis, [(i, (i + by) % n) for i in range(n)])]
    ppermute x9 -> x8, waiting for transfers between devices: 80.8 us -> 55.7 us  [cross(): return lax.ppermute(v, ('section', 'ylo'), [(0, 3), (1, 2), (2, 1), (3, 0)])]
    dot_general x26 -> x22, matrix products: 38.3 us -> 23.4 us  [mm_left(): lax.dot_general(a, b, (((0,), (0,)), ((), ())), preferred_element_type=f32)]
    all_gather x6 -> x5, waiting for transfers between devices: 33.8 us -> 44.5 us  [gather_x(): return lax.all_gather(rows, 'x', axis=0, tiled=True)]
    ppermute x55 -> x51, starting transfers between devices: 69.3 us -> 78.9 us  [swap(): return lax.ppermute(v, axis, [(0, 1), (1, 0)])]
    ppermute x6 -> x0, local copies, waits for them, and re-layouts: 8.91 us -> none  [the longest x4 7.19 us: swap(): return lax.ppermute(v, axis, [(0, 1), (1, 0)])]
    ppermute x9 -> x8, starting transfers between devices: 21.7 us -> 13 us  [cross(): return lax.ppermute(v, ('section', 'ylo'), [(0, 3), (1, 2), (2, 1), (3, 0)])]
    select_n x32 -> x30, other arithmetic: 18.7 us -> 13.1 us  [pick(): return jnp.where(flag, a, b)]
  transfers between devices with their start and end apart: 145 -> 137, of which waited for: 68 -> 71; matrix products, arithmetic and copies ran while one was open for 30% -> 23% of each run, Pallas kernels for 0% -> 0%
where the time goes in v3:
time: 736 us; the launch traced here: 726 us
  waiting for transfers between devices  319 us (43%)
  starting transfers between devices  177 us (24%)
  matrix products  75.4 us (10%)
  other arithmetic  71.2 us (10%)
  between operations  44 us (6%)
  local copies, waits for them, and re-layouts  39.3 us (5%)
    ppermute x51, waiting for transfers between devices, swap(): return lax.ppermute(v, axis, [(0, 1), (1, 0)])  92.8 us
    ppermute x54, waiting for transfers between devices, turn(): return lax.ppermute(v, axis, [(i, (i + by) % n) for i in range(n)])  87.4 us
    ppermute x51, starting transfers between devices, swap(): return lax.ppermute(v, axis, [(0, 1), (1, 0)])  78.9 us
    ppermute x54, starting transfers between devices, turn(): return lax.ppermute(v, axis, [(i, (i + by) % n) for i in range(n)])  61.4 us
    ppermute x8, waiting for transfers between devices, cross(): return lax.ppermute(v, ('section', 'ylo'), [(0, 3), (1, 2), (2, 1), (3, 0)])  55.7 us
    all_gather x5, waiting for transfers between devices, gather_x(): return lax.all_gather(rows, 'x', axis=0, tiled=True)  44.5 us
    ppermute x12, waiting for transfers between devices, shift(): lax.ppermute(v, axis, [(i, i + by) for i in range(n) if 0 <= i + by < n])  37.1 us
    dot_general x17, matrix products, mm(): lax.dot_general(a, b, (((1,), (0,)), ((), ())), preferred_element_type=f32)  30 us
  transfers between devices with their start and end apart: 137, of which 71 were waited for; matrix products, arithmetic and copies ran while one was open for 23% of the time, Pallas kernels for 0%

profile of v3, /device:TPU:1, one launch (start us, length us, event | category | flops | bytes accessed | tf_op | source)
XLA Modules:
  0.0 725.7 jit_solution(2700675647379481270)
XLA Ops:
  14.4 2.9 collective-permute-start.2
  18.0 15.4 %collective-permute-done.2 = bf16[256,690]{0,1:T(8,128)(2,1)S(1)} collective-permute-done((bf16[256,690]{0,1:T(8,128)(2,1)S(1)}, bf16[256,690]{0,1:T(8,128)(2,1)S(1)}, u32[]{:S(2)}, u32[]{:S(2)}) %collective-permute-start.2) | collective-permute-done | bytes 353312 | tf_op jit(solution)/shard_map/weights_key_value/ppermute | solution.py:48
  37.4 2.8 collective-permute-start
  50.0 8.8 %collective-permute-done.6 = bf16[256,1120]{0,1:T(8,128)(2,1)S(1)} collective-permute-done((bf16[256,1120]{0,1:T(8,128)(2,1)S(1)}, bf16[256,1120]{0,1:T(8,128)(2,1)S(1)}, u32[]{:S(2)}, u32[]{:S(2)}) %collective-permute-start.6) | collective-permute-done | bytes 573472 | tf_op jit(solution)/shard_map/weights_query_gate_out/ppermute | solution.py:44
  62.5 3.3 collective-permute-start.8
  73.3 4.0 collective-permute-done.14
  96.6 2.8 convolution_convert_fusion.4
  100.2 6.2 collective-permute-done.28
  106.4 14.1 %collective-permute-done.29 = bf16[256,1296]{0,1:T(8,128)(2,1)} collective-permute-done((bf16[256,1296]{0,1:T(8,128)(2,1)S(1)}, bf16[256,1296]{0,1:T(8,128)(2,1)}, u32[]{:S(2)}, u32[]{:S(2)}) %collective-permute-start.29) | collective-permute-done | bytes 663584 | tf_op jit(solution)/shard_map/layer0_forward/weights_gate_up_down/ppermute | solution.py:44
  122.4 2.8 broadcast_select_fusion.7
  132.0 4.4 collective-permute-start.18
  140.2 4.2 collective-permute-done.18
  147.1 3.1 fusion.15
  159.2 3.8 collective-permute-start.22
  163.8 4.8 collective-permute-done.22
  169.0 3.3 collective-permute-done.20
  175.8 6.2 collective-permute-done.25
  185.4 9.4 %all-gather.10.cloned.1.call-done = bf16[2048,1296]{0,1:T(8,128)(2,1)} async-done(((bf16[512,1296]{0,1:T(8,128)(2,1)}), bf16[2048,1296]{0,1:T(8,128)(2,1)}) %all-gather.10.cloned.1.call-update) | async-done | bytes 5308432 | tf_op jit(solution)/shard_map/layer0_forward/weights_gate_up_down/all_gather | solution.py:276
  194.8 3.1 fusion.12
  212.0 2.9 collective-permute-done.34
  215.6 3.9 collective-permute-done.32
  227.7 3.4 collective-permute-done.37
  236.8 35.0 %all-gather.12.cloned.1.call-done = bf16[2048,1808]{0,1:T(8,128)(2,1)} async-done(((bf16[512,1808]{0,1:T(8,128)(2,1)}), bf16[2048,1808]{0,1:T(8,128)(2,1)}) %all-gather.12.cloned.1.call-update) | async-done | bytes 7405584 | tf_op jit(solution)/shard_map/gather_weights/all_gather | solution.py:276
  271.8 5.6 fusion.206
  280.1 4.1 collective-permute-done.39
  284.2 3.0 collective-permute-start.42
  291.3 9.2 %collective-permute-done.42 = bf16[256,432]{0,1:T(8,128)(2,1)S(1)} collective-permute-done((bf16[256,432]{0,1:T(8,128)(2,1)S(1)}, bf16[256,432]{0,1:T(8,128)(2,1)S(1)}, u32[]{:S(2)}, u32[]{:S(2)}) %collective-permute-start.42) | collective-permute-done | bytes 221216 | tf_op jit(solution)/shard_map/layer1_forward/earlier_states/ppermute | solution.py:58
  300.5 7.3 %collective-permute-done.40 = bf16[256,432]{0,1:T(8,128)(2,1)S(1)} collective-permute-done((bf16[256,432]{0,1:T(8,128)(2,1)S(1)}, bf16[256,432]{0,1:T(8,128)(2,1)S(1)}, u32[]{:S(2)}, u32[]{:S(2)}) %collective-permute-start.40) | collective-permute-done | bytes 221216 | tf_op jit(solution)/shard_map/layer1_forward/earlier_states/ppermute | solution.py:58
  317.8 2.7 collective-permute-start.46
  322.8 3.0 collective-permute-done.46
  326.5 3.9 collective-permute-done.44
  334.9 5.4 collective-permute-done.54
  342.7 6.4 collective-permute-done.50
  350.2 5.1 collective-permute-done.48
  363.6 3.5 fusion.8
  378.1 18.6 %collective-permute-done.71 = bf16[256,864]{0,1:T(8,128)(2,1)S(1)} collective-permute-done((bf16[256,864]{0,1:T(8,128)(2,1)S(1)}, bf16[256,864]{0,1:T(8,128)(2,1)S(1)}, u32[]{:S(2)}, u32[]{:S(2)}) %collective-permute-start.71) | collective-permute-done | bytes 442400 | tf_op jit(solution)/shard_map/layer1_backward/ppermute | solution.py:44
  407.7 3.9 collective-permute-done.57
  412.6 3.4 collective-permute-done.67
  419.6 6.0 collective-permute-done.62
  431.4 3.1 pad_maximum_fusion
  442.5 5.4 collective-permute-done.72
  454.9 13.0 %collective-permute-done.75 = bf16[256,432]{0,1:T(8,128)(2,1)} collective-permute-done((bf16[256,432]{0,1:T(8,128)(2,1)S(1)}, bf16[256,432]{0,1:T(8,128)(2,1)}, u32[]{:S(2)}, u32[]{:S(2)}) %collective-permute-start.75) | collective-permute-done | bytes 221216 | tf_op jit(solution)/shard_map/layer1_backward/later_states/ppermute | solution.py:58
  471.6 4.5 fusion
  479.9 6.2 collective-permute-done.80
  502.5 3.5 collective-permute-done.83
  506.8 5.4 collective-permute-start.84
  524.0 5.9 collective-permute-done.93
  538.8 3.2 collective-permute-start.90
  543.8 3.7 collective-permute-done.90
  557.2 7.1 collective-permute-done.100
  567.2 3.6 collective-permute-start.94
  575.2 5.4 collective-permute-done.94
  588.5 4.0 collective-permute-done.99
  594.5 3.1 convolution_convert_fusion
  597.7 10.0 %collective-permute-start.124 = (bf16[128,864]{1,0:T(8,128)(2,1)S(1)}, bf16[128,864]{1,0:T(8,128)(2,1)S(1)}, u32[]{:S(2)}, u32[]{:S(2)}) collective-permute-start(bf16[128,864]{1,0:T(8,128)(2,1)S(1)} %select_convert_fusion), channel_id=1, source_target_pairs={{0,4},{4,0},{1,5},{5,1},{2,6},{6,2},{3,7},{7,3},{8,12},{12,8},{9,1... | collective-permute-start | bytes 663560 | tf_op jit(solution)/shard_map/owners/ppermute | solution.py:44
  616.3 2.9 convolution_add_fusion
  621.7 3.1 pad_maximum_fusion.1
  630.1 2.9 collective-permute-start.107
  633.2 2.8 collective-permute-start.105
  637.0 3.7 collective-permute-done.107
  640.7 8.5 %collective-permute-done.101 = bf16[256,688]{1,0:T(8,128)(2,1)S(1)} collective-permute-done((bf16[256,688]{1,0:T(8,128)(2,1)S(1)}, bf16[256,688]{1,0:T(8,128)(2,1)S(1)}, u32[]{:S(2)}, u32[]{:S(2)}) %collective-permute-start.101) | collective-permute-done | bytes 352288 | tf_op jit(solution)/shard_map/layer0_backward/ppermute | solution.py:48
  652.9 2.8 collective-permute-start.110
  660.4 3.7 collective-permute-start.111
  695.6 16.6 %collective-permute-done.122 = bf16[256,864]{1,0:T(8,128)(2,1)S(1)} collective-permute-done((bf16[256,864]{1,0:T(8,128)(2,1)S(1)}, bf16[256,864]{1,0:T(8,128)(2,1)S(1)}, u32[]{:S(2)}, u32[]{:S(2)}) %collective-permute-start.122) | collective-permute-done | bytes 442400 | tf_op jit(solution)/shard_map/owners/ppermute | solution.py:48
  (909 shorter events, 305.9 us)
Async XLA Ops:
  7.2 86.7 %all-gather.6.cloned.1.call-start = ((), (), s32[]{:S(2)}) async-start(), calls=%async_computation.7 | async-start | bytes 3563520 | tf_op jit(solution)/shard_map/gather_weights/all_gather | solution.py:276
  14.4 19.1 %collective-permute-start.2 = (bf16[256,690]{0,1:T(8,128)(2,1)S(1)}, bf16[256,690]{0,1:T(8,128)(2,1)S(1)}, u32[]{:S(2)}, u32[]{:S(2)}) collective-permute-start(bf16[256,690]{0,1:T(8,128)(2,1)S(1)} %maximum_select_fusion.11), channel_id=1, source_target_pairs={{0,72},{8,64},{64,8},{72,0},{1,73},{9,65},{65,9},{73,1},{2,74},{10... | collective-permute-start | bytes 1059848 | tf_op jit(solution)/shard_map/weights_key_value/ppermute | solution.py:48
  17.3 16.2 %collective-permute-start.3 = (bf16[256,690]{0,1:T(8,128)(2,1)S(1)}, bf16[256,690]{0,1:T(8,128)(2,1)S(1)}, u32[]{:S(2)}, u32[]{:S(2)}) collective-permute-start(bf16[256,690]{0,1:T(8,128)(2,1)S(1)} %maximum_select_fusion.11), channel_id=1, source_target_pairs={{0,64},{64,0},{1,65},{65,1},{2,66},{66,2},{3,67},{67,3},{4,68},{68... | collective-permute-start | bytes 1059848 | tf_op jit(solution)/shard_map/weights_key_value/ppermute | solution.py:44
  17.6 16.4 %collective-permute-start.4 = (bf16[256,690]{0,1:T(8,128)(2,1)S(1)}, bf16[256,690]{0,1:T(8,128)(2,1)S(1)}, u32[]{:S(2)}, u32[]{:S(2)}) collective-permute-start(bf16[256,690]{0,1:T(8,128)(2,1)S(1)} %maximum_select_fusion.11), channel_id=1, source_target_pairs={{0,8},{8,0},{1,9},{9,1},{2,10},{10,2},{3,11},{11,3},{4,12},{12,4},... | collective-permute-start | bytes 1059848 | tf_op jit(solution)/shard_map/weights_key_value/ppermute | solution.py:44
  36.4 110.7 %all-gather.8.cloned.1.call-start = ((), (), s32[]{:S(2)}) async-start(), calls=%async_computation.8 | async-start | bytes 5734400 | tf_op jit(solution)/shard_map/gather_weights/all_gather | solution.py:276
  44.0 14.8 %collective-permute-start.6 = (bf16[256,1120]{0,1:T(8,128)(2,1)S(1)}, bf16[256,1120]{0,1:T(8,128)(2,1)S(1)}, u32[]{:S(2)}, u32[]{:S(2)}) collective-permute-start(bf16[256,1120]{0,1:T(8,128)(2,1)S(1)} %fusion.49), channel_id=1, source_target_pairs={{0,8},{8,0},{1,9},{9,1},{2,10},{10,2},{3,11},{11,3},{4,12},{12,4},... | collective-permute-start | bytes 1720328 | tf_op jit(solution)/shard_map/weights_query_gate_out/ppermute | solution.py:44
  47.3 26.0 %collective-permute-start.13 = (bf16[256,1120]{0,1:T(8,128)(2,1)S(1)}, bf16[256,1120]{0,1:T(8,128)(2,1)S(1)}, u32[]{:S(2)}, u32[]{:S(2)}) collective-permute-start(bf16[256,1120]{0,1:T(8,128)(2,1)S(1)} %fusion.49), channel_id=1, source_target_pairs={{0,64},{64,0},{1,65},{65,1},{2,66},{66,2},{3,67},{67,3},{4,68},{68... | collective-permute-start | bytes 1720328 | tf_op jit(solution)/shard_map/weights_query_gate_out/ppermute | solution.py:44
  49.9 27.5 %collective-permute-start.14 = (bf16[256,1120]{0,1:T(8,128)(2,1)S(1)}, bf16[256,1120]{0,1:T(8,128)(2,1)S(1)}, u32[]{:S(2)}, u32[]{:S(2)}) collective-permute-start(bf16[256,1120]{0,1:T(8,128)(2,1)S(1)} %fusion.49), channel_id=1, source_target_pairs={{0,72},{8,64},{64,8},{72,0},{1,73},{9,65},{65,9},{73,1},{2,74},{10... | collective-permute-start | bytes 1720328 | tf_op jit(solution)/shard_map/weights_query_gate_out/ppermute | solution.py:48
  83.1 111.7 %all-gather.10.cloned.1.call-start = ((), (), s32[]{:S(2)}) async-start(), calls=%async_computation.9 | async-start | bytes 6635520 | tf_op jit(solution)/shard_map/layer0_forward/weights_gate_up_down/all_gather | solution.py:276
  89.7 16.7 %collective-permute-start.28 = (bf16[256,1296]{0,1:T(8,128)(2,1)S(1)}, bf16[256,1296]{0,1:T(8,128)(2,1)}, u32[]{:S(2)}, u32[]{:S(2)}) collective-permute-start(bf16[256,1296]{0,1:T(8,128)(2,1)S(1)} %maximum_select_fusion.2), channel_id=1, source_target_pairs={{0,8},{8,0},{1,9},{9,1},{2,10},{10,2},{3,11},{11,3},{4,12},{12,4},... | collective-permute-start | bytes 1990664 | tf_op jit(solution)/shard_map/layer0_forward/weights_gate_up_down/ppermute | solution.py:44
  89.8 30.7 %collective-permute-start.29 = (bf16[256,1296]{0,1:T(8,128)(2,1)S(1)}, bf16[256,1296]{0,1:T(8,128)(2,1)}, u32[]{:S(2)}, u32[]{:S(2)}) collective-permute-start(bf16[256,1296]{0,1:T(8,128)(2,1)S(1)} %maximum_select_fusion.2), channel_id=1, source_target_pairs={{0,64},{64,0},{1,65},{65,1},{2,66},{66,2},{3,67},{67,3},{4,68},{68... | collective-permute-start | bytes 1990664 | tf_op jit(solution)/shard_map/layer0_forward/weights_gate_up_down/ppermute | solution.py:44
  91.0 31.4 %collective-permute-start.30 = (bf16[256,1296]{0,1:T(8,128)(2,1)S(1)}, bf16[256,1296]{0,1:T(8,128)(2,1)}, u32[]{:S(2)}, u32[]{:S(2)}) collective-permute-start(bf16[256,1296]{0,1:T(8,128)(2,1)S(1)} %maximum_select_fusion.2), channel_id=1, source_target_pairs={{0,72},{8,64},{64,8},{72,0},{1,73},{9,65},{65,9},{73,1},{2,74},{10... | collective-permute-start | bytes 1990664 | tf_op jit(solution)/shard_map/layer0_forward/weights_gate_up_down/ppermute | solution.py:48
  99.6 25.7 %collective-permute-start.15 = (bf16[256,432]{0,1:T(8,128)(2,1)S(1)}, bf16[256,432]{0,1:T(8,128)(2,1)S(1)}, u32[]{:S(2)}, u32[]{:S(2)}) collective-permute-start(bf16[256,432]{0,1:T(8,128)(2,1)S(1)} %convolution_convert_fusion.8), channel_id=1, source_target_pairs={{0,8},{8,0},{1,9},{9,1},{2,10},{10,2},{3,11},{11,3},{4,12},{12,4},... | collective-permute-start | bytes 663560 | tf_op jit(solution)/shard_map/layer0_forward/earlier_states/ppermute | solution.py:44
  129.3 142.5 %all-gather.12.cloned.1.call-start = ((), (), s32[]{:S(2)}) async-start(), calls=%async_computation.10 | async-start | bytes 9256960 | tf_op jit(solution)/shard_map/gather_weights/all_gather | solution.py:276
  131.9 231.6 %all-gather.14.cloned.1.call-start = ((), (), s32[]{:S(2)}) async-start(), calls=%async_computation.11 | async-start | bytes 6635520 | tf_op jit(solution)/shard_map/layer0_forward/weights_gate_up_down/all_gather | solution.py:276
  132.0 12.5 %collective-permute-start.18 = (bf16[256,432]{0,1:T(8,128)(2,1)S(1)}, bf16[256,432]{0,1:T(8,128)(2,1)S(1)}, u32[]{:S(2)}, u32[]{:S(2)}) collective-permute-start(bf16[256,432]{0,1:T(8,128)(2,1)S(1)} %fusion.77), channel_id=1, source_target_pairs={{0,48},{1,49},{2,50},{3,51},{4,52},{5,53},{6,54},{7,55},{8,56},{9,... | collective-permute-start | bytes 663560 | tf_op jit(solution)/shard_map/layer0_forward/earlier_states/ppermute | solution.py:58
  212.0 240.4 %reduce-scatter.8.cloned.1.call-start = ((), (), s32[]{:S(2)}) async-start(), calls=%async_computation.12 | async-start | bytes 2293760 | tf_op jit(solution)/shard_map/layer1_backward/reduce_scatter | solution.py:306
  226.5 130.7 %collective-permute-start.64 = (bf16[256,1024]{1,0:T(8,128)(2,1)}, bf16[256,1024]{1,0:T(8,128)(2,1)S(1)}, u32[]{:S(2)}, u32[]{:S(2)}) collective-permute-start(bf16[256,1024]{1,0:T(8,128)(2,1)} %pad_maximum_fusion.18), channel_id=1, source_target_pairs={{0,8},{8,0},{1,9},{9,1},{2,10},{10,2},{3,11},{11,3},{4,12},{12,4},... | collective-permute-start | bytes 1572872 | tf_op jit(solution)/shard_map/ppermute | solution.py:44
  231.9 40.0 %collective-permute-start.38 = (bf16[128,2048]{1,0:T(8,128)(2,1)S(1)}, bf16[128,2048]{1,0:T(8,128)(2,1)}, u32[]{:S(2)}, u32[]{:S(2)}) collective-permute-start(bf16[128,2048]{1,0:T(8,128)(2,1)S(1)} %pad_maximum_fusion.13), channel_id=1, source_target_pairs={{0,4},{4,0},{1,5},{5,1},{2,6},{6,2},{3,7},{7,3},{8,12},{12,8},{9,1... | collective-permute-start | bytes 1572872 | tf_op jit(solution)/shard_map/spread/ppermute | solution.py:44
  284.2 16.3 %collective-permute-start.42 = (bf16[256,432]{0,1:T(8,128)(2,1)S(1)}, bf16[256,432]{0,1:T(8,128)(2,1)S(1)}, u32[]{:S(2)}, u32[]{:S(2)}) collective-permute-start(bf16[256,432]{0,1:T(8,128)(2,1)S(1)} %fusion.79), channel_id=1, source_target_pairs={{0,48},{1,49},{2,50},{3,51},{4,52},{5,53},{6,54},{7,55},{8,56},{9,... | collective-permute-start | bytes 663560 | tf_op jit(solution)/shard_map/layer1_forward/earlier_states/ppermute | solution.py:58
  287.3 13.3 %collective-permute-start.41 = (bf16[256,432]{0,1:T(8,128)(2,1)S(1)}, bf16[256,432]{0,1:T(8,128)(2,1)S(1)}, u32[]{:S(2)}, u32[]{:S(2)}) collective-permute-start(bf16[256,432]{0,1:T(8,128)(2,1)S(1)} %fusion.79), channel_id=1, source_target_pairs={{0,32},{16,48},{1,33},{17,49},{2,34},{18,50},{3,35},{19,51},{4,36}... | collective-permute-start | bytes 663560 | tf_op jit(solution)/shard_map/layer1_forward/earlier_states/ppermute | solution.py:58
  289.1 18.7 %collective-permute-start.40 = (bf16[256,432]{0,1:T(8,128)(2,1)S(1)}, bf16[256,432]{0,1:T(8,128)(2,1)S(1)}, u32[]{:S(2)}, u32[]{:S(2)}) collective-permute-start(bf16[256,432]{0,1:T(8,128)(2,1)S(1)} %fusion.79), channel_id=1, source_target_pairs={{0,16},{16,32},{32,48},{1,17},{17,33},{33,49},{2,18},{18,34},{34,5... | collective-permute-start | bytes 663560 | tf_op jit(solution)/shard_map/layer1_forward/earlier_states/ppermute | solution.py:58
  316.2 42.8 %collective-permute-start.65 = (bf16[256,1024]{1,0:T(8,128)(2,1)S(1)}, bf16[256,1024]{1,0:T(8,128)(2,1)S(1)}, u32[]{:S(2)}, u32[]{:S(2)}) collective-permute-start(bf16[256,1024]{1,0:T(8,128)(2,1)S(1)} %pad_maximum_fusion.19), channel_id=1, source_target_pairs={{0,8},{8,0},{1,9},{9,1},{2,10},{10,2},{3,11},{11,3},{4,12},{12,4},... | collective-permute-start | bytes 1572872 | tf_op jit(solution)/shard_map/ppermute | solution.py:44
  340.3 9.9 %collective-permute-start.49 = (bf16[32,2048]{1,0:T(8,128)(2,1)S(1)}, bf16[32,2048]{1,0:T(8,128)(2,1)S(1)}, u32[]{:S(2)}, u32[]{:S(2)}) collective-permute-start(bf16[32,2048]{1,0:T(8,128)(2,1)S(1)} %broadcast_select_fusion.57), channel_id=1, source_target_pairs={{0,2},{1,3},{2,0},{3,1},{4,6},{5,7},{6,4},{7,5},{8,10},{9,11},{10,... | collective-permute-start | bytes 393224 | tf_op jit(solution)/shard_map/layer1_backward/spread/ppermute | solution.py:53
  340.6 20.8 %collective-permute-start.47 = (bf16[256,1024]{1,0:T(8,128)(2,1)S(1)}, bf16[256,1024]{1,0:T(8,128)(2,1)S(1)}, u32[]{:S(2)}, u32[]{:S(2)}) collective-permute-start(bf16[256,1024]{1,0:T(8,128)(2,1)S(1)} %pad_maximum_fusion.14), channel_id=1, source_target_pairs={{0,8},{8,0},{1,9},{9,1},{2,10},{10,2},{3,11},{11,3},{4,12},{12,4},... | collective-permute-start | bytes 1572872 | tf_op jit(solution)/shard_map/ppermute | solution.py:44
  349.0 14.5 %collective-permute-start.55 = (bf16[128,2048]{1,0:T(8,128)(2,1)}, bf16[128,2048]{1,0:T(8,128)(2,1)}, u32[]{:S(2)}, u32[]{:S(2)}) collective-permute-start(bf16[128,2048]{1,0:T(8,128)(2,1)} %pad_maximum_fusion.16), channel_id=1, source_target_pairs={{0,4},{4,0},{1,5},{5,1},{2,6},{6,2},{3,7},{7,3},{8,12},{12,8},{9,1... | collective-permute-start | bytes 1572872 | tf_op jit(solution)/shard_map/layer1_forward/spread/ppermute | solution.py:44
  356.2 10.9 %collective-permute-start.51 = (bf16[128,2048]{1,0:T(8,128)(2,1)}, bf16[128,2048]{1,0:T(8,128)(2,1)}, u32[]{:S(2)}, u32[]{:S(2)}) collective-permute-start(bf16[128,2048]{1,0:T(8,128)(2,1)} %pad_maximum_fusion.15), channel_id=1, source_target_pairs={{0,4},{4,0},{1,5},{5,1},{2,6},{6,2},{3,7},{7,3},{8,12},{12,8},{9,1... | collective-permute-start | bytes 1572872 | tf_op jit(solution)/shard_map/layer1_backward/spread/ppermute | solution.py:44
  371.5 27.3 %collective-permute-start.56 = (bf16[128,2048]{1,0:T(8,128)(2,1)}, bf16[128,2048]{1,0:T(8,128)(2,1)}, u32[]{:S(2)}, u32[]{:S(2)}) collective-permute-start(bf16[128,2048]{1,0:T(8,128)(2,1)} %slice.1289), channel_id=1, source_target_pairs={{0,4},{4,0},{1,5},{5,1},{2,6},{6,2},{3,7},{7,3},{8,12},{12,8},{9,1... | collective-permute-start | bytes 1572872 | tf_op jit(solution)/shard_map/layer1_backward/collect/ppermute | solution.py:44
  373.6 23.1 %collective-permute-start.70 = (bf16[256,1024]{1,0:T(8,128)(2,1)S(1)}, bf16[256,1024]{1,0:T(8,128)(2,1)S(1)}, u32[]{:S(2)}, u32[]{:S(2)}) collective-permute-start(bf16[256,1024]{1,0:T(8,128)(2,1)S(1)} %pad_maximum_fusion.20), channel_id=1, source_target_pairs={{0,8},{8,0},{1,9},{9,1},{2,10},{10,2},{3,11},{11,3},{4,12},{12,4},... | collective-permute-start | bytes 1572872 | tf_op jit(solution)/shard_map/ppermute | solution.py:44
  374.9 21.8 %collective-permute-start.71 = (bf16[256,864]{0,1:T(8,128)(2,1)S(1)}, bf16[256,864]{0,1:T(8,128)(2,1)S(1)}, u32[]{:S(2)}, u32[]{:S(2)}) collective-permute-start(bf16[256,864]{0,1:T(8,128)(2,1)S(1)} %pad_maximum_fusion.24), channel_id=1, source_target_pairs={{0,8},{8,0},{1,9},{9,1},{2,10},{10,2},{3,11},{11,3},{4,12},{12,4},... | collective-permute-start | bytes 1327112 | tf_op jit(solution)/shard_map/layer1_backward/ppermute | solution.py:44
  376.8 25.6 %collective-permute-start.66 = (bf16[128,2048]{1,0:T(8,128)(2,1)}, bf16[128,2048]{1,0:T(8,128)(2,1)}, u32[]{:S(2)}, u32[]{:S(2)}) collective-permute-start(bf16[128,2048]{1,0:T(8,128)(2,1)} %slice.1288), channel_id=1, source_target_pairs={{0,4},{4,0},{1,5},{5,1},{2,6},{6,2},{3,7},{7,3},{8,12},{12,8},{9,1... | collective-permute-start | bytes 1572872 | tf_op jit(solution)/shard_map/layer1_out/collect/ppermute | solution.py:44
  398.8 133.3 %reduce-scatter.10.cloned.1.call-start = ((), (), s32[]{:S(2)}) async-start(), calls=%async_computation.13 | async-start | bytes 4587520 | tf_op jit(solution)/shard_map/layer1_backward/reduce_scatter | solution.py:306
  401.7 9.9 %collective-permute-start.57 = (bf16[32,2048]{1,0:T(8,128)(2,1)S(1)}, bf16[32,2048]{1,0:T(8,128)(2,1)S(1)}, u32[]{:S(2)}, u32[]{:S(2)}) collective-permute-start(bf16[32,2048]{1,0:T(8,128)(2,1)S(1)} %get-tuple-element.138), channel_id=1, source_target_pairs={{0,1},{1,2},{2,3},{3,0},{4,5},{5,6},{6,7},{7,4},{8,9},{9,10},{10,1... | collective-permute-start | bytes 393224 | tf_op jit(solution)/shard_map/layer1_backward/collect/ppermute | solution.py:53
  434.6 100.2 %reduce-scatter.12.cloned.1.call-start = ((), (), s32[]{:S(2)}) async-start(), calls=%async_computation.14 | async-start | bytes 3604480 | tf_op jit(solution)/shard_map/layer1_backward/reduce_scatter | solution.py:306
  448.0 19.8 %collective-permute-start.75 = (bf16[256,432]{0,1:T(8,128)(2,1)S(1)}, bf16[256,432]{0,1:T(8,128)(2,1)}, u32[]{:S(2)}, u32[]{:S(2)}) collective-permute-start(bf16[256,432]{0,1:T(8,128)(2,1)S(1)} %fusion.81), channel_id=1, source_target_pairs={{48,0},{49,1},{50,2},{51,3},{52,4},{53,5},{54,6},{55,7},{56,8},{57... | collective-permute-start | bytes 663560 | tf_op jit(solution)/shard_map/layer1_backward/later_states/ppermute | solution.py:58
  449.4 18.4 %collective-permute-start.74 = (bf16[256,432]{0,1:T(8,128)(2,1)S(1)}, bf16[256,432]{0,1:T(8,128)(2,1)}, u32[]{:S(2)}, u32[]{:S(2)}) collective-permute-start(bf16[256,432]{0,1:T(8,128)(2,1)S(1)} %fusion.81), channel_id=1, source_target_pairs={{32,0},{48,16},{33,1},{49,17},{34,2},{50,18},{35,3},{51,19},{36,4}... | collective-permute-start | bytes 663560 | tf_op jit(solution)/shard_map/layer1_backward/later_states/ppermute | solution.py:58
  450.7 17.1 %collective-permute-start.73 = (bf16[256,432]{0,1:T(8,128)(2,1)S(1)}, bf16[256,432]{0,1:T(8,128)(2,1)}, u32[]{:S(2)}, u32[]{:S(2)}) collective-permute-start(bf16[256,432]{0,1:T(8,128)(2,1)S(1)} %fusion.81), channel_id=1, source_target_pairs={{16,0},{32,16},{48,32},{17,1},{33,17},{49,33},{18,2},{34,18},{50,3... | collective-permute-start | bytes 663560 | tf_op jit(solution)/shard_map/layer1_backward/later_states/ppermute | solution.py:58
  470.3 15.8 %collective-permute-start.80 = (bf16[256,1376]{0,1:T(8,128)(2,1)S(1)}, bf16[256,1376]{0,1:T(8,128)(2,1)S(1)}, u32[]{:S(2)}, u32[]{:S(2)}) collective-permute-start(bf16[256,1376]{0,1:T(8,128)(2,1)S(1)} %pad_maximum_fusion.10), channel_id=1, source_target_pairs={{0,8},{8,0},{1,9},{9,1},{2,10},{10,2},{3,11},{11,3},{4,12},{12,4},... | collective-permute-start | bytes 2113544 | tf_op jit(solution)/shard_map/layer1_backward/ppermute | solution.py:44
  477.0 11.9 %collective-permute-start.76 = (bf16[128,2048]{1,0:T(8,128)(2,1)}, bf16[128,2048]{1,0:T(8,128)(2,1)}, u32[]{:S(2)}, u32[]{:S(2)}) collective-permute-start(bf16[128,2048]{1,0:T(8,128)(2,1)} %slice.1287), channel_id=1, source_target_pairs={{0,4},{4,0},{1,5},{5,1},{2,6},{6,2},{3,7},{7,3},{8,12},{12,8},{9,1... | collective-permute-start | bytes 1572872 | tf_op jit(solution)/shard_map/layer1_backward/collect/ppermute | solution.py:44
  488.8 78.3 %reduce-scatter.14.cloned.1.call-start = ((), (), s32[]{:S(2)}) async-start(), calls=%async_computation.15 | async-start | bytes 2293760 | tf_op jit(solution)/shard_map/layer0_backward/reduce_scatter | solution.py:306
  518.1 11.8 %collective-permute-start.93 = (bf16[256,864]{0,1:T(8,128)(2,1)S(1)}, bf16[256,864]{0,1:T(8,128)(2,1)S(1)}, u32[]{:S(2)}, u32[]{:S(2)}) collective-permute-start(bf16[256,864]{0,1:T(8,128)(2,1)S(1)} %pad_maximum_fusion.25), channel_id=1, source_target_pairs={{0,8},{8,0},{1,9},{9,1},{2,10},{10,2},{3,11},{11,3},{4,12},{12,4},... | collective-permute-start | bytes 1327112 | tf_op jit(solution)/shard_map/layer0_backward/ppermute | solution.py:44
  521.1 16.2 %collective-permute-start.88 = (bf16[32,2048]{1,0:T(8,128)(2,1)}, bf16[32,2048]{1,0:T(8,128)(2,1)S(1)}, u32[]{:S(2)}, u32[]{:S(2)}) collective-permute-start(bf16[32,2048]{1,0:T(8,128)(2,1)} %get-tuple-element.133), channel_id=1, source_target_pairs={{0,3},{1,0},{2,1},{3,2},{4,7},{5,4},{6,5},{7,6},{8,11},{9,8},{10,9... | collective-permute-start | bytes 393224 | tf_op jit(solution)/shard_map/layer0_backward/collect/ppermute | solution.py:53
  523.4 13.9 %collective-permute-start.87 = (bf16[32,2048]{1,0:T(8,128)(2,1)S(1)}, bf16[32,2048]{1,0:T(8,128)(2,1)S(1)}, u32[]{:S(2)}, u32[]{:S(2)}) collective-permute-start(bf16[32,2048]{1,0:T(8,128)(2,1)S(1)} %get-tuple-element.134), channel_id=1, source_target_pairs={{0,2},{1,3},{2,0},{3,1},{4,6},{5,7},{6,4},{7,5},{8,10},{9,11},{10,... | collective-permute-start | bytes 393224 | tf_op jit(solution)/shard_map/layer0_backward/collect/ppermute | solution.py:53
  523.4 13.9 %collective-permute-start.86 = (bf16[32,2048]{1,0:T(8,128)(2,1)S(1)}, bf16[32,2048]{1,0:T(8,128)(2,1)S(1)}, u32[]{:S(2)}, u32[]{:S(2)}) collective-permute-start(bf16[32,2048]{1,0:T(8,128)(2,1)S(1)} %get-tuple-element.132), channel_id=1, source_target_pairs={{0,1},{1,2},{2,3},{3,0},{4,5},{5,6},{6,7},{7,4},{8,9},{9,10},{10,1... | collective-permute-start | bytes 393224 | tf_op jit(solution)/shard_map/layer0_backward/collect/ppermute | solution.py:53
  532.0 97.9 %reduce-scatter.16.cloned.1.call-start = ((), (), s32[]{:S(2)}) async-start(), calls=%async_computation.16 | async-start | bytes 1966080 | tf_op jit(solution)/shard_map/layer0_backward/reduce_scatter | solution.py:306
  554.7 9.6 %collective-permute-start.100 = (bf16[256,688]{0,1:T(8,128)(2,1)S(1)}, bf16[256,688]{0,1:T(8,128)(2,1)S(1)}, u32[]{:S(2)}, u32[]{:S(2)}) collective-permute-start(bf16[256,688]{0,1:T(8,128)(2,1)S(1)} %pad_maximum_fusion.27), channel_id=1, source_target_pairs={{0,8},{8,0},{1,9},{9,1},{2,10},{10,2},{3,11},{11,3},{4,12},{12,4},... | collective-permute-start | bytes 1056776 | tf_op jit(solution)/shard_map/layer0_backward/ppermute | solution.py:44
  556.3 14.5 %collective-permute-start.95 = (bf16[256,432]{0,1:T(8,128)(2,1)S(1)}, bf16[256,432]{0,1:T(8,128)(2,1)S(1)}, u32[]{:S(2)}, u32[]{:S(2)}) collective-permute-start(bf16[256,432]{0,1:T(8,128)(2,1)S(1)} %convolution_convert_fusion.5), channel_id=1, source_target_pairs={{0,8},{8,0},{1,9},{9,1},{2,10},{10,2},{3,11},{11,3},{4,12},{12,4},... | collective-permute-start | bytes 663560 | tf_op jit(solution)/shard_map/layer0_backward/later_states/ppermute | solution.py:44
  566.2 63.7 %reduce-scatter.18.cloned.1.call-start = ((), (), s32[]{:S(2)}) async-start(), calls=%async_computation.17 | async-start | bytes 1966080 | tf_op jit(solution)/shard_map/layer0_backward/reduce_scatter | solution.py:306
  567.2 13.4 %collective-permute-start.94 = (bf16[256,864]{1,0:T(8,128)(2,1)S(1)}, bf16[256,864]{1,0:T(8,128)(2,1)S(1)}, u32[]{:S(2)}, u32[]{:S(2)}) collective-permute-start(bf16[256,864]{1,0:T(8,128)(2,1)S(1)} %broadcast_select_fusion.21), channel_id=1, source_target_pairs={{0,72},{8,64},{64,8},{72,0},{1,73},{9,65},{65,9},{73,1},{2,74},{10... | collective-permute-start | bytes 1327112 | tf_op jit(solution)/shard_map/layer0_backward/ppermute | solution.py:48
  570.9 11.7 %collective-permute-start.98 = (bf16[256,432]{0,1:T(8,128)(2,1)S(1)}, bf16[256,432]{0,1:T(8,128)(2,1)S(1)}, u32[]{:S(2)}, u32[]{:S(2)}) collective-permute-start(bf16[256,432]{0,1:T(8,128)(2,1)S(1)} %fusion.83), channel_id=1, source_target_pairs={{48,0},{49,1},{50,2},{51,3},{52,4},{53,5},{54,6},{55,7},{56,8},{57... | collective-permute-start | bytes 663560 | tf_op jit(solution)/shard_map/layer0_backward/later_states/ppermute | solution.py:58
  572.3 12.2 %collective-permute-start.97 = (bf16[256,432]{0,1:T(8,128)(2,1)S(1)}, bf16[256,432]{0,1:T(8,128)(2,1)S(1)}, u32[]{:S(2)}, u32[]{:S(2)}) collective-permute-start(bf16[256,432]{0,1:T(8,128)(2,1)S(1)} %fusion.83), channel_id=1, source_target_pairs={{32,0},{48,16},{33,1},{49,17},{34,2},{50,18},{35,3},{51,19},{36,4}... | collective-permute-start | bytes 663560 | tf_op jit(solution)/shard_map/layer0_backward/later_states/ppermute | solution.py:58
  573.6 10.9 %collective-permute-start.96 = (bf16[256,432]{0,1:T(8,128)(2,1)S(1)}, bf16[256,432]{0,1:T(8,128)(2,1)S(1)}, u32[]{:S(2)}, u32[]{:S(2)}) collective-permute-start(bf16[256,432]{0,1:T(8,128)(2,1)S(1)} %fusion.83), channel_id=1, source_target_pairs={{16,0},{32,16},{48,32},{17,1},{33,17},{49,33},{18,2},{34,18},{50,3... | collective-permute-start | bytes 663560 | tf_op jit(solution)/shard_map/layer0_backward/later_states/ppermute | solution.py:58
  594.4 94.0 %reduce-scatter.20.cloned.1.call-start = ((), (), s32[]{:S(2)}) async-start(), calls=%async_computation.18 | async-start | bytes 4587520 | tf_op jit(solution)/shard_map/layer0_backward/reduce_scatter | solution.py:306
  597.7 11.1 %collective-permute-start.124 = (bf16[128,864]{1,0:T(8,128)(2,1)S(1)}, bf16[128,864]{1,0:T(8,128)(2,1)S(1)}, u32[]{:S(2)}, u32[]{:S(2)}) collective-permute-start(bf16[128,864]{1,0:T(8,128)(2,1)S(1)} %select_convert_fusion), channel_id=1, source_target_pairs={{0,4},{4,0},{1,5},{5,1},{2,6},{6,2},{3,7},{7,3},{8,12},{12,8},{9,1... | collective-permute-start | bytes 663560 | tf_op jit(solution)/shard_map/owners/ppermute | solution.py:44
  630.1 10.6 %collective-permute-start.107 = (bf16[256,688]{1,0:T(8,128)(2,1)S(1)}, bf16[256,688]{1,0:T(8,128)(2,1)S(1)}, u32[]{:S(2)}, u32[]{:S(2)}) collective-permute-start(bf16[256,688]{1,0:T(8,128)(2,1)S(1)} %get-tuple-element.127), channel_id=1, source_target_pairs={{0,72},{8,64},{64,8},{72,0},{1,73},{9,65},{65,9},{73,1},{2,74},{10... | collective-permute-start | bytes 1056776 | tf_op jit(solution)/shard_map/owners/ppermute | solution.py:48
  633.0 16.3 %collective-permute-start.101 = (bf16[256,688]{1,0:T(8,128)(2,1)S(1)}, bf16[256,688]{1,0:T(8,128)(2,1)S(1)}, u32[]{:S(2)}, u32[]{:S(2)}) collective-permute-start(bf16[256,688]{1,0:T(8,128)(2,1)S(1)} %get-tuple-element.128), channel_id=1, source_target_pairs={{0,72},{8,64},{64,8},{72,0},{1,73},{9,65},{65,9},{73,1},{2,74},{10... | collective-permute-start | bytes 1056776 | tf_op jit(solution)/shard_map/layer0_backward/ppermute | solution.py:48
  633.2 18.4 %collective-permute-start.105 = (bf16[32,2048]{1,0:T(8,128)(2,1)S(1)}, bf16[32,2048]{1,0:T(8,128)(2,1)S(1)}, u32[]{:S(2)}, u32[]{:S(2)}) collective-permute-start(bf16[32,2048]{1,0:T(8,128)(2,1)S(1)} %get-tuple-element.130), channel_id=1, source_target_pairs={{0,3},{1,0},{2,1},{3,2},{4,7},{5,4},{6,5},{7,6},{8,11},{9,8},{10,9... | collective-permute-start | bytes 393224 | tf_op jit(solution)/shard_map/layer0_backward/collect/ppermute | solution.py:53
  635.9 15.7 %collective-permute-start.104 = (bf16[32,2048]{1,0:T(8,128)(2,1)S(1)}, bf16[32,2048]{1,0:T(8,128)(2,1)S(1)}, u32[]{:S(2)}, u32[]{:S(2)}) collective-permute-start(bf16[32,2048]{1,0:T(8,128)(2,1)S(1)} %get-tuple-element.131), channel_id=1, source_target_pairs={{0,2},{1,3},{2,0},{3,1},{4,6},{5,7},{6,4},{7,5},{8,10},{9,11},{10,... | collective-permute-start | bytes 393224 | tf_op jit(solution)/shard_map/layer0_backward/collect/ppermute | solution.py:53
  636.3 15.3 %collective-permute-start.103 = (bf16[32,2048]{1,0:T(8,128)(2,1)S(1)}, bf16[32,2048]{1,0:T(8,128)(2,1)S(1)}, u32[]{:S(2)}, u32[]{:S(2)}) collective-permute-start(bf16[32,2048]{1,0:T(8,128)(2,1)S(1)} %get-tuple-element.129), channel_id=1, source_target_pairs={{0,1},{1,2},{2,3},{3,0},{4,5},{5,6},{6,7},{7,4},{8,9},{9,10},{10,1... | collective-permute-start | bytes 393224 | tf_op jit(solution)/shard_map/layer0_backward/collect/ppermute | solution.py:53
  673.9 9.5 %collective-permute-start.117 = (f32[4,2048]{1,0:T(4,128)S(1)}, f32[4,2048]{1,0:T(4,128)S(1)}, u32[]{:S(2)}, u32[]{:S(2)}) collective-permute-start(f32[4,2048]{1,0:T(4,128)S(1)} %add_add_fusion), channel_id=1, source_target_pairs={{0,64},{64,0},{1,65},{65,1},{2,66},{66,2},{3,67},{67,3},{4,68},{68... | collective-permute-start | bytes 98312 | tf_op jit(solution)/shard_map/owners/gains/ppermute | solution.py:44
  677.9 16.9 %collective-permute-start.106 = (f32[32,2048]{1,0:T(8,128)S(1)}, f32[32,2048]{1,0:T(8,128)S(1)}, u32[]{:S(2)}, u32[]{:S(2)}) collective-permute-start(f32[32,2048]{1,0:T(8,128)S(1)} %get-tuple-element.122), channel_id=1, source_target_pairs={{0,64},{64,0},{1,65},{65,1},{2,66},{66,2},{3,67},{67,3},{4,68},{68... | collective-permute-start | bytes 786440 | tf_op jit(solution)/shard_map/ppermute | solution.py:44
  689.8 22.5 %collective-permute-start.122 = (bf16[256,864]{1,0:T(8,128)(2,1)S(1)}, bf16[256,864]{1,0:T(8,128)(2,1)S(1)}, u32[]{:S(2)}, u32[]{:S(2)}) collective-permute-start(bf16[256,864]{1,0:T(8,128)(2,1)S(1)} %get-tuple-element.124), channel_id=1, source_target_pairs={{0,72},{8,64},{64,8},{72,0},{1,73},{9,65},{65,9},{73,1},{2,74},{10... | collective-permute-start | bytes 1327112 | tf_op jit(solution)/shard_map/owners/ppermute | solution.py:48
  690.6 21.6 %collective-permute-start.121 = (bf16[256,864]{1,0:T(8,128)(2,1)S(1)}, bf16[256,864]{1,0:T(8,128)(2,1)S(1)}, u32[]{:S(2)}, u32[]{:S(2)}) collective-permute-start(bf16[256,864]{1,0:T(8,128)(2,1)S(1)} %get-tuple-element.123), channel_id=1, source_target_pairs={{0,64},{64,0},{1,65},{65,1},{2,66},{66,2},{3,67},{67,3},{4,68},{68... | collective-permute-start | bytes 1327112 | tf_op jit(solution)/shard_map/owners/ppermute | solution.py:44
  693.3 19.0 %collective-permute-start.120 = (bf16[256,864]{1,0:T(8,128)(2,1)S(1)}, bf16[256,864]{1,0:T(8,128)(2,1)S(1)}, u32[]{:S(2)}, u32[]{:S(2)}) collective-permute-start(bf16[256,864]{1,0:T(8,128)(2,1)S(1)} %broadcast_select_fusion.20), channel_id=1, source_target_pairs={{0,8},{8,0},{1,9},{9,1},{2,10},{10,2},{3,11},{11,3},{4,12},{12,4},... | collective-permute-start | bytes 1327112 | tf_op jit(solution)/shard_map/owners/ppermute | solution.py:44
  (283 other events, 3046.8 us)
Sparse Core Ops, SparseCore 0:
  36.5 39.5 all-gather.5
  83.2 51.9 all-gather.7
  136.9 57.8 all-gather.9
  196.3 75.4 all-gather.11
  273.3 64.8 all-gather.13
  398.9 26.6 reduce-scatter.7
  434.7 51.1 reduce-scatter.9
  488.8 44.8 reduce-scatter.11
  536.1 30.8 reduce-scatter.13
  569.3 33.4 reduce-scatter.15
  605.2 23.8 reduce-scatter.17
  631.4 44.6 reduce-scatter.19

commit v4 on v3

--- a/solution.py
+++ b/solution.py
@@ -1,6 +1,7 @@
 import jax
 import jax.numpy as jnp
 from jax import lax
+from jax.experimental import pallas as pl
 from jax.experimental.layout import Layout, with_layout_constraint
 from jax.sharding import Mesh, PartitionSpec as P
 
@@ -148,7 +149,7 @@
     return v * jax.nn.sigmoid(v)
 
 
-def forward(h, a_rows, ffn_gain, weights, ctx, waits=()):
+def forward(h, a_rows, ffn_gain, weights, ctx, waits=((), ())):
     w_in, w_out, get_gud = weights
     K, V, F = ctx["sizes"]
     split = len(w_in) == 2
@@ -165,11 +166,11 @@
     retained = mm(scores, v) + mm(q, state_in) * ctx["from_start"]
     n = lax.rsqrt(jnp.mean(retained * retained, axis=-1, keepdims=True) + group_floor)
     gated = low(silu(ret_gate) * (retained * n))
-    mid = h + collect(mm_right(gated, w_out))
-    b_rows = spread(low(mid * rms_inverse(mid) * ffn_gain))
+    mid = hold(h + collect(mm_right(gated, w_out)), *waits[0])
+    b_rows = hold(spread(low(mid * rms_inverse(mid) * ffn_gain)), *waits[1])
     gu = mm(b_rows, w_gu)
     gate_pre, up_pre = gu[:, :F], gu[:, F:]
-    hidden = hold(low(silu(gate_pre) * up_pre), *waits)
+    hidden = low(silu(gate_pre) * up_pre)
     record = (a_rows, b_rows, gated, hidden, k, v, q, state_in, scores, ret_gate, retained, mid, gu)
     return record, (w_in, w_out, w_gu, w_down)
 
@@ -179,25 +180,27 @@
     return mid + collect(mm_right(hidden, weights[-1]))
 
 
-def backward(h, g_out, d_f_rows, record, pairs, gains, weights, ctx, waits):
-    a_pair, b_pair = pairs
+def backward(h, g_out, d_f, record, pairs, gains, weights, ctx, waits):
+    a_pair, b_pair, f_pair, gated_pair, hidden_pair = pairs
     w_in, w_out, w_gu, w_down = weights
     attn_gain, ffn_gain = gains
     K, V, F = ctx["sizes"]
     a_rows, b_rows, gated, hidden, k, v, q, state_in, scores, ret_gate, retained, mid, gu = record
-    d_f = spread(d_f_rows)
+    split = len(w_in) == 2
+    parts = {}
     d_hidden = mm(d_f, w_down)
     gate_pre, up_pre = gu[:, :F], gu[:, F:]
     s = jax.nn.sigmoid(gate_pre)
     d_gate = low(d_hidden * up_pre * s * (1.0 + gate_pre * (1.0 - s)))
     d_up = low(d_hidden * gate_pre * s)
     d_gu = jnp.concatenate([d_gate, d_up], axis=1)
-    d_b = collect(mm_right(d_gu, w_gu))
-    part_gu = settle(weight_grad(b_pair, d_gu))
-    d_b = hold(d_b, *waits[0])
+    gu_pair = with_partner(d_gu)
+    d_b = hold(collect(mm_right(d_gu, w_gu)), gu_pair[1], *waits[0](parts))
+    parts["gu"] = settle(weight_grad(b_pair, gu_pair))
     d_norm, grad_ffn_gain = norm_back(mid, ffn_gain, d_b)
     d_mid = g_out + d_norm
-    d_r = spread(low(d_mid))
+    d_r = hold(spread(low(d_mid)), *waits[1](parts))
+    r_pair = swap_half(d_r, ctx)
     d_gated = mm(d_r, w_out)
     s = jax.nn.sigmoid(ret_gate)
     n = lax.rsqrt(jnp.mean(retained * retained, axis=-1, keepdims=True) + group_floor)
@@ -209,31 +212,56 @@
     d_ret_low = low(d_ret)
     d_ret_start = low(d_ret * ctx["from_start"])
     beyond = low(later_states(mm_left(q, d_ret_start), ctx))
-    grad_od = [row_major(low(mm_left(left, right))) for left, right in ((d_r, gated), (d_f, hidden))]
-    part_od = settle(jnp.concatenate(grad_od, axis=1))
-    beyond = hold(beyond, *waits[1](part_gu))
     d_scores = low(mm_right(d_ret_low, v) * ctx["decay_mask"])
     d_q = low(mm(d_scores, k) + mm_right(d_ret_start, state_in))
     d_qg = jnp.concatenate([d_q, d_ret_gate], axis=1)
-    if len(w_in) == 2:
-        part_qg = settle(weight_grad(a_pair, d_qg))
+    grads = [weight_grad(r_pair, gated_pair), weight_grad(f_pair, hidden_pair)]
+    swapped = [r_pair[1]]
+    if split:
+        qg_pair = with_partner(d_qg)
+        swapped.append(qg_pair[1])
+        grads.append(weight_grad(a_pair, qg_pair))
+    grad_od = row_major(jnp.concatenate(grads, axis=1))
+    parts["od"] = settle(grad_od)
+    beyond = hold(beyond, *swapped, *waits[2](parts))
     d_k = low(mm_left(d_scores, q) + mm_right(v, beyond) * ctx["to_end"])
     d_v = low(mm_left(scores, d_ret_low) + mm(k, beyond) * ctx["to_end"])
     d_kv = jnp.concatenate([d_k, d_v], axis=1)
-    if len(w_in) == 2:
+    d_in = d_kv if split else jnp.concatenate([d_kv, d_qg], axis=1)
+    if split:
         d_kv_wide = jnp.pad(d_kv, ((0, 0), (0, w_in[0].shape[1] - d_kv.shape[1])))
-        d_a = collect(mm_right(d_qg, w_in[1]) + mm_right(d_kv_wide, w_in[0]))
-        grad_kv = weight_grad(a_pair, d_kv)
-        part_kv = settle(grad_kv)
-        d_a = hold(d_a, grad_kv, *waits[2](part_qg))
+        partial = mm_right(d_qg, w_in[1]) + mm_right(d_kv_wide, w_in[0])
     else:
-        d_in = jnp.concatenate([d_kv, d_qg], axis=1)
-        d_a = collect(mm_right(d_in, w_in[0]))
-        part_in = settle(weight_grad(a_pair, d_in))
-        part_kv, part_qg = part_in[:, : K + V], part_in[:, K + V :]
+        partial = mm_right(d_in, w_in[0])
+    in_pair = with_partner(d_in)
+    parts["in_partner"] = in_pair[1]
+    if split:
+        in_pair = in_pair[0], hold(in_pair[1], grad_od)
+    parts["grad_in"] = weight_grad(a_pair, in_pair)
+    parts["in"] = settle(parts["grad_in"])
+    d_a = hold(collect(partial), *waits[3](parts))
     d_norm, grad_attn_gain = norm_back(h, attn_gain, d_a)
-    parts = (part_kv, part_qg, part_od, part_gu)
     return d_mid + d_norm, parts, (grad_attn_gain, grad_ffn_gain)
+
+
+def with_partner(v):
+    return v, swap(v, "ylo")
+
+
+def swap_half(v, ctx):
+    n = lax.axis_size("x")
+    width = v.shape[1] // (2 * n)
+    cut = [v[:, i * width : (i + 1) * width] for i in range(2 * n)]
+
+    def half(which):
+        return jnp.concatenate([pick(which == 0, cut[2 * i], cut[2 * i + 1]) for i in range(n)], axis=1)
+
+    place = ctx["place"]
+    return half(place), swap(half(1 - place), "ylo")
+
+
+def weight_grad(left, right):
+    return row_major(low(mm_left(left[0], right[0]) + mm_left(left[1], right[1])))
 
 
 def halves(w, core):
@@ -242,27 +270,25 @@
     return pick(core == 0, first, second), pick(core == 0, second, first)
 
 
-def swap_half(v, ctx):
-    n = lax.axis_size("x")
-    width = v.shape[1] // (2 * n)
-    cut = [v[:, i * width : (i + 1) * width] for i in range(2 * n)]
-
-    def half(which):
-        return jnp.concatenate([pick(which == 0, cut[2 * i], cut[2 * i + 1]) for i in range(n)], axis=1)
-
-    place = ctx["place"]
-    return half(place), swap(half(1 - place), "ylo")
-
-
-def weight_grad(left, right):
-    return row_major(low(mm_left(left[0], right) + mm_left(left[1], swap(right, "ylo"))))
+def hold(v, *others):
+    if not others:
+        return v
+    anywhere = pl.BlockSpec(memory_space=pl.ANY)
+    return pl.pallas_call(
+        lambda *refs: None,
+        out_shape=jax.ShapeDtypeStruct(v.shape, v.dtype),
+        in_specs=[anywhere] * (1 + len(others)),
+        out_specs=anywhere,
+        input_output_aliases={0: 0},
+        cost_estimate=pl.CostEstimate(flops=0, bytes_accessed=0, transcendentals=0),
+    )(v, *others)
 
 
 def corner(v):
     return v[tuple(slice(n - 1, n) for n in v.shape)].reshape(1, 1)
 
 
-def hold(v, *others):
+def hold_by_corner(v, *others):
     if not others:
         return v
     corners = [corner(other) for other in others]
@@ -299,7 +325,7 @@
 
 def y_then_x(own, moved, ctx, ready=()):
     first, second = both_layers(own, moved, ctx)
-    return hold(jnp.concatenate(first), *ready), jnp.concatenate(second)
+    return hold_by_corner(jnp.concatenate(first), *ready), jnp.concatenate(second)
 
 
 def settle(grad):
@@ -376,7 +402,7 @@
     head = tensor * 2 + core
 
     def context(layer, docs, rates_ready=()):
-        rates = hold(pick(section == layer, decays_all, decays_far)[None], *rates_ready)[0]
+        rates = hold_by_corner(pick(section == layer, decays_all, decays_far)[None], *rates_ready)[0]
         rate = lax.dynamic_index_in_dim(rates, head, 0, False)
         gap = places[:, None] - places[None, :]
         allowed = (gap >= 0) & (docs[:, None] == docs[None, :])
@@ -405,9 +431,9 @@
         kv0, kv1 = y_then_x(own_kv, along_y(own_kv), ctx)
         kv0 = jnp.concatenate([kv0, kv1[:, K + V :]], axis=1)
     with jax.named_scope("weights_query_gate_out"):
-        own_qgo = hold(pack((w_query[0], w_gate_ret[0], w_out[0].T), ctx), kv0)
+        own_qgo = hold_by_corner(pack((w_query[0], w_gate_ret[0], w_out[0].T), ctx), kv0)
         moved_qgo = along_y(own_qgo)
-    h0_rows = wide(spread(hold(h0, moved_qgo[0])))
+    h0_rows = wide(spread(hold_by_corner(h0, moved_qgo[0])))
     ctx0 = context(0, docs)
     with jax.named_scope("weights_query_gate_out"):
         qgo0, qgo1 = y_then_x(own_qgo, moved_qgo, ctx, (h0_rows, ctx0["decay_mask"]))
@@ -438,37 +464,57 @@
     h1 = wide(low(out_first))
     a1 = spread(low(h1 * rms_inverse(h1) * gains1[0]))
     ctx1 = context(1, docs, (h1,))
-    pairs0 = swap_half(a0, ctx0), swap_half(record0[1], ctx0)
-    early = [pair[1] for pair in pairs0]
+    def early_pairs(record, ctx):
+        gated, hidden = record[2], record[3]
+        got = swap(jnp.concatenate([gated, hidden], axis=1), "ylo")
+        return (
+            swap_half(record[0], ctx),
+            swap_half(record[1], ctx),
+            (gated, got[:, :V]),
+            (hidden, got[:, V:]),
+            got,
+        )
+
+    a_pair0, b_pair0, gated_pair0, hidden_pair0, got0 = early_pairs(record0, ctx0)
+    d_f1 = spread(hold(g1, h1))
+    f_pair1 = swap_half(d_f1, ctx1)
+    a1 = hold(a1, a_pair0[1], b_pair0[1], got0, f_pair1[1])
+    a_pair1 = swap_half(a1, ctx1)
     with jax.named_scope("layer1_forward"):
-        record1, weights1 = forward(h1, a1, gains1[1], weights1, ctx1, early)
-    pairs1 = swap_half(a1, ctx1), swap_half(record1[1], ctx1)
+        waits = (a_pair1[1:], ())
+        record1, weights1 = forward(h1, a1, gains1[1], weights1, ctx1, waits)
+    a_pair1, b_pair1, gated_pair1, hidden_pair1, got1 = early_pairs(record1, ctx1)
 
     with jax.named_scope("layer1_out"):
         out_second = layer_out(record1, weights1)
     with jax.named_scope("layer1_backward"):
-        waits = (pairs1[0][1:], lambda part: (out_second, part))
+        waits = (
+            lambda parts: (),
+            lambda parts: b_pair1[1:],
+            lambda parts: (out_second,),
+            lambda parts: (got1, parts["gu"]),
+        )
+        pairs = a_pair1, b_pair1, f_pair1, gated_pair1, hidden_pair1
         d_h1, parts1, gain_grads1 = backward(
-            h1, wide(g1), hold(g1, h1), record1, pairs1, gains1, weights1, ctx1, waits
+            h1, wide(g1), d_f1, record1, pairs, gains1, weights1, ctx1, waits
         )
-    d_f0 = low(d_h1)
-    kv1, qg1, od1, gu1 = parts1
-    sums = {}
-
-    def sum_gu(part):
-        sums["gu"] = sum_across(part, gu1, ctx)
-        return (sums["gu"],)
-
-    def sum_qg(part):
-        sums["qg"] = sum_across(part, qg1, ctx)
-        return (sums["qg"],)
+    d_f0_rows = low(d_h1)
+    def last_in(parts):
+        return parts["in_partner"], parts["grad_in"]
 
     with jax.named_scope("layer0_backward"):
-        waits = ((od1, kv1), sum_gu, sum_qg)
+        d_f0 = spread(d_f0_rows)
+        f_pair0 = swap_half(d_f0, ctx0)
+        waits = (
+            lambda parts: (parts1["in_partner"],),
+            lambda parts: (f_pair0[1], parts1["od"]),
+            lambda parts: (parts1["in"],),
+            last_in,
+        )
+        pairs = a_pair0, b_pair0, f_pair0, gated_pair0, hidden_pair0
         d_h0, parts0, gain_grads0 = backward(
-            h0, wide(d_f0), d_f0, record0, pairs0, gains0, weights0, ctx0, waits
+            h0, wide(d_f0_rows), d_f0, record0, pairs, gains0, weights0, ctx0, waits
         )
-    kv0, qg0, od0, gu0 = parts0
     gain_grads = jnp.stack(gain_grads0 + gain_grads1)
 
     def reduce_gains(*moves):
@@ -476,19 +522,21 @@
             return gain_grads + sum(move(gain_grads) for move in moves)
 
     with jax.named_scope("owners"):
-        gain_grads = reduce_gains(*(lambda v, k=k: turn(v, "tensor", k) for k in (1, 2, 3)))
+        gu = sum_across(parts0["gu"], parts1["gu"], ctx)
+        gain_grads = hold(reduce_gains(*(lambda v, k=k: turn(v, "tensor", k) for k in (1, 2, 3))), gu)
         gain_grads = reduce_gains(lambda v: swap(v, "core"))
         gain_grads = reduce_gains(*(lambda v, k=k: turn(v, "x", k) for k in (1, 2, 3)))
-        kv = sum_across(kv0, kv1, ctx)
-        gain_grads = hold(reduce_gains(lambda v: swap(v, "ylo"), cross, lambda v: swap(v, "section")), kv)
-        od = sum_along_y(od0, od1, ctx)
-        kv, qg, od, gu = (share_out(total, ctx) for total in (kv, sums["qg"], od, sums["gu"]))
+        gain_grads = reduce_gains(lambda v: swap(v, "ylo"), cross, lambda v: swap(v, "section"))
+        odqg1 = jnp.concatenate([parts1["od"], parts1["in"][:, K + V :]], axis=1)
+        odqg = sum_across(parts0["od"], odqg1, ctx)
+        kv = sum_across(parts0["in"], parts1["in"][:, : K + V], ctx)
+        kv, odqg, gu = (share_out(total, ctx) for total in (kv, odqg, gu))
     grad_key = both(kv, 0, K, ctx)
     grad_value = both(kv, K, K + V, ctx)
-    grad_query = both(qg, 0, K, ctx)
-    grad_gate_ret = both(qg, K, K + V, ctx)
-    grad_out = both(od, 0, V, ctx).T
-    grad_down = both(od, V, V + F, ctx).T
+    grad_out = both(odqg, 0, V, ctx).T
+    grad_down = both(odqg, V, V + F, ctx).T
+    grad_query = both(odqg, V + F, V + F + K, ctx)
+    grad_gate_ret = both(odqg, V + F + K, V + F + K + V, ctx)
     grad_gate = both(gu, 0, F, ctx)
     grad_up = both(gu, F, 2 * F, ctx)
 

time: 736 us -> 716 us (0.973)
  waiting for transfers between devices: 319 us -> 248 us
  other arithmetic: 71.2 us -> 110 us
  matrix products: 75.4 us -> 100 us
  between operations: 44 us -> 29.1 us
    all_gather x5, waiting for transfers between devices: 44.5 us -> 0.08 us  [gather_x(): return lax.all_gather(rows, 'x', axis=0, tiled=True)]
    ppermute x8 -> x7, waiting for transfers between devices: 55.7 us -> 37.7 us  [cross(): return lax.ppermute(v, ('section', 'ylo'), [(0, 3), (1, 2), (2, 1), (3, 0)])]
    dot_general x22 -> x26, matrix products: 23.4 us -> 41 us  [mm_left(): lax.dot_general(a, b, (((0,), (0,)), ((), ())), preferred_element_type=f32)]
    concatenate x0 -> x3, local copies, waits for them, and re-layouts: none -> 9.48 us  [the longest x1 7 us: backward(): grad_od = row_major(jnp.concatenate(grads, axis=1))]
    slice x17 -> x6, local copies, waits for them, and re-layouts: 12.9 us -> 3.59 us  [corner(): return v[tuple((slice(n - 1, n) for n in v.shape))].reshape(1, 1)]
    concatenate x3 -> x7, other arithmetic: 2.4 us -> 9.94 us  [spread_rows(): return row_major(jnp.concatenate([own, row_major(swap(own, 'core'))]))]
    ppermute x54, waiting for transfers between devices: 87.4 us -> 79.9 us  [turn(): return lax.ppermute(v, axis, [(i, (i + by) % n) for i in range(n)])]
    select_n x30 -> x33, other arithmetic: 13.1 us -> 20.2 us  [pick(): return jnp.where(flag, a, b)]
  transfers between devices with their start and end apart: 137 -> 138, of which waited for: 71 -> 70; matrix products, arithmetic and copies ran while one was open for 23% -> 33% of each run, Pallas kernels for 0% -> 0%
where the time goes in v4:
time: 716 us; the launch traced here: 705 us
  waiting for transfers between devices  248 us (35%)
  starting transfers between devices  175 us (24%)
  other arithmetic  110 us (15%)
  matrix products  100 us (14%)
  local copies, waits for them, and re-layouts  42.1 us (6%)
  between operations  29.1 us (4%)
    ppermute x54, waiting for transfers between devices, swap(): return lax.ppermute(v, axis, [(0, 1), (1, 0)])  90.1 us
    ppermute x54, waiting for transfers between devices, turn(): return lax.ppermute(v, axis, [(i, (i + by) % n) for i in range(n)])  79.9 us
    ppermute x54, starting transfers between devices, swap(): return lax.ppermute(v, axis, [(0, 1), (1, 0)])  77.9 us
    ppermute x54, starting transfers between devices, turn(): return lax.ppermute(v, axis, [(i, (i + by) % n) for i in range(n)])  59.7 us
    dot_general x26, matrix products, mm_left(): lax.dot_general(a, b, (((0,), (0,)), ((), ())), preferred_element_type=f32)  41 us
    ppermute x12, waiting for transfers between devices, shift(): lax.ppermute(v, axis, [(i, i + by) for i in range(n) if 0 <= i + by < n])  39.7 us
    ppermute x7, waiting for transfers between devices, cross(): return lax.ppermute(v, ('section', 'ylo'), [(0, 3), (1, 2), (2, 1), (3, 0)])  37.7 us
    dot_general x17, matrix products, mm(): lax.dot_general(a, b, (((1,), (0,)), ((), ())), preferred_element_type=f32)  32.4 us
  transfers between devices with their start and end apart: 138, of which 70 were waited for; matrix products, arithmetic and copies ran while one was open for 33% of the time, Pallas kernels for 0%

profile of v4, /device:TPU:1, one launch (start us, length us, event | category | flops | bytes accessed | tf_op | source)
XLA Modules:
  0.0 704.8 jit_solution(17632870918376801782)
XLA Ops:
  13.5 2.9 collective-permute-start.2
  17.7 2.8 collective-permute-start
  21.3 11.0 %collective-permute-done.2 = bf16[256,690]{0,1:T(8,128)(2,1)S(1)} collective-permute-done((bf16[256,690]{0,1:T(8,128)(2,1)S(1)}, bf16[256,690]{0,1:T(8,128)(2,1)S(1)}, u32[]{:S(2)}, u32[]{:S(2)}) %collective-permute-start.2) | collective-permute-done | bytes 353312 | tf_op jit(solution)/shard_map/weights_key_value/ppermute | solution.py:49
  37.4 3.0 collective-permute-start.12
  49.7 8.6 %collective-permute-done.6 = bf16[256,1120]{0,1:T(8,128)(2,1)S(1)} collective-permute-done((bf16[256,1120]{0,1:T(8,128)(2,1)S(1)}, bf16[256,1120]{0,1:T(8,128)(2,1)S(1)}, u32[]{:S(2)}, u32[]{:S(2)}) %collective-permute-start.6) | collective-permute-done | bytes 573472 | tf_op jit(solution)/shard_map/weights_query_gate_out/ppermute | solution.py:45
  62.1 3.3 collective-permute-start.8
  90.1 3.1 collective-permute-start.29
  97.0 2.8 convolution_convert_fusion
  100.7 5.9 collective-permute-done.28
  106.7 15.9 %collective-permute-done.29 = bf16[256,1296]{0,1:T(8,128)(2,1)} collective-permute-done((bf16[256,1296]{0,1:T(8,128)(2,1)S(1)}, bf16[256,1296]{0,1:T(8,128)(2,1)}, u32[]{:S(2)}, u32[]{:S(2)}) %collective-permute-start.29) | collective-permute-done | bytes 663584 | tf_op jit(solution)/shard_map/layer0_forward/weights_gate_up_down/ppermute | solution.py:45
  124.5 2.8 broadcast_select_fusion.6
  133.9 4.4 collective-permute-start.18
  142.1 4.2 collective-permute-done.18
  148.8 3.1 fusion.16
  160.0 4.4 collective-permute-start.19
  166.1 5.6 collective-permute-start.22
  172.4 5.0 collective-permute-done.22
  177.7 3.3 collective-permute-done.20
  184.9 6.2 collective-permute-done.25
  197.9 3.5 fusion.12
  212.2 3.1 collective-permute-done.33
  215.3 3.4 collective-permute-done.32
  223.1 5.5 collective-permute-done.44
  232.2 3.4 collective-permute-start.36
  253.5 9.8 %collective-permute-done.41.refs_3_ = bf16[256,864]{1,0:T(8,128)(2,1)S(1)} collective-permute-done((bf16[256,864]{1,0:T(8,128)(2,1)}, bf16[256,864]{1,0:T(8,128)(2,1)S(1)}, u32[]{:S(2)}, u32[]{:S(2)}) %collective-permute-start.41) | collective-permute-done | bytes 442400 | tf_op jit(solution)/shard_map/ppermute | solution.py:45
  263.4 11.2 %collective-permute-done.46.refs_4_ = bf16[256,1024]{1,0:T(8,128)(2,1)} collective-permute-done((bf16[256,1024]{1,0:T(8,128)(2,1)}, bf16[256,1024]{1,0:T(8,128)(2,1)}, u32[]{:S(2)}, u32[]{:S(2)}) %collective-permute-start.46) | collective-permute-done | bytes 524320 | tf_op jit(solution)/shard_map/ppermute | solution.py:45
  274.7 4.8 fusion.249
  281.5 3.8 collective-permute-done.47
  292.0 9.2 %collective-permute-done.50 = bf16[256,432]{0,1:T(8,128)(2,1)S(1)} collective-permute-done((bf16[256,432]{0,1:T(8,128)(2,1)S(1)}, bf16[256,432]{0,1:T(8,128)(2,1)S(1)}, u32[]{:S(2)}, u32[]{:S(2)}) %collective-permute-start.50) | collective-permute-done | bytes 221216 | tf_op jit(solution)/shard_map/layer1_forward/earlier_states/ppermute | solution.py:59
  301.2 7.1 %collective-permute-done.48 = bf16[256,432]{0,1:T(8,128)(2,1)S(1)} collective-permute-done((bf16[256,432]{0,1:T(8,128)(2,1)S(1)}, bf16[256,432]{0,1:T(8,128)(2,1)S(1)}, u32[]{:S(2)}, u32[]{:S(2)}) %collective-permute-start.48) | collective-permute-done | bytes 221216 | tf_op jit(solution)/shard_map/layer1_forward/earlier_states/ppermute | solution.py:59
  312.1 3.3 collective-permute-start.51
  323.3 3.5 collective-permute-done.52
  327.6 5.1 collective-permute-done.55.refs_1_
  336.8 3.6 collective-permute-start.57
  345.8 3.3 collective-permute-start.59
  350.8 3.8 fusion.8
  379.8 3.3 collective-permute-done.77
  394.6 4.6 collective-permute-start.68
  401.9 3.1 add_convert_fusion.2
  415.0 2.9 collective-permute-start.70
  419.8 3.9 collective-permute-done.70
  428.7 12.2 %collective-permute-done.73 = bf16[256,432]{0,1:T(8,128)(2,1)S(1)} collective-permute-done((bf16[256,432]{0,1:T(8,128)(2,1)S(1)}, bf16[256,432]{0,1:T(8,128)(2,1)S(1)}, u32[]{:S(2)}, u32[]{:S(2)}) %collective-permute-start.73) | collective-permute-done | bytes 221216 | tf_op jit(solution)/shard_map/layer1_backward/later_states/ppermute | solution.py:59
  448.4 4.4 fusion
  461.8 2.7 collective-permute-start.82
  470.5 4.0 collective-permute-done.80
  484.1 4.0 collective-permute-done.86
  498.7 3.2 fusion.10
  514.0 3.4 collective-permute-done.89
  525.8 4.5 collective-permute-done.96
  533.0 3.3 add_convert_fusion.1
  536.4 2.8 add_convert_fusion.5
  558.4 4.3 collective-permute-done.104.refs_2_
  564.5 5.8 collective-permute-done.102
  571.3 2.7 collective-permute-done.103.refs_1_
  581.9 7.0 concatenate.458.refs_1_
  592.5 3.0 add_convert_fusion.3.refs_2_
  595.6 3.0 fusion.14
  608.9 2.9 collective-permute-start.114
  614.1 3.3 collective-permute-done.106
  626.9 4.2 collective-permute-done.110
  657.0 4.6 collective-permute-done.124
  661.8 4.1 collective-permute-start.125
  667.6 3.1 collective-permute-start.122
  672.7 16.4 %collective-permute-done.122 = bf16[256,1552]{0,1:T(8,128)(2,1)} collective-permute-done((bf16[256,1552]{0,1:T(8,128)(2,1)}, bf16[256,1552]{0,1:T(8,128)(2,1)}, u32[]{:S(2)}, u32[]{:S(2)}) %collective-permute-start.122) | collective-permute-done | bytes 794656 | tf_op jit(solution)/shard_map/owners/ppermute | solution.py:49
  (870 shorter events, 363.6 us)
Async XLA Ops:
  7.2 87.0 %all-gather.6.cloned.1.call-start = ((), (), s32[]{:S(2)}) async-start(), calls=%async_computation.6 | async-start | bytes 3563520 | tf_op jit(solution)/shard_map/gather_weights/all_gather | solution.py:302
  13.5 18.8 %collective-permute-start.2 = (bf16[256,690]{0,1:T(8,128)(2,1)S(1)}, bf16[256,690]{0,1:T(8,128)(2,1)S(1)}, u32[]{:S(2)}, u32[]{:S(2)}) collective-permute-start(bf16[256,690]{0,1:T(8,128)(2,1)S(1)} %maximum_select_fusion.11), channel_id=1, source_target_pairs={{0,72},{8,64},{64,8},{72,0},{1,73},{9,65},{65,9},{73,1},{2,74},{10... | collective-permute-start | bytes 1059848 | tf_op jit(solution)/shard_map/weights_key_value/ppermute | solution.py:49
  16.4 15.9 %collective-permute-start.3 = (bf16[256,690]{0,1:T(8,128)(2,1)S(1)}, bf16[256,690]{0,1:T(8,128)(2,1)S(1)}, u32[]{:S(2)}, u32[]{:S(2)}) collective-permute-start(bf16[256,690]{0,1:T(8,128)(2,1)S(1)} %maximum_select_fusion.11), channel_id=1, source_target_pairs={{0,64},{64,0},{1,65},{65,1},{2,66},{66,2},{3,67},{67,3},{4,68},{68... | collective-permute-start | bytes 1059848 | tf_op jit(solution)/shard_map/weights_key_value/ppermute | solution.py:45
  16.7 16.0 %collective-permute-start.4 = (bf16[256,690]{0,1:T(8,128)(2,1)S(1)}, bf16[256,690]{0,1:T(8,128)(2,1)S(1)}, u32[]{:S(2)}, u32[]{:S(2)}) collective-permute-start(bf16[256,690]{0,1:T(8,128)(2,1)S(1)} %maximum_select_fusion.11), channel_id=1, source_target_pairs={{0,8},{8,0},{1,9},{9,1},{2,10},{10,2},{3,11},{11,3},{4,12},{12,4},... | collective-permute-start | bytes 1059848 | tf_op jit(solution)/shard_map/weights_key_value/ppermute | solution.py:45
  17.7 27.9 %collective-permute-start = (bf16[32,2048]{1,0:T(8,128)(2,1)}, bf16[32,2048]{1,0:T(8,128)(2,1)S(1)}, u32[]{:S(2)}, u32[]{:S(2)}) collective-permute-start(bf16[32,2048]{1,0:T(8,128)(2,1)} %select_bitcast_fusion.1), channel_id=1, source_target_pairs={{0,64},{64,0},{1,65},{65,1},{2,66},{66,2},{3,67},{67,3},{4,68},{68... | collective-permute-start | bytes 393224 | tf_op jit(solution)/shard_map/ppermute | solution.py:45
  35.1 113.7 %all-gather.8.cloned.1.call-start = ((), (), s32[]{:S(2)}) async-start(), calls=%async_computation.7 | async-start | bytes 5734400 | tf_op jit(solution)/shard_map/gather_weights/all_gather | solution.py:302
  43.7 14.6 %collective-permute-start.6 = (bf16[256,1120]{0,1:T(8,128)(2,1)S(1)}, bf16[256,1120]{0,1:T(8,128)(2,1)S(1)}, u32[]{:S(2)}, u32[]{:S(2)}) collective-permute-start(bf16[256,1120]{0,1:T(8,128)(2,1)S(1)} %fusion.56), channel_id=1, source_target_pairs={{0,8},{8,0},{1,9},{9,1},{2,10},{10,2},{3,11},{11,3},{4,12},{12,4},... | collective-permute-start | bytes 1720328 | tf_op jit(solution)/shard_map/weights_query_gate_out/ppermute | solution.py:45
  46.3 26.5 %collective-permute-start.13 = (bf16[256,1120]{0,1:T(8,128)(2,1)S(1)}, bf16[256,1120]{0,1:T(8,128)(2,1)S(1)}, u32[]{:S(2)}, u32[]{:S(2)}) collective-permute-start(bf16[256,1120]{0,1:T(8,128)(2,1)S(1)} %fusion.56), channel_id=1, source_target_pairs={{0,64},{64,0},{1,65},{65,1},{2,66},{66,2},{3,67},{67,3},{4,68},{68... | collective-permute-start | bytes 1720328 | tf_op jit(solution)/shard_map/weights_query_gate_out/ppermute | solution.py:45
  47.8 27.4 %collective-permute-start.14 = (bf16[256,1120]{0,1:T(8,128)(2,1)S(1)}, bf16[256,1120]{0,1:T(8,128)(2,1)S(1)}, u32[]{:S(2)}, u32[]{:S(2)}) collective-permute-start(bf16[256,1120]{0,1:T(8,128)(2,1)S(1)} %fusion.56), channel_id=1, source_target_pairs={{0,72},{8,64},{64,8},{72,0},{1,73},{9,65},{65,9},{73,1},{2,74},{10... | collective-permute-start | bytes 1720328 | tf_op jit(solution)/shard_map/weights_query_gate_out/ppermute | solution.py:49
  81.1 116.8 %all-gather.10.cloned.1.call-start = ((), (), s32[]{:S(2)}) async-start(), calls=%async_computation.8 | async-start | bytes 6635520 | tf_op jit(solution)/shard_map/layer0_forward/weights_gate_up_down/all_gather | solution.py:302
  90.0 16.7 %collective-permute-start.28 = (bf16[256,1296]{0,1:T(8,128)(2,1)S(1)}, bf16[256,1296]{0,1:T(8,128)(2,1)}, u32[]{:S(2)}, u32[]{:S(2)}) collective-permute-start(bf16[256,1296]{0,1:T(8,128)(2,1)S(1)} %maximum_select_fusion.2), channel_id=1, source_target_pairs={{0,8},{8,0},{1,9},{9,1},{2,10},{10,2},{3,11},{11,3},{4,12},{12,4},... | collective-permute-start | bytes 1990664 | tf_op jit(solution)/shard_map/layer0_forward/weights_gate_up_down/ppermute | solution.py:45
  90.1 32.5 %collective-permute-start.29 = (bf16[256,1296]{0,1:T(8,128)(2,1)S(1)}, bf16[256,1296]{0,1:T(8,128)(2,1)}, u32[]{:S(2)}, u32[]{:S(2)}) collective-permute-start(bf16[256,1296]{0,1:T(8,128)(2,1)S(1)} %maximum_select_fusion.2), channel_id=1, source_target_pairs={{0,64},{64,0},{1,65},{65,1},{2,66},{66,2},{3,67},{67,3},{4,68},{68... | collective-permute-start | bytes 1990664 | tf_op jit(solution)/shard_map/layer0_forward/weights_gate_up_down/ppermute | solution.py:45
  93.1 31.4 %collective-permute-start.30 = (bf16[256,1296]{0,1:T(8,128)(2,1)S(1)}, bf16[256,1296]{0,1:T(8,128)(2,1)}, u32[]{:S(2)}, u32[]{:S(2)}) collective-permute-start(bf16[256,1296]{0,1:T(8,128)(2,1)S(1)} %maximum_select_fusion.2), channel_id=1, source_target_pairs={{0,72},{8,64},{64,8},{72,0},{1,73},{9,65},{65,9},{73,1},{2,74},{10... | collective-permute-start | bytes 1990664 | tf_op jit(solution)/shard_map/layer0_forward/weights_gate_up_down/ppermute | solution.py:49
  100.2 27.1 %collective-permute-start.15 = (bf16[256,432]{0,1:T(8,128)(2,1)S(1)}, bf16[256,432]{0,1:T(8,128)(2,1)S(1)}, u32[]{:S(2)}, u32[]{:S(2)}) collective-permute-start(bf16[256,432]{0,1:T(8,128)(2,1)S(1)} %convolution_convert_fusion.4), channel_id=1, source_target_pairs={{0,8},{8,0},{1,9},{9,1},{2,10},{10,2},{3,11},{11,3},{4,12},{12,4},... | collective-permute-start | bytes 663560 | tf_op jit(solution)/shard_map/layer0_forward/earlier_states/ppermute | solution.py:45
  131.4 143.3 %all-gather.12.cloned.1.call-start = ((), (), s32[]{:S(2)}) async-start(), calls=%async_computation.9 | async-start | bytes 9256960 | tf_op jit(solution)/shard_map/gather_weights/all_gather | solution.py:302
  133.9 215.3 %all-gather.14.cloned.1.call-start = ((), (), s32[]{:S(2)}) async-start(), calls=%async_computation.10 | async-start | bytes 6635520 | tf_op jit(solution)/shard_map/layer0_forward/weights_gate_up_down/all_gather | solution.py:302
  133.9 12.5 %collective-permute-start.18 = (bf16[256,432]{0,1:T(8,128)(2,1)S(1)}, bf16[256,432]{0,1:T(8,128)(2,1)S(1)}, u32[]{:S(2)}, u32[]{:S(2)}) collective-permute-start(bf16[256,432]{0,1:T(8,128)(2,1)S(1)} %fusion.116), channel_id=1, source_target_pairs={{0,48},{1,49},{2,50},{3,51},{4,52},{5,53},{6,54},{7,55},{8,56},{9,... | collective-permute-start | bytes 663560 | tf_op jit(solution)/shard_map/layer0_forward/earlier_states/ppermute | solution.py:59
  166.1 11.2 %collective-permute-start.22 = (bf16[32,2048]{1,0:T(8,128)(2,1)S(1)}, bf16[32,2048]{1,0:T(8,128)(2,1)S(1)}, u32[]{:S(2)}, u32[]{:S(2)}) collective-permute-start(bf16[32,2048]{1,0:T(8,128)(2,1)S(1)} %get-tuple-element.195), channel_id=1, source_target_pairs={{0,3},{1,0},{2,1},{3,2},{4,7},{5,4},{6,5},{7,6},{8,11},{9,8},{10,9... | collective-permute-start | bytes 393224 | tf_op jit(solution)/shard_map/layer0_forward/collect/ppermute | solution.py:54
  171.7 9.2 %collective-permute-start.20 = (bf16[32,2048]{1,0:T(8,128)(2,1)S(1)}, bf16[32,2048]{1,0:T(8,128)(2,1)S(1)}, u32[]{:S(2)}, u32[]{:S(2)}) collective-permute-start(bf16[32,2048]{1,0:T(8,128)(2,1)S(1)} %get-tuple-element.194), channel_id=1, source_target_pairs={{0,1},{1,2},{2,3},{3,0},{4,5},{5,6},{6,7},{7,4},{8,9},{9,10},{10,1... | collective-permute-start | bytes 393224 | tf_op jit(solution)/shard_map/layer0_forward/collect/ppermute | solution.py:54
  197.8 278.6 %reduce-scatter.7.cloned.1.call-start = ((), (), s32[]{:S(2)}) async-start(), calls=%async_computation.11 | async-start | bytes 2293760 | tf_op jit(solution)/shard_map/layer1_backward/reduce_scatter | solution.py:332
  205.9 45.1 %collective-permute-start.39 = (bf16[256,1024]{1,0:T(8,128)(2,1)}, bf16[256,1024]{1,0:T(8,128)(2,1)S(1)}, u32[]{:S(2)}, u32[]{:S(2)}) collective-permute-start(bf16[256,1024]{1,0:T(8,128)(2,1)} %pad_maximum_fusion.13), channel_id=1, source_target_pairs={{0,8},{8,0},{1,9},{9,1},{2,10},{10,2},{3,11},{11,3},{4,12},{12,4},... | collective-permute-start | bytes 1572872 | tf_op jit(solution)/shard_map/ppermute | solution.py:45
  209.5 9.2 %collective-permute-start.32 = (bf16[32,2048]{1,0:T(8,128)(2,1)S(1)}, bf16[32,2048]{1,0:T(8,128)(2,1)S(1)}, u32[]{:S(2)}, u32[]{:S(2)}) collective-permute-start(bf16[32,2048]{1,0:T(8,128)(2,1)S(1)} %get-tuple-element.191), channel_id=1, source_target_pairs={{0,1},{1,2},{2,3},{3,0},{4,5},{5,6},{6,7},{7,4},{8,9},{9,10},{10,1... | collective-permute-start | bytes 393224 | tf_op jit(solution)/shard_map/layer0_forward/collect/ppermute | solution.py:54
  219.5 9.1 %collective-permute-start.44 = (bf16[32,2048]{1,0:T(8,128)(2,1)}, bf16[32,2048]{1,0:T(8,128)(2,1)S(1)}, u32[]{:S(2)}, u32[]{:S(2)}) collective-permute-start(bf16[32,2048]{1,0:T(8,128)(2,1)} %shard_map.212), channel_id=1, source_target_pairs={{0,1},{1,2},{2,3},{3,0},{4,5},{5,6},{6,7},{7,4},{8,9},{9,10},{10,1... | collective-permute-start | bytes 393224 | tf_op jit(solution)/shard_map/spread/ppermute | solution.py:54
  219.5 9.1 %collective-permute-start.43 = (bf16[32,2048]{1,0:T(8,128)(2,1)}, bf16[32,2048]{1,0:T(8,128)(2,1)S(1)}, u32[]{:S(2)}, u32[]{:S(2)}) collective-permute-start(bf16[32,2048]{1,0:T(8,128)(2,1)} %shard_map.212), channel_id=1, source_target_pairs={{0,2},{1,3},{2,0},{3,1},{4,6},{5,7},{6,4},{7,5},{8,10},{9,11},{10,... | collective-permute-start | bytes 393224 | tf_op jit(solution)/shard_map/spread/ppermute | solution.py:54
  229.7 15.8 %collective-permute-start.45 = (bf16[128,2048]{1,0:T(8,128)(2,1)S(1)}, bf16[128,2048]{1,0:T(8,128)(2,1)S(1)}, u32[]{:S(2)}, u32[]{:S(2)}) collective-permute-start(bf16[128,2048]{1,0:T(8,128)(2,1)S(1)} %pad_maximum_fusion.15), channel_id=1, source_target_pairs={{0,4},{4,0},{1,5},{5,1},{2,6},{6,2},{3,7},{7,3},{8,12},{12,8},{9,1... | collective-permute-start | bytes 1572872 | tf_op jit(solution)/shard_map/spread/ppermute | solution.py:45
  232.2 9.9 %collective-permute-start.36 = (bf16[32,2048]{1,0:T(8,128)(2,1)S(1)}, bf16[32,2048]{1,0:T(8,128)(2,1)S(1)}, u32[]{:S(2)}, u32[]{:S(2)}) collective-permute-start(bf16[32,2048]{1,0:T(8,128)(2,1)S(1)} %fusion.126), channel_id=1, source_target_pairs={{0,2},{1,3},{2,0},{3,1},{4,6},{5,7},{6,4},{7,5},{8,10},{9,11},{10,... | collective-permute-start | bytes 393224 | tf_op jit(solution)/shard_map/spread/ppermute | solution.py:54
  240.3 13.3 %collective-permute-start.40 = (bf16[256,1024]{1,0:T(8,128)(2,1)}, bf16[256,1024]{1,0:T(8,128)(2,1)}, u32[]{:S(2)}, u32[]{:S(2)}) collective-permute-start(bf16[256,1024]{1,0:T(8,128)(2,1)} %pad_maximum_fusion.14), channel_id=1, source_target_pairs={{0,8},{8,0},{1,9},{9,1},{2,10},{10,2},{3,11},{11,3},{4,12},{12,4},... | collective-permute-start | bytes 1572872 | tf_op jit(solution)/shard_map/ppermute | solution.py:45
  242.1 21.3 %collective-permute-start.41 = (bf16[256,864]{1,0:T(8,128)(2,1)}, bf16[256,864]{1,0:T(8,128)(2,1)S(1)}, u32[]{:S(2)}, u32[]{:S(2)}) collective-permute-start(bf16[256,864]{1,0:T(8,128)(2,1)} %pad_maximum_fusion.27), channel_id=1, source_target_pairs={{0,8},{8,0},{1,9},{9,1},{2,10},{10,2},{3,11},{11,3},{4,12},{12,4},... | collective-permute-start | bytes 1327112 | tf_op jit(solution)/shard_map/ppermute | solution.py:45
  247.4 27.2 %collective-permute-start.46 = (bf16[256,1024]{1,0:T(8,128)(2,1)}, bf16[256,1024]{1,0:T(8,128)(2,1)}, u32[]{:S(2)}, u32[]{:S(2)}) collective-permute-start(bf16[256,1024]{1,0:T(8,128)(2,1)} %pad_maximum_fusion.16), channel_id=1, source_target_pairs={{0,8},{8,0},{1,9},{9,1},{2,10},{10,2},{3,11},{11,3},{4,12},{12,4},... | collective-permute-start | bytes 1572872 | tf_op jit(solution)/shard_map/ppermute | solution.py:45
  285.4 15.8 %collective-permute-start.50 = (bf16[256,432]{0,1:T(8,128)(2,1)S(1)}, bf16[256,432]{0,1:T(8,128)(2,1)S(1)}, u32[]{:S(2)}, u32[]{:S(2)}) collective-permute-start(bf16[256,432]{0,1:T(8,128)(2,1)S(1)} %fusion.118), channel_id=1, source_target_pairs={{0,48},{1,49},{2,50},{3,51},{4,52},{5,53},{6,54},{7,55},{8,56},{9,... | collective-permute-start | bytes 663560 | tf_op jit(solution)/shard_map/layer1_forward/earlier_states/ppermute | solution.py:59
  288.0 13.2 %collective-permute-start.49 = (bf16[256,432]{0,1:T(8,128)(2,1)S(1)}, bf16[256,432]{0,1:T(8,128)(2,1)S(1)}, u32[]{:S(2)}, u32[]{:S(2)}) collective-permute-start(bf16[256,432]{0,1:T(8,128)(2,1)S(1)} %fusion.118), channel_id=1, source_target_pairs={{0,32},{16,48},{1,33},{17,49},{2,34},{18,50},{3,35},{19,51},{4,36}... | collective-permute-start | bytes 663560 | tf_op jit(solution)/shard_map/layer1_forward/earlier_states/ppermute | solution.py:59
  289.8 18.5 %collective-permute-start.48 = (bf16[256,432]{0,1:T(8,128)(2,1)S(1)}, bf16[256,432]{0,1:T(8,128)(2,1)S(1)}, u32[]{:S(2)}, u32[]{:S(2)}) collective-permute-start(bf16[256,432]{0,1:T(8,128)(2,1)S(1)} %fusion.118), channel_id=1, source_target_pairs={{0,16},{16,32},{32,48},{1,17},{17,33},{33,49},{2,18},{18,34},{34,5... | collective-permute-start | bytes 663560 | tf_op jit(solution)/shard_map/layer1_forward/earlier_states/ppermute | solution.py:59
  320.0 12.7 %collective-permute-start.55 = (bf16[256,1024]{1,0:T(8,128)(2,1)S(1)}, bf16[256,1024]{1,0:T(8,128)(2,1)S(1)}, u32[]{:S(2)}, u32[]{:S(2)}) collective-permute-start(bf16[256,1024]{1,0:T(8,128)(2,1)S(1)} %pad_maximum_fusion.17), channel_id=1, source_target_pairs={{0,8},{8,0},{1,9},{9,1},{2,10},{10,2},{3,11},{11,3},{4,12},{12,4},... | collective-permute-start | bytes 1572872 | tf_op jit(solution)/shard_map/ppermute | solution.py:45
  355.6 22.5 %collective-permute-start.64 = (bf16[256,864]{1,0:T(8,128)(2,1)S(1)}, bf16[256,864]{1,0:T(8,128)(2,1)}, u32[]{:S(2)}, u32[]{:S(2)}) collective-permute-start(bf16[256,864]{1,0:T(8,128)(2,1)S(1)} %pad_maximum_fusion.28), channel_id=1, source_target_pairs={{0,8},{8,0},{1,9},{9,1},{2,10},{10,2},{3,11},{11,3},{4,12},{12,4},... | collective-permute-start | bytes 1327112 | tf_op jit(solution)/shard_map/layer1_backward/ppermute | solution.py:45
  362.1 39.8 %collective-permute-start.69 = (bf16[256,1024]{1,0:T(8,128)(2,1)}, bf16[256,1024]{1,0:T(8,128)(2,1)}, u32[]{:S(2)}, u32[]{:S(2)}) collective-permute-start(bf16[256,1024]{1,0:T(8,128)(2,1)} %pad_maximum_fusion.20), channel_id=1, source_target_pairs={{0,8},{8,0},{1,9},{9,1},{2,10},{10,2},{3,11},{11,3},{4,12},{12,4},... | collective-permute-start | bytes 1572872 | tf_op jit(solution)/shard_map/ppermute | solution.py:45
  368.0 9.3 %collective-permute-start.61 = (bf16[32,2048]{1,0:T(8,128)(2,1)S(1)}, bf16[32,2048]{1,0:T(8,128)(2,1)S(1)}, u32[]{:S(2)}, u32[]{:S(2)}) collective-permute-start(bf16[32,2048]{1,0:T(8,128)(2,1)S(1)} %get-tuple-element.182), channel_id=1, source_target_pairs={{0,1},{1,2},{2,3},{3,0},{4,5},{5,6},{6,7},{7,4},{8,9},{9,10},{10,1... | collective-permute-start | bytes 393224 | tf_op jit(solution)/shard_map/layer1_backward/collect/ppermute | solution.py:54
  370.4 28.9 %collective-permute-start.83 = (bf16[256,864]{1,0:T(8,128)(2,1)}, bf16[256,864]{1,0:T(8,128)(2,1)}, u32[]{:S(2)}, u32[]{:S(2)}) collective-permute-start(bf16[256,864]{1,0:T(8,128)(2,1)} %pad_maximum_fusion.29), channel_id=1, source_target_pairs={{0,8},{8,0},{1,9},{9,1},{2,10},{10,2},{3,11},{11,3},{4,12},{12,4},... | collective-permute-start | bytes 1327112 | tf_op jit(solution)/shard_map/ppermute | solution.py:45
  394.6 10.9 %collective-permute-start.68 = (bf16[128,2048]{1,0:T(8,128)(2,1)}, bf16[128,2048]{1,0:T(8,128)(2,1)}, u32[]{:S(2)}, u32[]{:S(2)}) collective-permute-start(bf16[128,2048]{1,0:T(8,128)(2,1)} %pad_maximum_fusion.19), channel_id=1, source_target_pairs={{0,4},{4,0},{1,5},{5,1},{2,6},{6,2},{3,7},{7,3},{8,12},{12,8},{9,1... | collective-permute-start | bytes 1572872 | tf_op jit(solution)/shard_map/layer1_backward/spread/ppermute | solution.py:45
  405.1 136.3 %reduce-scatter.9.cloned.1.call-start = ((), (), s32[]{:S(2)}) async-start(), calls=%async_computation.12 | async-start | bytes 2293760 | tf_op jit(solution)/shard_map/layer1_backward/reduce_scatter | solution.py:332
  418.8 24.7 %collective-permute-start.74 = (bf16[256,1024]{1,0:T(8,128)(2,1)}, bf16[256,1024]{1,0:T(8,128)(2,1)S(1)}, u32[]{:S(2)}, u32[]{:S(2)}) collective-permute-start(bf16[256,1024]{1,0:T(8,128)(2,1)} %pad_maximum_fusion.21), channel_id=1, source_target_pairs={{0,8},{8,0},{1,9},{9,1},{2,10},{10,2},{3,11},{11,3},{4,12},{12,4},... | collective-permute-start | bytes 1572872 | tf_op jit(solution)/shard_map/layer1_backward/ppermute | solution.py:45
  423.8 17.0 %collective-permute-start.73 = (bf16[256,432]{0,1:T(8,128)(2,1)S(1)}, bf16[256,432]{0,1:T(8,128)(2,1)S(1)}, u32[]{:S(2)}, u32[]{:S(2)}) collective-permute-start(bf16[256,432]{0,1:T(8,128)(2,1)S(1)} %fusion.120), channel_id=1, source_target_pairs={{48,0},{49,1},{50,2},{51,3},{52,4},{53,5},{54,6},{55,7},{56,8},{57... | collective-permute-start | bytes 663560 | tf_op jit(solution)/shard_map/layer1_backward/later_states/ppermute | solution.py:59
  425.1 15.7 %collective-permute-start.72 = (bf16[256,432]{0,1:T(8,128)(2,1)S(1)}, bf16[256,432]{0,1:T(8,128)(2,1)S(1)}, u32[]{:S(2)}, u32[]{:S(2)}) collective-permute-start(bf16[256,432]{0,1:T(8,128)(2,1)S(1)} %fusion.120), channel_id=1, source_target_pairs={{32,0},{48,16},{33,1},{49,17},{34,2},{50,18},{35,3},{51,19},{36,4}... | collective-permute-start | bytes 663560 | tf_op jit(solution)/shard_map/layer1_backward/later_states/ppermute | solution.py:59
  426.4 14.4 %collective-permute-start.71 = (bf16[256,432]{0,1:T(8,128)(2,1)S(1)}, bf16[256,432]{0,1:T(8,128)(2,1)S(1)}, u32[]{:S(2)}, u32[]{:S(2)}) collective-permute-start(bf16[256,432]{0,1:T(8,128)(2,1)S(1)} %fusion.120), channel_id=1, source_target_pairs={{16,0},{32,16},{48,32},{17,1},{33,17},{49,33},{18,2},{34,18},{50,3... | collective-permute-start | bytes 663560 | tf_op jit(solution)/shard_map/layer1_backward/later_states/ppermute | solution.py:59
  458.5 115.6 %reduce-scatter.11.cloned.1.call-start = ((), (), s32[]{:S(2)}) async-start(), calls=%async_computation.13 | async-start | bytes 3604480 | tf_op jit(solution)/shard_map/layer1_backward/reduce_scatter | solution.py:332
  464.9 9.7 %collective-permute-start.80 = (bf16[32,2048]{1,0:T(8,128)(2,1)}, bf16[32,2048]{1,0:T(8,128)(2,1)}, u32[]{:S(2)}, u32[]{:S(2)}) collective-permute-start(bf16[32,2048]{1,0:T(8,128)(2,1)} %get-tuple-element.179), channel_id=1, source_target_pairs={{0,1},{1,2},{2,3},{3,0},{4,5},{5,6},{6,7},{7,4},{8,9},{9,10},{10,1... | collective-permute-start | bytes 393224 | tf_op jit(solution)/shard_map/layer1_backward/collect/ppermute | solution.py:54
  466.7 24.1 %collective-permute-start.93 = (bf16[256,1376]{0,1:T(8,128)(2,1)}, bf16[256,1376]{0,1:T(8,128)(2,1)S(1)}, u32[]{:S(2)}, u32[]{:S(2)}) collective-permute-start(bf16[256,1376]{0,1:T(8,128)(2,1)} %copy.157), channel_id=1, source_target_pairs={{0,8},{8,0},{1,9},{9,1},{2,10},{10,2},{3,11},{11,3},{4,12},{12,4},... | collective-permute-start | bytes 2113544 | tf_op jit(solution)/shard_map/layer1_backward/ppermute | solution.py:45
  479.2 9.0 %collective-permute-start.86 = (bf16[32,2048]{1,0:T(8,128)(2,1)S(1)}, bf16[32,2048]{1,0:T(8,128)(2,1)S(1)}, u32[]{:S(2)}, u32[]{:S(2)}) collective-permute-start(bf16[32,2048]{1,0:T(8,128)(2,1)S(1)} %fusion.132), channel_id=1, source_target_pairs={{0,1},{1,2},{2,3},{3,0},{4,5},{5,6},{6,7},{7,4},{8,9},{9,10},{10,1... | collective-permute-start | bytes 393224 | tf_op jit(solution)/shard_map/layer0_backward/spread/ppermute | solution.py:54
  493.5 115.3 %reduce-scatter.13.cloned.1.call-start = ((), (), s32[]{:S(2)}) async-start(), calls=%async_computation.14 | async-start | bytes 2293760 | tf_op jit(solution)/shard_map/layer0_backward/reduce_scatter | solution.py:332
  497.5 20.6 %collective-permute-start.92 = (bf16[256,864]{1,0:T(8,128)(2,1)S(1)}, bf16[256,864]{1,0:T(8,128)(2,1)}, u32[]{:S(2)}, u32[]{:S(2)}) collective-permute-start(bf16[256,864]{1,0:T(8,128)(2,1)S(1)} %pad_maximum_fusion.30), channel_id=1, source_target_pairs={{0,8},{8,0},{1,9},{9,1},{2,10},{10,2},{3,11},{11,3},{4,12},{12,4},... | collective-permute-start | bytes 1327112 | tf_op jit(solution)/shard_map/layer0_backward/ppermute | solution.py:45
  505.3 31.1 %collective-permute-start.98 = (bf16[256,1024]{1,0:T(8,128)(2,1)}, bf16[256,1024]{1,0:T(8,128)(2,1)}, u32[]{:S(2)}, u32[]{:S(2)}) collective-permute-start(bf16[256,1024]{1,0:T(8,128)(2,1)} %pad_maximum_fusion.24), channel_id=1, source_target_pairs={{0,8},{8,0},{1,9},{9,1},{2,10},{10,2},{3,11},{11,3},{4,12},{12,4},... | collective-permute-start | bytes 1572872 | tf_op jit(solution)/shard_map/layer0_backward/ppermute | solution.py:45
  508.1 9.2 %collective-permute-start.89 = (bf16[32,2048]{1,0:T(8,128)(2,1)S(1)}, bf16[32,2048]{1,0:T(8,128)(2,1)S(1)}, u32[]{:S(2)}, u32[]{:S(2)}) collective-permute-start(bf16[32,2048]{1,0:T(8,128)(2,1)S(1)} %get-tuple-element.176), channel_id=1, source_target_pairs={{0,1},{1,2},{2,3},{3,0},{4,5},{5,6},{6,7},{7,4},{8,9},{9,10},{10,1... | collective-permute-start | bytes 393224 | tf_op jit(solution)/shard_map/layer0_backward/collect/ppermute | solution.py:54
  536.3 115.4 %reduce-scatter.17.cloned.1.call-start = ((), (), s32[]{:S(2)}) async-start(), calls=%async_computation.16 | async-start | bytes 1966080 | tf_op jit(solution)/shard_map/layer0_backward/reduce_scatter | solution.py:332
  548.3 14.4 %collective-permute-start.104 = (bf16[256,688]{1,0:T(8,128)(2,1)S(1)}, bf16[256,688]{1,0:T(8,128)(2,1)S(1)}, u32[]{:S(2)}, u32[]{:S(2)}) collective-permute-start(bf16[256,688]{1,0:T(8,128)(2,1)S(1)} %pad_maximum_fusion.31), channel_id=1, source_target_pairs={{0,8},{8,0},{1,9},{9,1},{2,10},{10,2},{3,11},{11,3},{4,12},{12,4},... | collective-permute-start | bytes 1056776 | tf_op jit(solution)/shard_map/layer0_backward/ppermute | solution.py:45
  550.7 23.3 %collective-permute-start.103 = (bf16[256,1024]{1,0:T(8,128)(2,1)}, bf16[256,1024]{1,0:T(8,128)(2,1)}, u32[]{:S(2)}, u32[]{:S(2)}) collective-permute-start(bf16[256,1024]{1,0:T(8,128)(2,1)} %pad_maximum_fusion.25), channel_id=1, source_target_pairs={{0,8},{8,0},{1,9},{9,1},{2,10},{10,2},{3,11},{11,3},{4,12},{12,4},... | collective-permute-start | bytes 1572872 | tf_op jit(solution)/shard_map/layer0_backward/ppermute | solution.py:45
  554.5 15.8 %collective-permute-start.102 = (bf16[256,432]{0,1:T(8,128)(2,1)S(1)}, bf16[256,432]{0,1:T(8,128)(2,1)S(1)}, u32[]{:S(2)}, u32[]{:S(2)}) collective-permute-start(bf16[256,432]{0,1:T(8,128)(2,1)S(1)} %fusion.122), channel_id=1, source_target_pairs={{48,0},{49,1},{50,2},{51,3},{52,4},{53,5},{54,6},{55,7},{56,8},{57... | collective-permute-start | bytes 663560 | tf_op jit(solution)/shard_map/layer0_backward/later_states/ppermute | solution.py:59
  555.8 14.5 %collective-permute-start.101 = (bf16[256,432]{0,1:T(8,128)(2,1)S(1)}, bf16[256,432]{0,1:T(8,128)(2,1)S(1)}, u32[]{:S(2)}, u32[]{:S(2)}) collective-permute-start(bf16[256,432]{0,1:T(8,128)(2,1)S(1)} %fusion.122), channel_id=1, source_target_pairs={{32,0},{48,16},{33,1},{49,17},{34,2},{50,18},{35,3},{51,19},{36,4}... | collective-permute-start | bytes 663560 | tf_op jit(solution)/shard_map/layer0_backward/later_states/ppermute | solution.py:59
  557.1 13.2 %collective-permute-start.100 = (bf16[256,432]{0,1:T(8,128)(2,1)S(1)}, bf16[256,432]{0,1:T(8,128)(2,1)S(1)}, u32[]{:S(2)}, u32[]{:S(2)}) collective-permute-start(bf16[256,432]{0,1:T(8,128)(2,1)S(1)} %fusion.122), channel_id=1, source_target_pairs={{16,0},{32,16},{48,32},{17,1},{33,17},{49,33},{18,2},{34,18},{50,3... | collective-permute-start | bytes 663560 | tf_op jit(solution)/shard_map/layer0_backward/later_states/ppermute | solution.py:59
  578.2 12.5 %collective-permute-start.109 = (bf16[256,688]{1,0:T(8,128)(2,1)}, bf16[256,688]{1,0:T(8,128)(2,1)}, u32[]{:S(2)}, u32[]{:S(2)}) collective-permute-start(bf16[256,688]{1,0:T(8,128)(2,1)} %pad_maximum_fusion.32), channel_id=1, source_target_pairs={{0,8},{8,0},{1,9},{9,1},{2,10},{10,2},{3,11},{11,3},{4,12},{12,4},... | collective-permute-start | bytes 1056776 | tf_op jit(solution)/shard_map/layer0_backward/ppermute | solution.py:45
  595.5 70.4 %reduce-scatter.15.cloned.1.call-start = ((), (), s32[]{:S(2)}) async-start(), calls=%async_computation.15 | async-start | bytes 4259840 | tf_op jit(solution)/shard_map/layer0_backward/reduce_scatter | solution.py:332
  608.1 9.2 %collective-permute-start.106 = (bf16[32,2048]{1,0:T(8,128)(2,1)S(1)}, bf16[32,2048]{1,0:T(8,128)(2,1)S(1)}, u32[]{:S(2)}, u32[]{:S(2)}) collective-permute-start(bf16[32,2048]{1,0:T(8,128)(2,1)S(1)} %get-tuple-element.173), channel_id=1, source_target_pairs={{0,1},{1,2},{2,3},{3,0},{4,5},{5,6},{6,7},{7,4},{8,9},{9,10},{10,1... | collective-permute-start | bytes 393224 | tf_op jit(solution)/shard_map/layer0_backward/collect/ppermute | solution.py:54
  608.9 22.9 %collective-permute-start.114 = (bf16[256,864]{1,0:T(8,128)(2,1)S(1)}, bf16[256,864]{1,0:T(8,128)(2,1)S(1)}, u32[]{:S(2)}, u32[]{:S(2)}) collective-permute-start(bf16[256,864]{1,0:T(8,128)(2,1)S(1)} %broadcast_select_fusion.17), channel_id=1, source_target_pairs={{0,72},{8,64},{64,8},{72,0},{1,73},{9,65},{65,9},{73,1},{2,74},{10... | collective-permute-start | bytes 1327112 | tf_op jit(solution)/shard_map/owners/ppermute | solution.py:49
  640.4 11.2 %collective-permute-start.126 = (bf16[128,864]{1,0:T(8,128)(2,1)S(1)}, bf16[128,864]{1,0:T(8,128)(2,1)S(1)}, u32[]{:S(2)}, u32[]{:S(2)}) collective-permute-start(bf16[128,864]{1,0:T(8,128)(2,1)S(1)} %select_convert_fusion.1), channel_id=1, source_target_pairs={{0,4},{4,0},{1,5},{5,1},{2,6},{6,2},{3,7},{7,3},{8,12},{12,8},{9,1... | collective-permute-start | bytes 663560 | tf_op jit(solution)/shard_map/owners/ppermute | solution.py:45
  652.6 9.0 %collective-permute-start.124 = (bf16[256,688]{1,0:T(8,128)(2,1)}, bf16[256,688]{1,0:T(8,128)(2,1)S(1)}, u32[]{:S(2)}, u32[]{:S(2)}) collective-permute-start(bf16[256,688]{1,0:T(8,128)(2,1)} %get-tuple-element.171), channel_id=1, source_target_pairs={{0,72},{8,64},{64,8},{72,0},{1,73},{9,65},{65,9},{73,1},{2,74},{10... | collective-permute-start | bytes 1056776 | tf_op jit(solution)/shard_map/owners/ppermute | solution.py:49
  667.6 21.5 %collective-permute-start.122 = (bf16[256,1552]{0,1:T(8,128)(2,1)}, bf16[256,1552]{0,1:T(8,128)(2,1)}, u32[]{:S(2)}, u32[]{:S(2)}) collective-permute-start(bf16[256,1552]{0,1:T(8,128)(2,1)} %copy.169), channel_id=1, source_target_pairs={{0,72},{8,64},{64,8},{72,0},{1,73},{9,65},{65,9},{73,1},{2,74},{10... | collective-permute-start | bytes 2383880 | tf_op jit(solution)/shard_map/owners/ppermute | solution.py:49
  (249 other events, 2238.3 us)
Sparse Core Ops, SparseCore 0:
  35.2 40.8 all-gather.5
  81.2 53.6 all-gather.7
  136.5 57.8 all-gather.9
  196.0 75.4 all-gather.11
  273.0 64.8 all-gather.13
  405.2 33.4 reduce-scatter.6
  458.6 27.1 reduce-scatter.8
  493.6 34.4 reduce-scatter.10
  536.4 26.0 reduce-scatter.12
  595.6 23.6 reduce-scatter.16
  621.7 42.5 reduce-scatter.14

commit v5 on v4

--- a/solution.py
+++ b/solution.py
@@ -478,10 +478,10 @@
     a_pair0, b_pair0, gated_pair0, hidden_pair0, got0 = early_pairs(record0, ctx0)
     d_f1 = spread(hold(g1, h1))
     f_pair1 = swap_half(d_f1, ctx1)
-    a1 = hold(a1, a_pair0[1], b_pair0[1], got0, f_pair1[1])
+    a1 = hold(a1, a_pair0[1], b_pair0[1], f_pair1[1])
     a_pair1 = swap_half(a1, ctx1)
     with jax.named_scope("layer1_forward"):
-        waits = (a_pair1[1:], ())
+        waits = (a_pair1[1:], (got0,))
         record1, weights1 = forward(h1, a1, gains1[1], weights1, ctx1, waits)
     a_pair1, b_pair1, gated_pair1, hidden_pair1, got1 = early_pairs(record1, ctx1)
 

time: 716 us -> 724 us (1.011)
  waiting for transfers between devices: 248 us -> 258 us
    all_gather x5, waiting for transfers between devices: 0.08 us -> 11.5 us  [gather_x(): return lax.all_gather(rows, 'x', axis=0, tiled=True)]
    unnamed x361 -> x423, local copies, waits for them, and re-layouts: 16.3 us -> 19.4 us
  transfers between devices with their start and end apart: 138 -> 138, of which waited for: 70 -> 73; matrix products, arithmetic and copies ran while one was open for 33% -> 31% of each run, Pallas kernels for 0% -> 0%
where the time goes in v5:
time: 724 us; the launch traced here: 713 us
  waiting for transfers between devices  258 us (36%)
  starting transfers between devices  180 us (25%)
  other arithmetic  105 us (15%)
  matrix products  94 us (13%)
  local copies, waits for them, and re-layouts  47 us (6%)
  between operations  29.4 us (4%)
    ppermute x54, waiting for transfers between devices, swap(): return lax.ppermute(v, axis, [(0, 1), (1, 0)])  84.7 us
    ppermute x54, starting transfers between devices, swap(): return lax.ppermute(v, axis, [(0, 1), (1, 0)])  82 us
    ppermute x54, waiting for transfers between devices, turn(): return lax.ppermute(v, axis, [(i, (i + by) % n) for i in range(n)])  79 us
    ppermute x54, starting transfers between devices, turn(): return lax.ppermute(v, axis, [(i, (i + by) % n) for i in range(n)])  61 us
    ppermute x12, waiting for transfers between devices, shift(): lax.ppermute(v, axis, [(i, i + by) for i in range(n) if 0 <= i + by < n])  43.1 us
    ppermute x7, waiting for transfers between devices, cross(): return lax.ppermute(v, ('section', 'ylo'), [(0, 3), (1, 2), (2, 1), (3, 0)])  39.4 us
    dot_general x26, matrix products, mm_left(): lax.dot_general(a, b, (((0,), (0,)), ((), ())), preferred_element_type=f32)  35.9 us
    dot_general x17, matrix products, mm(): lax.dot_general(a, b, (((1,), (0,)), ((), ())), preferred_element_type=f32)  30.2 us
  transfers between devices with their start and end apart: 138, of which 73 were waited for; matrix products, arithmetic and copies ran while one was open for 31% of the time, Pallas kernels for 0%

profile of v5, /device:TPU:1, one launch (start us, length us, event | category | flops | bytes accessed | tf_op | source)
XLA Modules:
  0.0 713.3 jit_solution(12531782287972624545)
XLA Ops:
  13.5 2.9 collective-permute-start.2
  17.7 2.8 collective-permute-start
  20.6 11.6 %collective-permute-done.2 = bf16[256,690]{0,1:T(8,128)(2,1)S(1)} collective-permute-done((bf16[256,690]{0,1:T(8,128)(2,1)S(1)}, bf16[256,690]{0,1:T(8,128)(2,1)S(1)}, u32[]{:S(2)}, u32[]{:S(2)}) %collective-permute-start.2) | collective-permute-done | bytes 353312 | tf_op jit(solution)/shard_map/weights_key_value/ppermute | solution.py:49
  37.4 3.0 collective-permute-start.12
  49.7 8.6 %collective-permute-done.6 = bf16[256,1120]{0,1:T(8,128)(2,1)S(1)} collective-permute-done((bf16[256,1120]{0,1:T(8,128)(2,1)S(1)}, bf16[256,1120]{0,1:T(8,128)(2,1)S(1)}, u32[]{:S(2)}, u32[]{:S(2)}) %collective-permute-start.6) | collective-permute-done | bytes 573472 | tf_op jit(solution)/shard_map/weights_query_gate_out/ppermute | solution.py:45
  62.0 3.3 collective-permute-start.8
  90.0 3.1 collective-permute-start.29
  96.9 3.2 convolution_convert_fusion
  101.0 5.5 collective-permute-done.28
  106.6 15.9 %collective-permute-done.29 = bf16[256,1296]{0,1:T(8,128)(2,1)} collective-permute-done((bf16[256,1296]{0,1:T(8,128)(2,1)S(1)}, bf16[256,1296]{0,1:T(8,128)(2,1)}, u32[]{:S(2)}, u32[]{:S(2)}) %collective-permute-start.29) | collective-permute-done | bytes 663584 | tf_op jit(solution)/shard_map/layer0_forward/weights_gate_up_down/ppermute | solution.py:45
  124.4 2.8 broadcast_select_fusion.6
  133.9 4.4 collective-permute-start.18
  142.1 4.6 collective-permute-done.18
  148.2 3.0 fusion.16
  156.9 4.9 collective-permute-start.19
  163.6 5.3 collective-permute-start.22
  169.6 5.0 collective-permute-done.22
  174.9 3.3 collective-permute-done.20
  181.7 6.2 collective-permute-done.25
  191.2 3.2 all-gather.10.cloned.1.call-done
  194.5 3.3 fusion.12
  208.5 2.7 collective-permute-start.34
  212.4 3.8 collective-permute-done.34
  216.7 4.3 collective-permute-done.32
  221.9 2.7 collective-permute-start.41
  226.0 5.0 collective-permute-done.43
  245.4 5.9 collective-permute-done.40.refs_2_
  251.3 11.2 %collective-permute-done.45.refs_3_ = bf16[256,1024]{1,0:T(8,128)(2,1)S(1)} collective-permute-done((bf16[256,1024]{1,0:T(8,128)(2,1)}, bf16[256,1024]{1,0:T(8,128)(2,1)S(1)}, u32[]{:S(2)}, u32[]{:S(2)}) %collective-permute-start.45) | collective-permute-done | bytes 524320 | tf_op jit(solution)/shard_map/ppermute | solution.py:45
  263.3 8.1 %all-gather.12.cloned.1.call-done = bf16[2048,1808]{0,1:T(8,128)(2,1)} async-done(((bf16[512,1808]{0,1:T(8,128)(2,1)}), bf16[2048,1808]{0,1:T(8,128)(2,1)}) %all-gather.12.cloned.1.call-update) | async-done | bytes 7405584 | tf_op jit(solution)/shard_map/gather_weights/all_gather | solution.py:302
  271.5 4.8 fusion.249
  278.2 4.7 collective-permute-done.46
  283.1 3.0 collective-permute-start.49
  290.1 9.4 %collective-permute-done.49 = bf16[256,432]{0,1:T(8,128)(2,1)S(1)} collective-permute-done((bf16[256,432]{0,1:T(8,128)(2,1)S(1)}, bf16[256,432]{0,1:T(8,128)(2,1)S(1)}, u32[]{:S(2)}, u32[]{:S(2)}) %collective-permute-start.49) | collective-permute-done | bytes 221216 | tf_op jit(solution)/shard_map/layer1_forward/earlier_states/ppermute | solution.py:59
  299.5 7.2 %collective-permute-done.47 = bf16[256,432]{0,1:T(8,128)(2,1)S(1)} collective-permute-done((bf16[256,432]{0,1:T(8,128)(2,1)S(1)}, bf16[256,432]{0,1:T(8,128)(2,1)S(1)}, u32[]{:S(2)}, u32[]{:S(2)}) %collective-permute-start.47) | collective-permute-done | bytes 221216 | tf_op jit(solution)/shard_map/layer1_forward/earlier_states/ppermute | solution.py:59
  314.8 2.7 collective-permute-start.53
  323.4 3.9 collective-permute-done.51
  328.1 3.0 collective-permute-done.54.refs_1_
  341.6 3.5 collective-permute-start.58
  349.5 9.0 %collective-permute-done.59.refs_1_ = bf16[256,864]{1,0:T(8,128)(2,1)S(1)} collective-permute-done((bf16[256,864]{1,0:T(8,128)(2,1)}, bf16[256,864]{1,0:T(8,128)(2,1)S(1)}, u32[]{:S(2)}, u32[]{:S(2)}) %collective-permute-start.59) | collective-permute-done | bytes 442400 | tf_op jit(solution)/shard_map/ppermute | solution.py:45
  361.8 3.4 fusion.8
  384.0 2.7 collective-permute-start.78
  404.7 5.0 collective-permute-start.68
  410.3 3.1 add_convert_fusion.2
  434.7 14.2 %collective-permute-done.73 = bf16[256,432]{0,1:T(8,128)(2,1)S(1)} collective-permute-done((bf16[256,432]{0,1:T(8,128)(2,1)S(1)}, bf16[256,432]{0,1:T(8,128)(2,1)S(1)}, u32[]{:S(2)}, u32[]{:S(2)}) %collective-permute-start.73) | collective-permute-done | bytes 221216 | tf_op jit(solution)/shard_map/layer1_backward/later_states/ppermute | solution.py:59
  456.5 4.4 fusion
  461.8 2.8 collective-permute-start.79
  470.9 2.7 collective-permute-start.82
  476.5 2.7 collective-permute-done.82
  479.4 4.2 collective-permute-done.80
  492.9 4.2 collective-permute-done.86
  507.4 3.2 fusion.10
  522.6 3.4 collective-permute-done.89
  535.3 4.5 collective-permute-done.96
  565.7 4.4 collective-permute-done.104.refs_2_
  571.9 6.5 collective-permute-done.102
  589.6 7.0 concatenate.458.refs_1_
  600.3 2.9 add_convert_fusion.3.refs_2_
  603.3 3.0 fusion.14
  617.3 2.9 collective-permute-start.114
  622.0 3.9 collective-permute-done.106
  635.5 4.0 collective-permute-done.110
  665.4 5.5 collective-permute-done.124
  671.1 3.6 collective-permute-start.125
  681.1 16.2 %collective-permute-done.122 = bf16[256,1552]{0,1:T(8,128)(2,1)} collective-permute-done((bf16[256,1552]{0,1:T(8,128)(2,1)}, bf16[256,1552]{0,1:T(8,128)(2,1)}, u32[]{:S(2)}, u32[]{:S(2)}) %collective-permute-start.122) | collective-permute-done | bytes 794656 | tf_op jit(solution)/shard_map/owners/ppermute | solution.py:49
  (933 shorter events, 362.3 us)
Async XLA Ops:
  7.2 86.9 %all-gather.6.cloned.1.call-start = ((), (), s32[]{:S(2)}) async-start(), calls=%async_computation.6 | async-start | bytes 3563520 | tf_op jit(solution)/shard_map/gather_weights/all_gather | solution.py:302
  13.5 18.8 %collective-permute-start.2 = (bf16[256,690]{0,1:T(8,128)(2,1)S(1)}, bf16[256,690]{0,1:T(8,128)(2,1)S(1)}, u32[]{:S(2)}, u32[]{:S(2)}) collective-permute-start(bf16[256,690]{0,1:T(8,128)(2,1)S(1)} %maximum_select_fusion.11), channel_id=1, source_target_pairs={{0,72},{8,64},{64,8},{72,0},{1,73},{9,65},{65,9},{73,1},{2,74},{10... | collective-permute-start | bytes 1059848 | tf_op jit(solution)/shard_map/weights_key_value/ppermute | solution.py:49
  16.4 15.9 %collective-permute-start.3 = (bf16[256,690]{0,1:T(8,128)(2,1)S(1)}, bf16[256,690]{0,1:T(8,128)(2,1)S(1)}, u32[]{:S(2)}, u32[]{:S(2)}) collective-permute-start(bf16[256,690]{0,1:T(8,128)(2,1)S(1)} %maximum_select_fusion.11), channel_id=1, source_target_pairs={{0,64},{64,0},{1,65},{65,1},{2,66},{66,2},{3,67},{67,3},{4,68},{68... | collective-permute-start | bytes 1059848 | tf_op jit(solution)/shard_map/weights_key_value/ppermute | solution.py:45
  16.7 16.0 %collective-permute-start.4 = (bf16[256,690]{0,1:T(8,128)(2,1)S(1)}, bf16[256,690]{0,1:T(8,128)(2,1)S(1)}, u32[]{:S(2)}, u32[]{:S(2)}) collective-permute-start(bf16[256,690]{0,1:T(8,128)(2,1)S(1)} %maximum_select_fusion.11), channel_id=1, source_target_pairs={{0,8},{8,0},{1,9},{9,1},{2,10},{10,2},{3,11},{11,3},{4,12},{12,4},... | collective-permute-start | bytes 1059848 | tf_op jit(solution)/shard_map/weights_key_value/ppermute | solution.py:45
  17.7 27.8 %collective-permute-start = (bf16[32,2048]{1,0:T(8,128)(2,1)}, bf16[32,2048]{1,0:T(8,128)(2,1)S(1)}, u32[]{:S(2)}, u32[]{:S(2)}) collective-permute-start(bf16[32,2048]{1,0:T(8,128)(2,1)} %select_bitcast_fusion.1), channel_id=1, source_target_pairs={{0,64},{64,0},{1,65},{65,1},{2,66},{66,2},{3,67},{67,3},{4,68},{68... | collective-permute-start | bytes 393224 | tf_op jit(solution)/shard_map/ppermute | solution.py:45
  35.0 113.1 %all-gather.8.cloned.1.call-start = ((), (), s32[]{:S(2)}) async-start(), calls=%async_computation.7 | async-start | bytes 5734400 | tf_op jit(solution)/shard_map/gather_weights/all_gather | solution.py:302
  43.7 14.6 %collective-permute-start.6 = (bf16[256,1120]{0,1:T(8,128)(2,1)S(1)}, bf16[256,1120]{0,1:T(8,128)(2,1)S(1)}, u32[]{:S(2)}, u32[]{:S(2)}) collective-permute-start(bf16[256,1120]{0,1:T(8,128)(2,1)S(1)} %fusion.56), channel_id=1, source_target_pairs={{0,8},{8,0},{1,9},{9,1},{2,10},{10,2},{3,11},{11,3},{4,12},{12,4},... | collective-permute-start | bytes 1720328 | tf_op jit(solution)/shard_map/weights_query_gate_out/ppermute | solution.py:45
  46.2 26.5 %collective-permute-start.13 = (bf16[256,1120]{0,1:T(8,128)(2,1)S(1)}, bf16[256,1120]{0,1:T(8,128)(2,1)S(1)}, u32[]{:S(2)}, u32[]{:S(2)}) collective-permute-start(bf16[256,1120]{0,1:T(8,128)(2,1)S(1)} %fusion.56), channel_id=1, source_target_pairs={{0,64},{64,0},{1,65},{65,1},{2,66},{66,2},{3,67},{67,3},{4,68},{68... | collective-permute-start | bytes 1720328 | tf_op jit(solution)/shard_map/weights_query_gate_out/ppermute | solution.py:45
  47.8 27.4 %collective-permute-start.14 = (bf16[256,1120]{0,1:T(8,128)(2,1)S(1)}, bf16[256,1120]{0,1:T(8,128)(2,1)S(1)}, u32[]{:S(2)}, u32[]{:S(2)}) collective-permute-start(bf16[256,1120]{0,1:T(8,128)(2,1)S(1)} %fusion.56), channel_id=1, source_target_pairs={{0,72},{8,64},{64,8},{72,0},{1,73},{9,65},{65,9},{73,1},{2,74},{10... | collective-permute-start | bytes 1720328 | tf_op jit(solution)/shard_map/weights_query_gate_out/ppermute | solution.py:49
  81.1 113.4 %all-gather.10.cloned.1.call-start = ((), (), s32[]{:S(2)}) async-start(), calls=%async_computation.8 | async-start | bytes 6635520 | tf_op jit(solution)/shard_map/layer0_forward/weights_gate_up_down/all_gather | solution.py:302
  89.9 16.7 %collective-permute-start.28 = (bf16[256,1296]{0,1:T(8,128)(2,1)S(1)}, bf16[256,1296]{0,1:T(8,128)(2,1)}, u32[]{:S(2)}, u32[]{:S(2)}) collective-permute-start(bf16[256,1296]{0,1:T(8,128)(2,1)S(1)} %maximum_select_fusion.2), channel_id=1, source_target_pairs={{0,8},{8,0},{1,9},{9,1},{2,10},{10,2},{3,11},{11,3},{4,12},{12,4},... | collective-permute-start | bytes 1990664 | tf_op jit(solution)/shard_map/layer0_forward/weights_gate_up_down/ppermute | solution.py:45
  90.0 32.5 %collective-permute-start.29 = (bf16[256,1296]{0,1:T(8,128)(2,1)S(1)}, bf16[256,1296]{0,1:T(8,128)(2,1)}, u32[]{:S(2)}, u32[]{:S(2)}) collective-permute-start(bf16[256,1296]{0,1:T(8,128)(2,1)S(1)} %maximum_select_fusion.2), channel_id=1, source_target_pairs={{0,64},{64,0},{1,65},{65,1},{2,66},{66,2},{3,67},{67,3},{4,68},{68... | collective-permute-start | bytes 1990664 | tf_op jit(solution)/shard_map/layer0_forward/weights_gate_up_down/ppermute | solution.py:45
  93.0 31.4 %collective-permute-start.30 = (bf16[256,1296]{0,1:T(8,128)(2,1)S(1)}, bf16[256,1296]{0,1:T(8,128)(2,1)}, u32[]{:S(2)}, u32[]{:S(2)}) collective-permute-start(bf16[256,1296]{0,1:T(8,128)(2,1)S(1)} %maximum_select_fusion.2), channel_id=1, source_target_pairs={{0,72},{8,64},{64,8},{72,0},{1,73},{9,65},{65,9},{73,1},{2,74},{10... | collective-permute-start | bytes 1990664 | tf_op jit(solution)/shard_map/layer0_forward/weights_gate_up_down/ppermute | solution.py:49
  100.5 26.8 %collective-permute-start.15 = (bf16[256,432]{0,1:T(8,128)(2,1)S(1)}, bf16[256,432]{0,1:T(8,128)(2,1)S(1)}, u32[]{:S(2)}, u32[]{:S(2)}) collective-permute-start(bf16[256,432]{0,1:T(8,128)(2,1)S(1)} %convolution_convert_fusion.4), channel_id=1, source_target_pairs={{0,8},{8,0},{1,9},{9,1},{2,10},{10,2},{3,11},{11,3},{4,12},{12,4},... | collective-permute-start | bytes 663560 | tf_op jit(solution)/shard_map/layer0_forward/earlier_states/ppermute | solution.py:45
  131.3 140.2 %all-gather.12.cloned.1.call-start = ((), (), s32[]{:S(2)}) async-start(), calls=%async_computation.9 | async-start | bytes 9256960 | tf_op jit(solution)/shard_map/gather_weights/all_gather | solution.py:302
  133.8 227.9 %all-gather.14.cloned.1.call-start = ((), (), s32[]{:S(2)}) async-start(), calls=%async_computation.10 | async-start | bytes 6635520 | tf_op jit(solution)/shard_map/layer0_forward/weights_gate_up_down/all_gather | solution.py:302
  133.9 12.8 %collective-permute-start.18 = (bf16[256,432]{0,1:T(8,128)(2,1)}, bf16[256,432]{0,1:T(8,128)(2,1)S(1)}, u32[]{:S(2)}, u32[]{:S(2)}) collective-permute-start(bf16[256,432]{0,1:T(8,128)(2,1)} %copy-done.152), channel_id=1, source_target_pairs={{0,48},{1,49},{2,50},{3,51},{4,52},{5,53},{6,54},{7,55},{8,56},{9,... | collective-permute-start | bytes 663560 | tf_op jit(solution)/shard_map/layer0_forward/earlier_states/ppermute | solution.py:59
  163.6 11.0 %collective-permute-start.22 = (bf16[32,2048]{1,0:T(8,128)(2,1)S(1)}, bf16[32,2048]{1,0:T(8,128)(2,1)S(1)}, u32[]{:S(2)}, u32[]{:S(2)}) collective-permute-start(bf16[32,2048]{1,0:T(8,128)(2,1)S(1)} %get-tuple-element.195), channel_id=1, source_target_pairs={{0,3},{1,0},{2,1},{3,2},{4,7},{5,4},{6,5},{7,6},{8,11},{9,8},{10,9... | collective-permute-start | bytes 393224 | tf_op jit(solution)/shard_map/layer0_forward/collect/ppermute | solution.py:54
  168.9 9.2 %collective-permute-start.20 = (bf16[32,2048]{1,0:T(8,128)(2,1)S(1)}, bf16[32,2048]{1,0:T(8,128)(2,1)S(1)}, u32[]{:S(2)}, u32[]{:S(2)}) collective-permute-start(bf16[32,2048]{1,0:T(8,128)(2,1)S(1)} %get-tuple-element.194), channel_id=1, source_target_pairs={{0,1},{1,2},{2,3},{3,0},{4,5},{5,6},{6,7},{7,4},{8,9},{9,10},{10,1... | collective-permute-start | bytes 393224 | tf_op jit(solution)/shard_map/layer0_forward/collect/ppermute | solution.py:54
  204.1 281.2 %reduce-scatter.7.cloned.1.call-start = ((), (), s32[]{:S(2)}) async-start(), calls=%async_computation.11 | async-start | bytes 2293760 | tf_op jit(solution)/shard_map/layer1_backward/reduce_scatter | solution.py:332
  205.9 39.5 %collective-permute-start.39 = (bf16[256,1024]{1,0:T(8,128)(2,1)}, bf16[256,1024]{1,0:T(8,128)(2,1)S(1)}, u32[]{:S(2)}, u32[]{:S(2)}) collective-permute-start(bf16[256,1024]{1,0:T(8,128)(2,1)} %pad_maximum_fusion.13), channel_id=1, source_target_pairs={{0,8},{8,0},{1,9},{9,1},{2,10},{10,2},{3,11},{11,3},{4,12},{12,4},... | collective-permute-start | bytes 1572872 | tf_op jit(solution)/shard_map/ppermute | solution.py:45
  211.6 9.3 %collective-permute-start.32 = (bf16[32,2048]{1,0:T(8,128)(2,1)S(1)}, bf16[32,2048]{1,0:T(8,128)(2,1)S(1)}, u32[]{:S(2)}, u32[]{:S(2)}) collective-permute-start(bf16[32,2048]{1,0:T(8,128)(2,1)S(1)} %get-tuple-element.191), channel_id=1, source_target_pairs={{0,1},{1,2},{2,3},{3,0},{4,5},{5,6},{6,7},{7,4},{8,9},{9,10},{10,1... | collective-permute-start | bytes 393224 | tf_op jit(solution)/shard_map/layer0_forward/collect/ppermute | solution.py:54
  221.7 9.2 %collective-permute-start.43 = (bf16[32,2048]{1,0:T(8,128)(2,1)}, bf16[32,2048]{1,0:T(8,128)(2,1)S(1)}, u32[]{:S(2)}, u32[]{:S(2)}) collective-permute-start(bf16[32,2048]{1,0:T(8,128)(2,1)} %shard_map.212), channel_id=1, source_target_pairs={{0,1},{1,2},{2,3},{3,0},{4,5},{5,6},{6,7},{7,4},{8,9},{9,10},{10,1... | collective-permute-start | bytes 393224 | tf_op jit(solution)/shard_map/spread/ppermute | solution.py:54
  221.7 9.2 %collective-permute-start.42 = (bf16[32,2048]{1,0:T(8,128)(2,1)}, bf16[32,2048]{1,0:T(8,128)(2,1)S(1)}, u32[]{:S(2)}, u32[]{:S(2)}) collective-permute-start(bf16[32,2048]{1,0:T(8,128)(2,1)} %shard_map.212), channel_id=1, source_target_pairs={{0,2},{1,3},{2,0},{3,1},{4,6},{5,7},{6,4},{7,5},{8,10},{9,11},{10,... | collective-permute-start | bytes 393224 | tf_op jit(solution)/shard_map/spread/ppermute | solution.py:54
  221.9 9.1 %collective-permute-start.41 = (bf16[32,2048]{1,0:T(8,128)(2,1)}, bf16[32,2048]{1,0:T(8,128)(2,1)S(1)}, u32[]{:S(2)}, u32[]{:S(2)}) collective-permute-start(bf16[32,2048]{1,0:T(8,128)(2,1)} %shard_map.212), channel_id=1, source_target_pairs={{0,3},{1,0},{2,1},{3,2},{4,7},{5,4},{6,5},{7,6},{8,11},{9,8},{10,9... | collective-permute-start | bytes 393224 | tf_op jit(solution)/shard_map/spread/ppermute | solution.py:54
  225.4 12.2 %collective-permute-start.37 = (bf16[32,2048]{1,0:T(8,128)(2,1)S(1)}, bf16[32,2048]{1,0:T(8,128)(2,1)S(1)}, u32[]{:S(2)}, u32[]{:S(2)}) collective-permute-start(bf16[32,2048]{1,0:T(8,128)(2,1)S(1)} %fusion.126), channel_id=1, source_target_pairs={{0,1},{1,2},{2,3},{3,0},{4,5},{5,6},{6,7},{7,4},{8,9},{9,10},{10,1... | collective-permute-start | bytes 393224 | tf_op jit(solution)/shard_map/spread/ppermute | solution.py:54
  237.6 13.7 %collective-permute-start.40 = (bf16[256,1024]{1,0:T(8,128)(2,1)S(1)}, bf16[256,1024]{1,0:T(8,128)(2,1)S(1)}, u32[]{:S(2)}, u32[]{:S(2)}) collective-permute-start(bf16[256,1024]{1,0:T(8,128)(2,1)S(1)} %pad_maximum_fusion.14), channel_id=1, source_target_pairs={{0,8},{8,0},{1,9},{9,1},{2,10},{10,2},{3,11},{11,3},{4,12},{12,4},... | collective-permute-start | bytes 1572872 | tf_op jit(solution)/shard_map/ppermute | solution.py:45
  241.0 21.5 %collective-permute-start.45 = (bf16[256,1024]{1,0:T(8,128)(2,1)}, bf16[256,1024]{1,0:T(8,128)(2,1)S(1)}, u32[]{:S(2)}, u32[]{:S(2)}) collective-permute-start(bf16[256,1024]{1,0:T(8,128)(2,1)} %pad_maximum_fusion.16), channel_id=1, source_target_pairs={{0,8},{8,0},{1,9},{9,1},{2,10},{10,2},{3,11},{11,3},{4,12},{12,4},... | collective-permute-start | bytes 1572872 | tf_op jit(solution)/shard_map/ppermute | solution.py:45
  283.1 16.5 %collective-permute-start.49 = (bf16[256,432]{0,1:T(8,128)(2,1)S(1)}, bf16[256,432]{0,1:T(8,128)(2,1)S(1)}, u32[]{:S(2)}, u32[]{:S(2)}) collective-permute-start(bf16[256,432]{0,1:T(8,128)(2,1)S(1)} %fusion.118), channel_id=1, source_target_pairs={{0,48},{1,49},{2,50},{3,51},{4,52},{5,53},{6,54},{7,55},{8,56},{9,... | collective-permute-start | bytes 663560 | tf_op jit(solution)/shard_map/layer1_forward/earlier_states/ppermute | solution.py:59
  286.1 13.4 %collective-permute-start.48 = (bf16[256,432]{0,1:T(8,128)(2,1)S(1)}, bf16[256,432]{0,1:T(8,128)(2,1)S(1)}, u32[]{:S(2)}, u32[]{:S(2)}) collective-permute-start(bf16[256,432]{0,1:T(8,128)(2,1)S(1)} %fusion.118), channel_id=1, source_target_pairs={{0,32},{16,48},{1,33},{17,49},{2,34},{18,50},{3,35},{19,51},{4,36}... | collective-permute-start | bytes 663560 | tf_op jit(solution)/shard_map/layer1_forward/earlier_states/ppermute | solution.py:59
  288.0 18.7 %collective-permute-start.47 = (bf16[256,432]{0,1:T(8,128)(2,1)S(1)}, bf16[256,432]{0,1:T(8,128)(2,1)S(1)}, u32[]{:S(2)}, u32[]{:S(2)}) collective-permute-start(bf16[256,432]{0,1:T(8,128)(2,1)S(1)} %fusion.118), channel_id=1, source_target_pairs={{0,16},{16,32},{32,48},{1,17},{17,33},{33,49},{2,18},{18,34},{34,5... | collective-permute-start | bytes 663560 | tf_op jit(solution)/shard_map/layer1_forward/earlier_states/ppermute | solution.py:59
  318.0 9.3 %collective-permute-start.51 = (bf16[32,2048]{1,0:T(8,128)(2,1)S(1)}, bf16[32,2048]{1,0:T(8,128)(2,1)S(1)}, u32[]{:S(2)}, u32[]{:S(2)}) collective-permute-start(bf16[32,2048]{1,0:T(8,128)(2,1)S(1)} %get-tuple-element.188), channel_id=1, source_target_pairs={{0,1},{1,2},{2,3},{3,0},{4,5},{5,6},{6,7},{7,4},{8,9},{9,10},{10,1... | collective-permute-start | bytes 393224 | tf_op jit(solution)/shard_map/layer1_forward/collect/ppermute | solution.py:54
  318.8 12.4 %collective-permute-start.54 = (bf16[256,1024]{1,0:T(8,128)(2,1)S(1)}, bf16[256,1024]{1,0:T(8,128)(2,1)S(1)}, u32[]{:S(2)}, u32[]{:S(2)}) collective-permute-start(bf16[256,1024]{1,0:T(8,128)(2,1)S(1)} %pad_maximum_fusion.17), channel_id=1, source_target_pairs={{0,8},{8,0},{1,9},{9,1},{2,10},{10,2},{3,11},{11,3},{4,12},{12,4},... | collective-permute-start | bytes 1572872 | tf_op jit(solution)/shard_map/ppermute | solution.py:45
  346.0 12.5 %collective-permute-start.59 = (bf16[256,864]{1,0:T(8,128)(2,1)}, bf16[256,864]{1,0:T(8,128)(2,1)S(1)}, u32[]{:S(2)}, u32[]{:S(2)}) collective-permute-start(bf16[256,864]{1,0:T(8,128)(2,1)} %pad_maximum_fusion.27), channel_id=1, source_target_pairs={{0,8},{8,0},{1,9},{9,1},{2,10},{10,2},{3,11},{11,3},{4,12},{12,4},... | collective-permute-start | bytes 1327112 | tf_op jit(solution)/shard_map/ppermute | solution.py:45
  366.6 23.1 %collective-permute-start.64 = (bf16[256,864]{1,0:T(8,128)(2,1)S(1)}, bf16[256,864]{1,0:T(8,128)(2,1)S(1)}, u32[]{:S(2)}, u32[]{:S(2)}) collective-permute-start(bf16[256,864]{1,0:T(8,128)(2,1)S(1)} %pad_maximum_fusion.28), channel_id=1, source_target_pairs={{0,8},{8,0},{1,9},{9,1},{2,10},{10,2},{3,11},{11,3},{4,12},{12,4},... | collective-permute-start | bytes 1327112 | tf_op jit(solution)/shard_map/layer1_backward/ppermute | solution.py:45
  372.4 37.9 %collective-permute-start.69 = (bf16[256,1024]{1,0:T(8,128)(2,1)}, bf16[256,1024]{1,0:T(8,128)(2,1)}, u32[]{:S(2)}, u32[]{:S(2)}) collective-permute-start(bf16[256,1024]{1,0:T(8,128)(2,1)} %pad_maximum_fusion.20), channel_id=1, source_target_pairs={{0,8},{8,0},{1,9},{9,1},{2,10},{10,2},{3,11},{11,3},{4,12},{12,4},... | collective-permute-start | bytes 1572872 | tf_op jit(solution)/shard_map/ppermute | solution.py:45
  381.6 28.1 %collective-permute-start.83 = (bf16[256,864]{1,0:T(8,128)(2,1)}, bf16[256,864]{1,0:T(8,128)(2,1)S(1)}, u32[]{:S(2)}, u32[]{:S(2)}) collective-permute-start(bf16[256,864]{1,0:T(8,128)(2,1)} %pad_maximum_fusion.29), channel_id=1, source_target_pairs={{0,8},{8,0},{1,9},{9,1},{2,10},{10,2},{3,11},{11,3},{4,12},{12,4},... | collective-permute-start | bytes 1327112 | tf_op jit(solution)/shard_map/ppermute | solution.py:45
  404.7 9.2 %collective-permute-start.68 = (bf16[128,2048]{1,0:T(8,128)(2,1)S(1)}, bf16[128,2048]{1,0:T(8,128)(2,1)}, u32[]{:S(2)}, u32[]{:S(2)}) collective-permute-start(bf16[128,2048]{1,0:T(8,128)(2,1)S(1)} %pad_maximum_fusion.19), channel_id=1, source_target_pairs={{0,4},{4,0},{1,5},{5,1},{2,6},{6,2},{3,7},{7,3},{8,12},{12,8},{9,1... | collective-permute-start | bytes 1572872 | tf_op jit(solution)/shard_map/layer1_backward/spread/ppermute | solution.py:45
  413.4 135.4 %reduce-scatter.9.cloned.1.call-start = ((), (), s32[]{:S(2)}) async-start(), calls=%async_computation.12 | async-start | bytes 2293760 | tf_op jit(solution)/shard_map/layer1_backward/reduce_scatter | solution.py:332
  426.4 25.3 %collective-permute-start.74 = (bf16[256,1024]{1,0:T(8,128)(2,1)}, bf16[256,1024]{1,0:T(8,128)(2,1)S(1)}, u32[]{:S(2)}, u32[]{:S(2)}) collective-permute-start(bf16[256,1024]{1,0:T(8,128)(2,1)} %pad_maximum_fusion.21), channel_id=1, source_target_pairs={{0,8},{8,0},{1,9},{9,1},{2,10},{10,2},{3,11},{11,3},{4,12},{12,4},... | collective-permute-start | bytes 1572872 | tf_op jit(solution)/shard_map/layer1_backward/ppermute | solution.py:45
  429.9 19.1 %collective-permute-start.73 = (bf16[256,432]{0,1:T(8,128)(2,1)S(1)}, bf16[256,432]{0,1:T(8,128)(2,1)S(1)}, u32[]{:S(2)}, u32[]{:S(2)}) collective-permute-start(bf16[256,432]{0,1:T(8,128)(2,1)S(1)} %fusion.120), channel_id=1, source_target_pairs={{48,0},{49,1},{50,2},{51,3},{52,4},{53,5},{54,6},{55,7},{56,8},{57... | collective-permute-start | bytes 663560 | tf_op jit(solution)/shard_map/layer1_backward/later_states/ppermute | solution.py:59
  431.2 17.8 %collective-permute-start.72 = (bf16[256,432]{0,1:T(8,128)(2,1)S(1)}, bf16[256,432]{0,1:T(8,128)(2,1)S(1)}, u32[]{:S(2)}, u32[]{:S(2)}) collective-permute-start(bf16[256,432]{0,1:T(8,128)(2,1)S(1)} %fusion.120), channel_id=1, source_target_pairs={{32,0},{48,16},{33,1},{49,17},{34,2},{50,18},{35,3},{51,19},{36,4}... | collective-permute-start | bytes 663560 | tf_op jit(solution)/shard_map/layer1_backward/later_states/ppermute | solution.py:59
  432.5 16.5 %collective-permute-start.71 = (bf16[256,432]{0,1:T(8,128)(2,1)S(1)}, bf16[256,432]{0,1:T(8,128)(2,1)S(1)}, u32[]{:S(2)}, u32[]{:S(2)}) collective-permute-start(bf16[256,432]{0,1:T(8,128)(2,1)S(1)} %fusion.120), channel_id=1, source_target_pairs={{16,0},{32,16},{48,32},{17,1},{33,17},{49,33},{18,2},{34,18},{50,3... | collective-permute-start | bytes 663560 | tf_op jit(solution)/shard_map/layer1_backward/later_states/ppermute | solution.py:59
  467.5 113.8 %reduce-scatter.11.cloned.1.call-start = ((), (), s32[]{:S(2)}) async-start(), calls=%async_computation.13 | async-start | bytes 3604480 | tf_op jit(solution)/shard_map/layer1_backward/reduce_scatter | solution.py:332
  473.9 9.7 %collective-permute-start.80 = (bf16[32,2048]{1,0:T(8,128)(2,1)}, bf16[32,2048]{1,0:T(8,128)(2,1)S(1)}, u32[]{:S(2)}, u32[]{:S(2)}) collective-permute-start(bf16[32,2048]{1,0:T(8,128)(2,1)} %get-tuple-element.179), channel_id=1, source_target_pairs={{0,1},{1,2},{2,3},{3,0},{4,5},{5,6},{6,7},{7,4},{8,9},{9,10},{10,1... | collective-permute-start | bytes 393224 | tf_op jit(solution)/shard_map/layer1_backward/collect/ppermute | solution.py:54
  475.3 24.4 %collective-permute-start.93 = (bf16[256,1376]{0,1:T(8,128)(2,1)}, bf16[256,1376]{0,1:T(8,128)(2,1)S(1)}, u32[]{:S(2)}, u32[]{:S(2)}) collective-permute-start(bf16[256,1376]{0,1:T(8,128)(2,1)} %copy.158), channel_id=1, source_target_pairs={{0,8},{8,0},{1,9},{9,1},{2,10},{10,2},{3,11},{11,3},{4,12},{12,4},... | collective-permute-start | bytes 2113544 | tf_op jit(solution)/shard_map/layer1_backward/ppermute | solution.py:45
  488.1 9.0 %collective-permute-start.86 = (bf16[32,2048]{1,0:T(8,128)(2,1)S(1)}, bf16[32,2048]{1,0:T(8,128)(2,1)S(1)}, u32[]{:S(2)}, u32[]{:S(2)}) collective-permute-start(bf16[32,2048]{1,0:T(8,128)(2,1)S(1)} %fusion.132), channel_id=1, source_target_pairs={{0,1},{1,2},{2,3},{3,0},{4,5},{5,6},{6,7},{7,4},{8,9},{9,10},{10,1... | collective-permute-start | bytes 393224 | tf_op jit(solution)/shard_map/layer0_backward/spread/ppermute | solution.py:54
  502.3 114.9 %reduce-scatter.13.cloned.1.call-start = ((), (), s32[]{:S(2)}) async-start(), calls=%async_computation.14 | async-start | bytes 2293760 | tf_op jit(solution)/shard_map/layer0_backward/reduce_scatter | solution.py:332
  506.2 20.6 %collective-permute-start.92 = (bf16[256,864]{1,0:T(8,128)(2,1)S(1)}, bf16[256,864]{1,0:T(8,128)(2,1)S(1)}, u32[]{:S(2)}, u32[]{:S(2)}) collective-permute-start(bf16[256,864]{1,0:T(8,128)(2,1)S(1)} %pad_maximum_fusion.30), channel_id=1, source_target_pairs={{0,8},{8,0},{1,9},{9,1},{2,10},{10,2},{3,11},{11,3},{4,12},{12,4},... | collective-permute-start | bytes 1327112 | tf_op jit(solution)/shard_map/layer0_backward/ppermute | solution.py:45
  513.9 30.8 %collective-permute-start.98 = (bf16[256,1024]{1,0:T(8,128)(2,1)}, bf16[256,1024]{1,0:T(8,128)(2,1)}, u32[]{:S(2)}, u32[]{:S(2)}) collective-permute-start(bf16[256,1024]{1,0:T(8,128)(2,1)} %pad_maximum_fusion.24), channel_id=1, source_target_pairs={{0,8},{8,0},{1,9},{9,1},{2,10},{10,2},{3,11},{11,3},{4,12},{12,4},... | collective-permute-start | bytes 1572872 | tf_op jit(solution)/shard_map/layer0_backward/ppermute | solution.py:45
  516.8 9.2 %collective-permute-start.89 = (bf16[32,2048]{1,0:T(8,128)(2,1)S(1)}, bf16[32,2048]{1,0:T(8,128)(2,1)S(1)}, u32[]{:S(2)}, u32[]{:S(2)}) collective-permute-start(bf16[32,2048]{1,0:T(8,128)(2,1)S(1)} %get-tuple-element.176), channel_id=1, source_target_pairs={{0,1},{1,2},{2,3},{3,0},{4,5},{5,6},{6,7},{7,4},{8,9},{9,10},{10,1... | collective-permute-start | bytes 393224 | tf_op jit(solution)/shard_map/layer0_backward/collect/ppermute | solution.py:54
  544.7 115.9 %reduce-scatter.17.cloned.1.call-start = ((), (), s32[]{:S(2)}) async-start(), calls=%async_computation.16 | async-start | bytes 1966080 | tf_op jit(solution)/shard_map/layer0_backward/reduce_scatter | solution.py:332
  555.9 14.3 %collective-permute-start.104 = (bf16[256,688]{1,0:T(8,128)(2,1)S(1)}, bf16[256,688]{1,0:T(8,128)(2,1)S(1)}, u32[]{:S(2)}, u32[]{:S(2)}) collective-permute-start(bf16[256,688]{1,0:T(8,128)(2,1)S(1)} %pad_maximum_fusion.31), channel_id=1, source_target_pairs={{0,8},{8,0},{1,9},{9,1},{2,10},{10,2},{3,11},{11,3},{4,12},{12,4},... | collective-permute-start | bytes 1056776 | tf_op jit(solution)/shard_map/layer0_backward/ppermute | solution.py:45
  559.1 22.3 %collective-permute-start.103 = (bf16[256,1024]{1,0:T(8,128)(2,1)}, bf16[256,1024]{1,0:T(8,128)(2,1)}, u32[]{:S(2)}, u32[]{:S(2)}) collective-permute-start(bf16[256,1024]{1,0:T(8,128)(2,1)} %pad_maximum_fusion.25), channel_id=1, source_target_pairs={{0,8},{8,0},{1,9},{9,1},{2,10},{10,2},{3,11},{11,3},{4,12},{12,4},... | collective-permute-start | bytes 1572872 | tf_op jit(solution)/shard_map/layer0_backward/ppermute | solution.py:45
  561.8 16.7 %collective-permute-start.102 = (bf16[256,432]{0,1:T(8,128)(2,1)S(1)}, bf16[256,432]{0,1:T(8,128)(2,1)S(1)}, u32[]{:S(2)}, u32[]{:S(2)}) collective-permute-start(bf16[256,432]{0,1:T(8,128)(2,1)S(1)} %fusion.122), channel_id=1, source_target_pairs={{48,0},{49,1},{50,2},{51,3},{52,4},{53,5},{54,6},{55,7},{56,8},{57... | collective-permute-start | bytes 663560 | tf_op jit(solution)/shard_map/layer0_backward/later_states/ppermute | solution.py:59
  563.1 15.4 %collective-permute-start.101 = (bf16[256,432]{0,1:T(8,128)(2,1)S(1)}, bf16[256,432]{0,1:T(8,128)(2,1)S(1)}, u32[]{:S(2)}, u32[]{:S(2)}) collective-permute-start(bf16[256,432]{0,1:T(8,128)(2,1)S(1)} %fusion.122), channel_id=1, source_target_pairs={{32,0},{48,16},{33,1},{49,17},{34,2},{50,18},{35,3},{51,19},{36,4}... | collective-permute-start | bytes 663560 | tf_op jit(solution)/shard_map/layer0_backward/later_states/ppermute | solution.py:59
  564.4 14.1 %collective-permute-start.100 = (bf16[256,432]{0,1:T(8,128)(2,1)S(1)}, bf16[256,432]{0,1:T(8,128)(2,1)S(1)}, u32[]{:S(2)}, u32[]{:S(2)}) collective-permute-start(bf16[256,432]{0,1:T(8,128)(2,1)S(1)} %fusion.122), channel_id=1, source_target_pairs={{16,0},{32,16},{48,32},{17,1},{33,17},{49,33},{18,2},{34,18},{50,3... | collective-permute-start | bytes 663560 | tf_op jit(solution)/shard_map/layer0_backward/later_states/ppermute | solution.py:59
  585.8 12.7 %collective-permute-start.109 = (bf16[256,688]{1,0:T(8,128)(2,1)}, bf16[256,688]{1,0:T(8,128)(2,1)}, u32[]{:S(2)}, u32[]{:S(2)}) collective-permute-start(bf16[256,688]{1,0:T(8,128)(2,1)} %pad_maximum_fusion.32), channel_id=1, source_target_pairs={{0,8},{8,0},{1,9},{9,1},{2,10},{10,2},{3,11},{11,3},{4,12},{12,4},... | collective-permute-start | bytes 1056776 | tf_op jit(solution)/shard_map/layer0_backward/ppermute | solution.py:45
  603.2 71.6 %reduce-scatter.15.cloned.1.call-start = ((), (), s32[]{:S(2)}) async-start(), calls=%async_computation.15 | async-start | bytes 4259840 | tf_op jit(solution)/shard_map/layer0_backward/reduce_scatter | solution.py:332
  616.5 9.4 %collective-permute-start.106 = (bf16[32,2048]{1,0:T(8,128)(2,1)S(1)}, bf16[32,2048]{1,0:T(8,128)(2,1)S(1)}, u32[]{:S(2)}, u32[]{:S(2)}) collective-permute-start(bf16[32,2048]{1,0:T(8,128)(2,1)S(1)} %get-tuple-element.173), channel_id=1, source_target_pairs={{0,1},{1,2},{2,3},{3,0},{4,5},{5,6},{6,7},{7,4},{8,9},{9,10},{10,1... | collective-permute-start | bytes 393224 | tf_op jit(solution)/shard_map/layer0_backward/collect/ppermute | solution.py:54
  617.3 23.0 %collective-permute-start.114 = (bf16[256,864]{1,0:T(8,128)(2,1)S(1)}, bf16[256,864]{1,0:T(8,128)(2,1)S(1)}, u32[]{:S(2)}, u32[]{:S(2)}) collective-permute-start(bf16[256,864]{1,0:T(8,128)(2,1)S(1)} %broadcast_select_fusion.17), channel_id=1, source_target_pairs={{0,72},{8,64},{64,8},{72,0},{1,73},{9,65},{65,9},{73,1},{2,74},{10... | collective-permute-start | bytes 1327112 | tf_op jit(solution)/shard_map/owners/ppermute | solution.py:49
  648.9 11.7 %collective-permute-start.126 = (bf16[128,864]{1,0:T(8,128)(2,1)S(1)}, bf16[128,864]{1,0:T(8,128)(2,1)S(1)}, u32[]{:S(2)}, u32[]{:S(2)}) collective-permute-start(bf16[128,864]{1,0:T(8,128)(2,1)S(1)} %select_convert_fusion.1), channel_id=1, source_target_pairs={{0,4},{4,0},{1,5},{5,1},{2,6},{6,2},{3,7},{7,3},{8,12},{12,8},{9,1... | collective-permute-start | bytes 663560 | tf_op jit(solution)/shard_map/owners/ppermute | solution.py:45
  661.5 9.4 %collective-permute-start.124 = (bf16[256,688]{1,0:T(8,128)(2,1)}, bf16[256,688]{1,0:T(8,128)(2,1)S(1)}, u32[]{:S(2)}, u32[]{:S(2)}) collective-permute-start(bf16[256,688]{1,0:T(8,128)(2,1)} %get-tuple-element.171), channel_id=1, source_target_pairs={{0,72},{8,64},{64,8},{72,0},{1,73},{9,65},{65,9},{73,1},{2,74},{10... | collective-permute-start | bytes 1056776 | tf_op jit(solution)/shard_map/owners/ppermute | solution.py:49
  676.5 20.9 %collective-permute-start.122 = (bf16[256,1552]{0,1:T(8,128)(2,1)}, bf16[256,1552]{0,1:T(8,128)(2,1)}, u32[]{:S(2)}, u32[]{:S(2)}) collective-permute-start(bf16[256,1552]{0,1:T(8,128)(2,1)} %copy.170), channel_id=1, source_target_pairs={{0,72},{8,64},{64,8},{72,0},{1,73},{9,65},{65,9},{73,1},{2,74},{10... | collective-permute-start | bytes 2383880 | tf_op jit(solution)/shard_map/owners/ppermute | solution.py:49
  (280 other events, 2601.9 us)
Sparse Core Ops, SparseCore 0:
  35.2 40.8 all-gather.5
  81.2 53.6 all-gather.7
  136.5 57.8 all-gather.9
  196.0 75.4 all-gather.11
  273.0 64.8 all-gather.13
  413.6 38.0 reduce-scatter.6
  467.7 27.2 reduce-scatter.8
  502.4 34.3 reduce-scatter.10
  544.8 31.3 reduce-scatter.12
  603.3 24.3 reduce-scatter.16
  630.2 42.5 reduce-scatter.14
